TPU v7x, 32 devices: a whole 2x2x4 slice. The times are simulated.
32 devices in a mesh: dp: 4 (over y, x), ctx: 4 (over z), tp: 2 (over core).
Axes of the slice: x: 2, y: 2, z: 4, core: 2. Of those that a mesh axis runs over, the one named last changes fastest.
Arguments:
- query_rows: bfloat16 [32768, 4096], P(('dp', 'ctx'), 'tp'), parts along dimension 0, may hold values from -6 to 6
- key_rows: bfloat16 [32768, 4096], P(('dp', 'ctx'), 'tp'), parts along dimension 0, may hold values from -16 to 16
- value_rows: bfloat16 [32768, 4096], P(('dp', 'ctx'), 'tp'), parts along dimension 0, may hold values from -72 to 72
- gate_rows: bfloat16 [32768, 4096], P(('dp', 'ctx'), 'tp'), parts along dimension 0, may hold values from -8 to 8
- decay_log: float32 [32, 32768], P('tp', ('dp', 'ctx')), parts along dimension 1, may hold values from -1 to 0
- norm_gain: float32 [4096], replicated, may hold values from 0.1 to 1.9
- doc_lengths: int32 [64], P('dp'), parts along dimension 0, may hold values from 1 to 4096, 8192 in all
- block_shard: int32 [128], P('dp'), parts along dimension 0, may hold values from 0 to 3, as said below
Outputs:
- placed: bfloat16 [32768, 4096], P(('dp', 'ctx', 'tp')), parts along dimension 0
There are 4 independent parts, one for each index of `dp`. A program takes and returns all parts, laid end to end along the dimension named above; an argument that names none is the same for every part. Nothing has to cross between parts.
Inputs may be any that keep to these rules, and one draw needn't show every extreme that they name: `doc_lengths`: the 16 lengths sum to 8192; the longest is exactly 4096. `block_shard`: of the 8 blocks of each index of ctx, exactly 2 go to each of the 4 shards.
All inputs are finite; a program needn't handle non-finite values.
Results may differ from a plain program's by a relative error of at most 0.0057.
Values may be sent and summed in bfloat16 or wider, within the bound.
No kernel may reach another device: no remote copies, remote signals or barrier semaphores. Data moves between devices by JAX's collectives and lax.ppermute only.
A program may use at most 192 MiB of HBM per device.

v0:
```python
import jax
import jax.numpy as jnp
from jax import lax
from jax.sharding import PartitionSpec as P

BLK = 256
CB = 512


norm_eps = 1e-05


def shifted(block, axis, distance):
    devices = range(lax.axis_size(axis))
    route = [(i - distance, i) for i in devices if i - distance in devices]
    return lax.ppermute(block, axis, route)


def doc_positions(doc_lengths, first, length):
    starts = jnp.cumsum(doc_lengths) - doc_lengths
    position = first + jnp.arange(length, dtype=jnp.int32)
    found = jnp.sum((position[:, None] >= starts[None, :]).astype(jnp.int32), axis=1)
    return found - 1


def block_terms(query_blk, key_blk, value_blk, decay_blk, doc_blk, doc_before):
    block_len = doc_blk.shape[0]
    cum_decay = jnp.cumsum(decay_blk, axis=1)
    later = jnp.arange(block_len)[:, None] >= jnp.arange(block_len)[None, :]
    allowed = (later & (doc_blk[:, None] == doc_blk[None, :]))[None]
    log_gap = cum_decay[:, :, None] - cum_decay[:, None, :]
    weight = jnp.where(allowed, jnp.exp(jnp.where(allowed, log_gap, 0.0)), 0.0)
    scores = jnp.einsum("thd,jhd->htj", query_blk, key_blk, preferred_element_type=jnp.float32)
    weights_low = (scores * weight).astype(jnp.bfloat16)
    intra_sum = jnp.einsum(
        "htj,jhd->thd", weights_low, value_blk, preferred_element_type=jnp.float32
    )
    same_last = (doc_blk == doc_blk[-1])[None, :]
    tail_gate = jnp.where(same_last, jnp.exp(cum_decay[:, -1:] - cum_decay), 0.0)
    scaled_keys = (key_blk.astype(jnp.float32) * tail_gate.T[:, :, None]).astype(jnp.bfloat16)
    update = jnp.einsum("jhd,jhe->hde", scaled_keys, value_blk, preferred_element_type=jnp.float32)
    carry_gate = jnp.where(doc_blk[-1] == doc_before, jnp.exp(cum_decay[:, -1]), 0.0)
    entry_gate = jnp.where((doc_blk == doc_before)[None, :], jnp.exp(cum_decay), 0.0)
    return (intra_sum, update, carry_gate, entry_gate)


def local_block(element):
    query_blk, key_blk, value_blk, decay_blk, doc_blk, doc_first = element
    return block_terms(query_blk, key_blk, value_blk, decay_blk, doc_blk, doc_first)


def finish_block(element):
    query_blk, intra_sum, entry_gate, kv_state = element
    reached = jnp.einsum(
        "thd,hde->the", query_blk.astype(jnp.float32), kv_state, precision=lax.Precision.HIGHEST
    )
    return (intra_sum + entry_gate.T[:, :, None] * reached).astype(jnp.bfloat16)


def accumulate(running, element):
    gate_run, state_run = running
    gate_now, update_now = element
    merged = (gate_run * gate_now, gate_now[:, None, None] * state_run + update_now)
    return (merged, (gate_run, state_run))


def local(
    query_rows, key_rows, value_rows, gate_rows, decay_log, norm_gain, doc_lengths, block_shard
):
    rows_dev = query_rows.shape[0]
    local_width = query_rows.shape[1]
    head_count = decay_log.shape[0]
    head_dim = local_width // head_count
    block_count = rows_dev // CB
    ctx_index = lax.axis_index("ctx")
    first_row = ctx_index * rows_dev
    doc_ids = doc_positions(doc_lengths, first_row, rows_dev)
    doc_prior = doc_positions(doc_lengths, first_row - 1, 1)
    doc_shifted = jnp.concatenate([doc_prior, doc_ids[:-1]])
    doc_before = doc_shifted.reshape(block_count, CB)[:, 0]
    query_blocks = query_rows.reshape(block_count, CB, head_count, head_dim)
    key_blocks = key_rows.reshape(block_count, CB, head_count, head_dim)
    value_blocks = value_rows.reshape(block_count, CB, head_count, head_dim)
    decay_blocks = decay_log.reshape(head_count, block_count, CB).transpose(1, 0, 2)
    doc_blocks = doc_ids.reshape(block_count, CB)
    intra_all, updates, carry_gates, entry_gates = lax.map(
        local_block, (query_blocks, key_blocks, value_blocks, decay_blocks, doc_blocks, doc_before)
    )
    unit_gate = jnp.ones((head_count,), jnp.float32)
    zero_state = jnp.zeros((head_count, head_dim, head_dim), jnp.float32)
    totals, befores = lax.scan(accumulate, (unit_gate, zero_state), (carry_gates, updates))
    total_gate, total_state = totals
    gate_before, state_before = befores

    def relay(section, incoming):
        return shifted(total_gate[:, None, None] * incoming + total_state, "ctx", 1)

    incoming = lax.fori_loop(0, lax.axis_size("ctx") - 1, relay, zero_state)
    entering = gate_before[:, :, None, None] * incoming[None] + state_before
    attended = lax.map(finish_block, (query_blocks, intra_all, entry_gates, entering)).reshape(
        rows_dev, local_width
    )
    blocks_dev = rows_dev // BLK
    local_shards = lax.dynamic_slice_in_dim(block_shard, ctx_index * blocks_dev, blocks_dev)
    block_order = jnp.argsort(local_shards, stable=True)
    attended_full = attended.astype(jnp.float32)
    square_part = jnp.sum(attended_full * attended_full, axis=1)
    square_total = lax.psum(square_part, "tp")
    scale_rows = lax.rsqrt(square_total / norm_gain.shape[0] + norm_eps)
    gain_local = lax.dynamic_slice_in_dim(
        norm_gain, lax.axis_index("tp") * local_width, local_width
    )
    normed = (
        attended_full
        * scale_rows[:, None]
        * gain_local[None, :]
        * jax.nn.sigmoid(gate_rows.astype(jnp.float32))
    ).astype(jnp.bfloat16)
    return lax.all_to_all(
        lax.all_to_all(
            normed.reshape(blocks_dev, BLK, normed.shape[1])[block_order].reshape(
                rows_dev, normed.shape[1]
            ),
            "ctx",
            split_axis=0,
            concat_axis=0,
            tiled=True,
        ),
        "tp",
        split_axis=0,
        concat_axis=1,
        tiled=True,
    )


def solution(mesh):
    return jax.shard_map(
        local,
        mesh=mesh,
        in_specs=(
            P(("dp", "ctx"), "tp"),
            P(("dp", "ctx"), "tp"),
            P(("dp", "ctx"), "tp"),
            P(("dp", "ctx"), "tp"),
            P("tp", ("dp", "ctx")),
            P(),
            P("dp"),
            P("dp"),
        ),
        out_specs=P(("dp", "ctx", "tp"), None),
        check_vma=False,
    )
```

profile of v0, /device:TPU:9, one launch (start us, length us, event | category | flops | bytes accessed | tf_op | source)
XLA Modules:
  0.0 560.8 jit_solution(5353088670778044538)
XLA Ops:
  3.1 9.7 %copy.65 = bf16[256,8,16,128]{3,2,1,0:T(8,128)(2,1)} copy(bf16[256,8,16,128]{3,1,2,0:T(8,128)(2,1)} %bitcast.171) | data formatting | bytes 16777216
  12.8 8.8 %copy.49 = bf16[4,512,16,128]{3,1,2,0:T(8,128)(2,1)} copy(bf16[4,512,16,128]{3,2,1,0:T(8,128)(2,1)} %bitcast.170) | data formatting | bytes 16777216 | tf_op jit(solution)/shard_map/while | solution.py:86
  21.6 9.7 %copy.64 = bf16[256,8,16,128]{3,2,1,0:T(8,128)(2,1)} copy(bf16[256,8,16,128]{3,1,2,0:T(8,128)(2,1)} %bitcast.172) | data formatting | bytes 16777216
  31.4 9.8 %copy.66 = bf16[256,8,16,128]{3,2,1,0:T(8,128)(2,1)} copy(bf16[256,8,16,128]{3,1,2,0:T(8,128)(2,1)} %bitcast.173) | data formatting | bytes 16777216
  44.3 120.8 %while.53 = (s32[]{:T(128)}, f32[4,512,16,128]{1,3,2,0:T(8,128)}, f32[4,16,128,128]{3,2,1,0:T(8,128)}, f32[4,16]{1,0:T(4,128)S(1)}, f32[4,16,512]{2,1,0:T(8,128)...) while((s32[]{:T(128)}, f32[4,512,16,128]{1,3,2,0:T(8,128)}, ...), condition=%wide.region_6.7_spmd, body=%wide.region_3.6_spmd.sunk | while | flops 2441897216 | bytes 37958068 | solution.py:86
  56.6 11.0 %bitcast_dynamic-update-slice_fusion.6 = f32[4,512,16,128]{1,3,2,0:T(8,128)} fusion(f32[4,512,16,128]{1,3,2,0:T(8,128)} %get-tuple-element.545, s32[]{:T(128)} %get-tuple-element.544, f32[16,512]{1,0:T(8,128)S(1)} %bitcast.175, pred[512,512]{1,0:T(8,128)(4,1)S(1)} %fusion.51, bf16[4,512,16,128]{3,1,2,0:T(8,128)(2,1)} %get-tuple-element.565, ...), kind=kOutput, calls=%fused_computation.20.clone.1 | convolution fusion | flops 2168455168 | bytes 10814464 | tf_op jit(solution)/shard_map/while/body/eval_jaxpr/htj,jhd->thd/dot_general | solution.py:35
  86.8 11.0 %bitcast_dynamic-update-slice_fusion.6 = f32[4,512,16,128]{1,3,2,0:T(8,128)} fusion(f32[4,512,16,128]{1,3,2,0:T(8,128)} %get-tuple-element.545, s32[]{:T(128)} %get-tuple-element.544, f32[16,512]{1,0:T(8,128)S(1)} %bitcast.175, pred[512,512]{1,0:T(8,128)(4,1)S(1)} %fusion.51, bf16[4,512,16,128]{3,1,2,0:T(8,128)(2,1)} %get-tuple-element.565, ...), kind=kOutput, calls=%fused_computation.20.clone.1 | convolution fusion | flops 2168455168 | bytes 10814464 | tf_op jit(solution)/shard_map/while/body/eval_jaxpr/htj,jhd->thd/dot_general | solution.py:35
  117.0 10.9 %bitcast_dynamic-update-slice_fusion.6 = f32[4,512,16,128]{1,3,2,0:T(8,128)} fusion(f32[4,512,16,128]{1,3,2,0:T(8,128)} %get-tuple-element.545, s32[]{:T(128)} %get-tuple-element.544, f32[16,512]{1,0:T(8,128)S(1)} %bitcast.175, pred[512,512]{1,0:T(8,128)(4,1)S(1)} %fusion.51, bf16[4,512,16,128]{3,1,2,0:T(8,128)(2,1)} %get-tuple-element.565, ...), kind=kOutput, calls=%fused_computation.20.clone.1 | convolution fusion | flops 2168455168 | bytes 10814464 | tf_op jit(solution)/shard_map/while/body/eval_jaxpr/htj,jhd->thd/dot_general | solution.py:35
  147.2 11.0 %bitcast_dynamic-update-slice_fusion.6 = f32[4,512,16,128]{1,3,2,0:T(8,128)} fusion(f32[4,512,16,128]{1,3,2,0:T(8,128)} %get-tuple-element.545, s32[]{:T(128)} %get-tuple-element.544, f32[16,512]{1,0:T(8,128)S(1)} %bitcast.175, pred[512,512]{1,0:T(8,128)(4,1)S(1)} %fusion.51, bf16[4,512,16,128]{3,1,2,0:T(8,128)(2,1)} %get-tuple-element.565, ...), kind=kOutput, calls=%fused_computation.20.clone.1 | convolution fusion | flops 2168455168 | bytes 10814464 | tf_op jit(solution)/shard_map/while/body/eval_jaxpr/htj,jhd->thd/dot_general | solution.py:35
  167.5 10.2 %while.56 = (s32[]{:T(128)}, f32[16]{0:T(128)S(1)}, f32[16,128,128]{2,1,0:T(8,128)S(1)}, f32[4,16]{1,0:T(4,128)S(1)}, f32[4,16,128,128]{3,2,1,0:T(8,128)}, /*ind...) while((s32[]{:T(128)}, f32[16]{0:T(128)S(1)}, ...), condition=%wide.region_8.9_spmd.clone, body=%wide.region_7.8_spmd.clone.sunk | while | flops 1048611 | bytes 5244021 | solution.py:91
  177.9 75.6 %while.54 = (s32[]{:T(128)}, f32[16,128,128]{2,1,0:T(8,128)S(1)}, f32[16]{0:T(128)S(1)}, f32[16,128,128]{2,1,0:T(8,128)S(1)}, s32[]{:T(128)}) while((s32[]{:T(128)}, f32[16,128,128]{2,1,0:T(8,128)S(1)}, f32[16]{0:T(128)S(1)}, f32[16,128,128]{2,1,0:T(8,128)S(1)}, s32[]{:T(128)}) %tuple.93), condition=%wide.region_10.11_spmd, body=%wide.region_9.10_spmd.sunk | while | flops 524290 | bytes 7340197 | solution.py:98
  181.2 22.7 %collective-permute-done = f32[16,128,128]{2,1,0:T(8,128)S(1)} collective-permute-done((f32[16,128,128]{2,1,0:T(8,128)S(1)}, f32[16,128,128]{2,1,0:T(8,128)S(1)}, u32[]{:S(2)}, u32[]{:S(2)}) %collective-permute-start) | collective-permute-done | bytes 1048608 | tf_op jit(solution)/shard_map/while/body/eval_jaxpr/ppermute | solution.py:16
  207.3 21.8 %collective-permute-done = f32[16,128,128]{2,1,0:T(8,128)S(1)} collective-permute-done((f32[16,128,128]{2,1,0:T(8,128)S(1)}, f32[16,128,128]{2,1,0:T(8,128)S(1)}, u32[]{:S(2)}, u32[]{:S(2)}) %collective-permute-start) | collective-permute-done | bytes 1048608 | tf_op jit(solution)/shard_map/while/body/eval_jaxpr/ppermute | solution.py:16
  232.5 21.0 %collective-permute-done = f32[16,128,128]{2,1,0:T(8,128)S(1)} collective-permute-done((f32[16,128,128]{2,1,0:T(8,128)S(1)}, f32[16,128,128]{2,1,0:T(8,128)S(1)}, u32[]{:S(2)}, u32[]{:S(2)}) %collective-permute-start) | collective-permute-done | bytes 1048608 | tf_op jit(solution)/shard_map/while/body/eval_jaxpr/ppermute | solution.py:16
  258.0 29.3 %while.55 = (s32[]{:T(128)}, bf16[4,512,16,128]{1,3,2,0:T(8,128)(2,1)}, f32[4,512,16,128]{1,3,2,0:T(8,128)}, f32[4,16,512]{2,1,0:T(8,128)}, f32[4,16,128,128]{3,...) while((s32[]{:T(128)}, bf16[4,512,16,128]{1,3,2,0:T(8,128)(2,1)}, ...), condition=%wide.region_12.13_spmd, body=%wide.region_11.12_spmd.sunk | while | flops 1613758464 | bytes 9537105 | solution.py:100
  258.8 6.6 %bitcast_dynamic-update-slice_fusion.7 = bf16[4,512,16,128]{1,3,2,0:T(8,128)(2,1)} fusion(bf16[4,512,16,128]{1,3,2,0:T(8,128)(2,1)} %get-tuple-element.624, s32[]{:T(128)} %get-tuple-element.623, bf16[4,512,16,128]{3,1,2,0:T(8,128)(2,1)} %get-tuple-element.635, f32[512,16]{0,1:T(8,128)S(1)} %dynamic-slice_bitcast_fusion.2, ...), kind=kOutput, calls=%fused_computation.5.clone.1 | convolution fusion | flops 1613758464 | bytes 9471488 | tf_op jit(solution)/shard_map/while/body/eval_jaxpr/thd,hde->the/dot_general | solution.py:54
  273.4 6.6 %bitcast_dynamic-update-slice_fusion.7 = bf16[4,512,16,128]{1,3,2,0:T(8,128)(2,1)} fusion(bf16[4,512,16,128]{1,3,2,0:T(8,128)(2,1)} %get-tuple-element.624, s32[]{:T(128)} %get-tuple-element.623, bf16[4,512,16,128]{3,1,2,0:T(8,128)(2,1)} %get-tuple-element.635, f32[512,16]{0,1:T(8,128)S(1)} %dynamic-slice_bitcast_fusion.2, ...), kind=kOutput, calls=%fused_computation.5.clone.1 | convolution fusion | flops 1613758464 | bytes 9471488 | tf_op jit(solution)/shard_map/while/body/eval_jaxpr/thd,hde->the/dot_general | solution.py:54
  287.3 15.7 %copy.54 = f32[4,512,16,128]{3,2,1,0:T(8,128)} copy(bf16[4,512,16,128]{1,3,2,0:T(8,128)(2,1)} %get-tuple-element.169) | data formatting | bytes 25165824 | tf_op jit(solution)/shard_map/convert_element_type | solution.py:106
  314.7 15.7 %fusion.37 = bf16[2048,2048]{1,0:T(8,128)(2,1)} fusion(f32[256,8,16,128]{3,2,1,0:T(8,128)} %bitcast.162, bf16[2048,2048]{1,0:T(8,128)(2,1)} %param.19, f32[2048]{0:T(1024)S(1)} %dynamic_slice.49, f32[2048]{0:T(1024)S(1)} %add_rsqrt_fusion), kind=kLoop, calls=%fused_computation.53 | loop fusion | flops 33554432 | bytes 33570816 | tf_op jit(solution)/shard_map/convert_element_type | solution.py:118
  330.5 8.1 %gather_fusion = bf16[8,256,2048]{2,1,0:T(8,128)(2,1)} fusion(bf16[8,256,2048]{2,1,0:T(8,128)(2,1)} %bitcast.166, s32[1024]{0:T(1024)S(1)} %pad_clamp_fusion), kind=kCustom, calls=%fused_computation | custom fusion | bytes 16777248 | tf_op jit(solution)/shard_map/gather | solution.py:121
  338.5 185.4 %all_to_all.28 = bf16[4,512,2048]{2,1,0:T(8,128)(2,1)S(1)} all-to-all(bf16[4,512,2048]{2,1,0:T(8,128)(2,1)} %bitcast.165), channel_id=1, replica_groups=mesh['dp'=4,'ctx'=4,'tp'=2] {'ctx'}, dimensions={0} | all-to-all | bytes 16777216 | tf_op jit(solution)/shard_map/all_to_all | solution.py:120
  523.9 13.1 %all_to_all.29 = bf16[2,1024,2048]{2,1,0:T(8,128)(2,1)} all-to-all(bf16[2,1024,2048]{2,1,0:T(8,128)(2,1)S(1)} %bitcast.167), channel_id=1, replica_groups=mesh['dp'=4,'ctx'=4,'tp'=2] {'tp'}, dimensions={0} | all-to-all | bytes 16777216 | tf_op jit(solution)/shard_map/all_to_all | solution.py:119
  537.0 11.9 %copy.55 = bf16[1024,2,2048]{0,2,1:T(8,128)(2,1)} copy(bf16[1024,2,2048]{2,0,1:T(8,128)(2,1)} %bitcast.168) | data formatting | bytes 16777216 | tf_op jit(solution)/shard_map/all_to_all | solution.py:119
  548.9 11.9 %copy.56 = bf16[1024,4096]{1,0:T(8,128)(2,1)} copy(bf16[1024,4096]{0,1:T(8,128)(2,1)} %bitcast.169) | data formatting | bytes 16777216 | tf_op jit(solution)/shard_map/all_to_all | solution.py:119
  (159 shorter events, 132.3 us)
Async XLA Ops:
  31.3 9.8 %copy-start.1 = (f32[16,2048]{1,0:T(8,128)S(1)}, f32[16,2048]{1,0:T(8,128)}, u32[]{:S(2)}) copy-start(f32[16,2048]{1,0:T(8,128)} %param.20) | copy-start | bytes 393220
  56.6 12.5 %copy-start = (bf16[1,512,16,128]{1,3,2,0:T(8,128)(2,1)S(1)}, bf16[1,512,16,128]{1,3,2,0:T(8,128)(2,1)}, u32[]{:S(2)}) copy-start(bf16[1,512,16,128]{1,3,2,0:T(8,128)(2,1)} %copy.96) | copy-start | bytes 6291460 | tf_op jit(solution)/shard_map/while
  86.8 12.6 %copy-start = (bf16[1,512,16,128]{1,3,2,0:T(8,128)(2,1)S(1)}, bf16[1,512,16,128]{1,3,2,0:T(8,128)(2,1)}, u32[]{:S(2)}) copy-start(bf16[1,512,16,128]{1,3,2,0:T(8,128)(2,1)} %copy.96) | copy-start | bytes 6291460 | tf_op jit(solution)/shard_map/while
  117.0 12.5 %copy-start = (bf16[1,512,16,128]{1,3,2,0:T(8,128)(2,1)S(1)}, bf16[1,512,16,128]{1,3,2,0:T(8,128)(2,1)}, u32[]{:S(2)}) copy-start(bf16[1,512,16,128]{1,3,2,0:T(8,128)(2,1)} %copy.96) | copy-start | bytes 6291460 | tf_op jit(solution)/shard_map/while
  147.2 12.5 %copy-start = (bf16[1,512,16,128]{1,3,2,0:T(8,128)(2,1)S(1)}, bf16[1,512,16,128]{1,3,2,0:T(8,128)(2,1)}, u32[]{:S(2)}) copy-start(bf16[1,512,16,128]{1,3,2,0:T(8,128)(2,1)} %copy.96) | copy-start | bytes 6291460 | tf_op jit(solution)/shard_map/while
  178.0 25.9 %collective-permute-start = (f32[16,128,128]{2,1,0:T(8,128)S(1)}, f32[16,128,128]{2,1,0:T(8,128)S(1)}, u32[]{:S(2)}, u32[]{:S(2)}) collective-permute-start(f32[16,128,128]{2,1,0:T(8,128)S(1)} %multiply_add_fusion.3), channel_id=1, source_target_pairs={{0,2},{2,4},{4,6},{1,3},{3,5},{5,7},{8,10},{10,12},{12,14},{9,11},... | collective-permute-start | bytes 3145736 | tf_op jit(solution)/shard_map/while/body/eval_jaxpr/ppermute | solution.py:16
  204.1 25.0 %collective-permute-start = (f32[16,128,128]{2,1,0:T(8,128)S(1)}, f32[16,128,128]{2,1,0:T(8,128)S(1)}, u32[]{:S(2)}, u32[]{:S(2)}) collective-permute-start(f32[16,128,128]{2,1,0:T(8,128)S(1)} %multiply_add_fusion.3), channel_id=1, source_target_pairs={{0,2},{2,4},{4,6},{1,3},{3,5},{5,7},{8,10},{10,12},{12,14},{9,11},... | collective-permute-start | bytes 3145736 | tf_op jit(solution)/shard_map/while/body/eval_jaxpr/ppermute | solution.py:16
  229.3 24.1 %collective-permute-start = (f32[16,128,128]{2,1,0:T(8,128)S(1)}, f32[16,128,128]{2,1,0:T(8,128)S(1)}, u32[]{:S(2)}, u32[]{:S(2)}) collective-permute-start(f32[16,128,128]{2,1,0:T(8,128)S(1)} %multiply_add_fusion.3), channel_id=1, source_target_pairs={{0,2},{2,4},{4,6},{1,3},{3,5},{5,7},{8,10},{10,12},{12,14},{9,11},... | collective-permute-start | bytes 3145736 | tf_op jit(solution)/shard_map/while/body/eval_jaxpr/ppermute | solution.py:16
  303.0 10.6 %copy-start.3 = (s32[32]{0:T(128)S(1)}, s32[32]{0:T(128)}, u32[]{:S(2)}) copy-start(s32[32]{0:T(128)} %param.23) | copy-start | bytes 388
  303.0 11.7 %copy-start.2 = (f32[4096]{0:T(1024)S(1)}, f32[4096]{0:T(1024)}, u32[]{:S(2)}) copy-start(f32[4096]{0:T(1024)} %param.21) | copy-start | bytes 49156
where the time goes:
time: 565 us; the launch traced here: 561 us
  blocking collectives  204 us (36%)
  local copies, waits for them, and re-layouts  134 us (24%)
  matrix products  88.9 us (16%)
  waiting for transfers between devices  65.5 us (12%)
  other arithmetic  53.1 us (9%)
  starting transfers between devices  9.47 us (2%)
    all_to_all x1, blocking collectives, local(): lax.all_to_all(normed.reshape(blocks_dev, BLK, normed.shape[1])[block_ord...  185 us
    ppermute x3, waiting for transfers between devices, shifted(): return lax.ppermute(block, axis, route)  65.5 us
    dot_general x4, matrix products, block_terms(): jnp.einsum('htj,jhd->thd', weights_low, value_blk, preferred_element_type...  43.9 us
    dynamic_slice x16, local copies, waits for them, and re-layouts, local(): lax.map(local_block, (query_blocks, key_blocks, value_blocks, decay_block...  34.5 us
    unnamed x10, local copies, waits for them, and re-layouts  29.3 us
    dot_general x4, matrix products, finish_block(): jnp.einsum('thd,hde->the', query_blk.astype(jnp.float32), kv_state, preci...  26.2 us
    all_to_all x2, local copies, waits for them, and re-layouts, local(): lax.all_to_all(lax.all_to_all(normed.reshape(blocks_dev, BLK, normed.shap...  23.8 us
    dot_general x4, matrix products, block_terms(): jnp.einsum('jhd,jhe->hde', scaled_keys, value_blk, preferred_element_type...  18.8 us
  transfers between devices with their start and end apart: 3, of which 3 were waited for; matrix products, arithmetic and copies ran while one was open for 0% of the time, Pallas kernels for 0%

commit v1 on v0

v1 whole, which is shorter than its diff:
```python
import functools

import jax
import jax.numpy as jnp
from jax import lax
from jax.experimental import pallas as pl
from jax.experimental.pallas import tpu as pltpu
from jax.sharding import PartitionSpec as P

BLK = 256
norm_eps = 1e-05
VMEM_LIMIT = 56 * 2**20
F32 = jnp.float32
BF16 = jnp.bfloat16


def params():
    return pltpu.CompilerParams(vmem_limit_bytes=VMEM_LIMIT)


def whole(shape):
    return pl.BlockSpec(shape, lambda *_: (0,) * len(shape))


def pad8(count):
    return -(-count // 8) * 8


def gates_kernel(base_ref, len_ref, decay_ref, rows_ref, cols_ref, docs_ref, total_ref, scr):
    heads, tokens = decay_ref.shape
    hp = pad8(heads)
    chunks = tokens // BLK
    base = base_ref[0]
    starts, run = [], jnp.int32(0)
    for i in range(len_ref.shape[0]):
        starts.append(run)
        run = run + len_ref[i]

    def doc_at(position):
        found = jnp.int32(0)
        for start in starts:
            found = found + (position >= start).astype(jnp.int32)
        return found - 1

    position = base + lax.broadcasted_iota(jnp.int32, (8, tokens), 1)
    doc = jnp.zeros((8, tokens), jnp.int32) - 1
    for start in starts:
        doc = doc + (position >= start).astype(jnp.int32)
    docs_ref[...] = doc.astype(F32)
    edges = [doc_at(base - 1)] + [doc_at(base + (c + 1) * BLK - 1) for c in range(chunks)]

    first = lax.broadcasted_iota(jnp.int32, (BLK, BLK), 0)
    second = lax.broadcasted_iota(jnp.int32, (BLK, BLK), 1)
    upto = jnp.where(first <= second, 1.0, 0.0).astype(F32)
    every = jnp.ones((BLK, BLK), F32)
    scr[...] = jnp.zeros_like(scr)
    cums, sums = [], []
    for c in range(chunks):
        part = decay_ref[:, c * BLK : (c + 1) * BLK]
        cums.append(jnp.dot(part, upto, precision=lax.Precision.HIGHEST, preferred_element_type=F32))
        sums.append(jnp.dot(part, every, precision=lax.Precision.HIGHEST, preferred_element_type=F32))
    after = [None] * chunks
    run = jnp.zeros_like(sums[0])
    for c in reversed(range(chunks)):
        after[c] = run
        run = run + sums[c]
    for c in range(chunks):
        span = slice(c * BLK, (c + 1) * BLK)
        doc_c = doc[:1, span]
        cum, total = cums[c], sums[c]
        rows_ref[0:heads, span] = cum
        rows_ref[hp : hp + heads, span] = jnp.where(doc_c == edges[c + 1], jnp.exp(total - cum), 0.0)
        rows_ref[2 * hp : 2 * hp + heads, span] = jnp.where(
            doc_c == edges[-1], jnp.exp(total - cum + after[c]), 0.0
        )
        rows_ref[3 * hp : 3 * hp + heads, span] = jnp.where(
            edges[c + 1] == edges[c], jnp.exp(total), 0.0
        )
        scr[0:heads, span] = cum
        scr[hp : hp + heads, span] = jnp.where(doc_c == edges[c], jnp.exp(cum), 0.0)
    scr[2 * hp : 2 * hp + 8, :] = doc.astype(F32)
    cols_ref[...] = scr[...].T
    total_ref[...] = jnp.where(edges[-1] == edges[0], jnp.exp(run[:, :128]), 0.0)


def gates(base, doc_lengths, decay):
    heads, tokens = decay.shape
    hp = pad8(heads)
    smem = pl.BlockSpec(memory_space=pltpu.SMEM)
    vmem = pl.BlockSpec(memory_space=pltpu.VMEM)
    return pl.pallas_call(
        gates_kernel,
        in_specs=[smem, smem, vmem],
        out_specs=[vmem] * 4,
        out_shape=[
            jax.ShapeDtypeStruct((4 * hp, tokens), F32),
            jax.ShapeDtypeStruct((tokens, 128), F32),
            jax.ShapeDtypeStruct((8, tokens), F32),
            jax.ShapeDtypeStruct((heads, 128), F32),
        ],
        scratch_shapes=[pltpu.VMEM((128, tokens), F32)],
        compiler_params=params(),
        name="gates",
    )(base, doc_lengths, decay)


def totals_kernel(lo, hp, count, key_ref, value_ref, rows_ref, low_ref, full_ref, acc):
    step = pl.program_id(0)

    @pl.when(step == 0)
    def _():
        acc[...] = jnp.zeros_like(acc)

    for h in range(count):
        cols = slice(h * 128, (h + 1) * 128)
        tail = rows_ref[2 * hp + lo + h : 2 * hp + lo + h + 1, :]
        key_t = key_ref[:, cols].T.astype(F32)
        acc[h] += jnp.dot((key_t * tail).astype(BF16), value_ref[:, cols], preferred_element_type=F32)

    @pl.when(step == pl.num_programs(0) - 1)
    def _():
        low_ref[...] = acc[...].astype(BF16)
        full_ref[...] = acc[...]


def totals(key_rows, value_rows, rows, lo, count):
    tokens = key_rows.shape[0]
    hp = rows.shape[0] // 4
    tile = 2 * BLK
    width = count * 128
    at = lo * 128 // width
    return pl.pallas_call(
        functools.partial(totals_kernel, lo, hp, count),
        grid=(tokens // tile,),
        in_specs=[
            pl.BlockSpec((tile, width), lambda c: (c, at)),
            pl.BlockSpec((tile, width), lambda c: (c, at)),
            pl.BlockSpec((rows.shape[0], tile), lambda c: (0, c)),
        ],
        out_specs=[whole((count, 128, 128))] * 2,
        out_shape=[
            jax.ShapeDtypeStruct((count, 128, 128), BF16),
            jax.ShapeDtypeStruct((count, 128, 128), F32),
        ],
        scratch_shapes=[pltpu.VMEM((count, 128, 128), F32)],
        compiler_params=params(),
        cost_estimate=pl.CostEstimate(
            flops=2 * tokens * 128 * width, bytes_accessed=4 * tokens * width, transcendentals=0
        ),
        name="totals",
    )(key_rows, value_rows, rows)


def attend_kernel(lo, hp, count, ops, *refs):
    (which_ref, _, _, query_ref, key_ref, value_ref, gate_ref, gain_ref, rows_ref, cols_ref, docs_ref, state_ref) = refs[:12]
    outs = refs[12 : 12 + ops]
    square_ref, state, gated, squares = refs[12 + ops :]
    step = pl.program_id(0)

    @pl.when(step == 0)
    def _():
        state[...] = state_ref[...].astype(F32)

    first = lax.broadcasted_iota(jnp.int32, (BLK, BLK), 0)
    second = lax.broadcasted_iota(jnp.int32, (BLK, BLK), 1)
    same = cols_ref[:, 2 * hp : 2 * hp + 1] == docs_ref[0:1, :]
    barred = jnp.where((first >= second) & same, 0.0, -1e30).astype(F32)
    square = jnp.zeros((BLK, 128), F32)
    for h in range(count):
        head = lo + h
        cols = slice(h * 128, (h + 1) * 128)
        query, value = query_ref[:, cols], value_ref[:, cols]
        key_t = key_ref[:, cols].T
        scores = jnp.dot(query, key_t, preferred_element_type=F32)
        gap = cols_ref[:, head : head + 1] - rows_ref[head : head + 1, :] + barred
        weights = (scores * jnp.exp(gap)).astype(BF16)
        intra = jnp.dot(weights, value, preferred_element_type=F32)
        reached = jnp.dot(query, state[h].astype(BF16), preferred_element_type=F32)
        attended = (intra + cols_ref[:, hp + head : hp + head + 1] * reached).astype(BF16).astype(F32)
        scaled = (key_t.astype(F32) * rows_ref[hp + head : hp + head + 1, :]).astype(BF16)
        carry = rows_ref[3 * hp + head : 3 * hp + head + 1, :128]
        state[h] = carry * state[h] + jnp.dot(scaled, value, preferred_element_type=F32)
        square = square + attended * attended
        gated[:, cols] = (
            attended * gain_ref[0:1, cols] * jax.nn.sigmoid(gate_ref[:, cols].astype(F32))
        ).astype(BF16)
    square_ref[0] = jnp.sum(square.T, axis=0, keepdims=True)
    for op in range(ops):

        @pl.when(which_ref[step] == op)
        def _():
            outs[op][0] = gated[...]


def attend(tables, query, key, value, gate, gain, rows, cols, docs, entering, lo, count):
    tokens = query.shape[0]
    chunks = tokens // BLK
    hp = rows.shape[0] // 4
    width = count * 128
    at = lo * 128 // width
    which, place, slot = tables
    ops = place.shape[0] // chunks
    per = chunks // ops
    wide = pl.BlockSpec((BLK, width), lambda c, *_: (c, at))

    def out_map(op, c, which_ref, place_ref, slot_ref):
        return (place_ref[op * chunks + c], 0, 0)

    out = pl.pallas_call(
        functools.partial(attend_kernel, lo, hp, count, ops),
        grid_spec=pltpu.PrefetchScalarGridSpec(
            num_scalar_prefetch=3,
            grid=(chunks,),
            in_specs=[
                wide,
                wide,
                wide,
                wide,
                pl.BlockSpec((1, width), lambda c, *_: (0, at)),
                pl.BlockSpec((rows.shape[0], BLK), lambda c, *_: (0, c)),
                pl.BlockSpec((BLK, 128), lambda c, *_: (c, 0)),
                pl.BlockSpec((8, BLK), lambda c, *_: (0, c)),
                whole((count, 128, 128)),
            ],
            out_specs=[
                pl.BlockSpec((1, BLK, width), functools.partial(out_map, op)) for op in range(ops)
            ]
            + [pl.BlockSpec((1, 1, BLK), lambda c, which_ref, place_ref, slot_ref: (slot_ref[c], 0, 0))],
            scratch_shapes=[
                pltpu.VMEM((count, 128, 128), F32),
                pltpu.VMEM((BLK, width), BF16),
                pltpu.VMEM((8, 128), F32),
            ],
        ),
        out_shape=[jax.ShapeDtypeStruct((per, BLK, width), BF16)] * ops
        + [jax.ShapeDtypeStruct((chunks, 1, BLK), F32)],
        compiler_params=params(),
        cost_estimate=pl.CostEstimate(
            flops=2 * tokens * width * (2 * BLK + 256),
            bytes_accessed=10 * tokens * width,
            transcendentals=tokens * count * (BLK + 128),
        ),
        name="attend",
    )(which, place, slot, query, key, value, gate, gain, rows, cols, docs, entering)
    return out[:ops], out[ops]


def place_kernel(features, pos_ref, piece_ref, square_ref, *refs):
    out_ref = refs[-1]
    scale = lax.rsqrt(square_ref[0] / features + norm_eps)
    scale = jnp.broadcast_to(scale, (128, BLK)).T
    for c in range(out_ref.shape[1] // 128):
        cols = slice(c * 128, (c + 1) * 128)
        out_ref[:, cols] = (piece_ref[0, :, cols].astype(F32) * scale).astype(BF16)


def place(position, piece, square, out, shape, features, unit):
    per, _, width = piece.shape
    in_specs = [
        pl.BlockSpec((1, BLK, unit), lambda k, j, pos: (k, 0, j)),
        pl.BlockSpec((1, 1, BLK), lambda k, j, pos: (k, 0, 0)),
    ]
    operands = [position, piece, square]
    aliases = {}
    if out is not None:
        in_specs.append(pl.BlockSpec(memory_space=pl.ANY))
        operands.append(out)
        aliases = {3: 0}
    return pl.pallas_call(
        functools.partial(place_kernel, features),
        grid_spec=pltpu.PrefetchScalarGridSpec(
            num_scalar_prefetch=1,
            grid=(per, width // unit),
            in_specs=in_specs,
            out_specs=pl.BlockSpec((BLK, unit), lambda k, j, pos: (pos[0] + k, pos[1] + j)),
        ),
        out_shape=jax.ShapeDtypeStruct(shape, BF16),
        input_output_aliases=aliases,
        compiler_params=params(),
        cost_estimate=pl.CostEstimate(
            flops=per * BLK * width, bytes_accessed=4 * per * BLK * width, transcendentals=0
        ),
        name="place",
    )(*operands)


def local(query_rows, key_rows, value_rows, gate_rows, decay_log, norm_gain, doc_lengths, block_shard):
    tokens, width = query_rows.shape
    heads = decay_log.shape[0]
    chunks = tokens // BLK
    features = norm_gain.shape[0]
    n, t = lax.axis_size("ctx"), lax.axis_size("tp")
    stride = n // t
    per = chunks // n
    ctx, tp = lax.axis_index("ctx"), lax.axis_index("tp")
    quarter = max(1, heads // 4)
    groups = [(lo, quarter) for lo in range(0, heads, quarter)]

    base = (ctx * tokens).astype(jnp.int32).reshape(1)
    rows, cols, docs, total_gate = gates(base, doc_lengths, decay_log)

    shards = lax.dynamic_slice_in_dim(block_shard, ctx * chunks, chunks)
    which = jnp.mod(shards - ctx - tp * stride, n).astype(jnp.int32)
    index = jnp.arange(chunks)
    earlier = index[None, :] < index[:, None]
    ranks = jnp.sum((earlier & (which[None, :] == which[:, None])).astype(jnp.int32), axis=1)
    seen = jnp.sum(
        (earlier[None] & (which[None, None, :] == jnp.arange(n)[:, None, None])).astype(jnp.int32), axis=2
    )
    tables = (which, jnp.minimum(seen, per - 1).reshape(-1), which * per + jnp.minimum(ranks, per - 1))
    gain = lax.dynamic_slice_in_dim(norm_gain, tp * width, width).reshape(1, width)

    hop = [(i, i + 1) for i in range(n - 1)]

    def route(op):
        return [
            (d * t + k, (d + op + k * stride) % n * t + d // stride) for d in range(n) for k in range(t)
        ]

    pieces, squares = [], None
    for lo, count in groups:
        low, full = totals(key_rows, value_rows, rows, lo, count)
        carry = total_gate[lo : lo + count, :1, None]
        entering = lax.ppermute(low, "ctx", hop)
        for _ in range(max(1, n // 2) - 1):
            entering = lax.ppermute((carry * entering.astype(F32) + full).astype(BF16), "ctx", hop)
        outs, square = attend(
            tables, query_rows, key_rows, value_rows, gate_rows, gain, rows, cols, docs, entering, lo, count
        )
        squares = square if squares is None else squares + square
        pieces.append([lax.ppermute(outs[op], ("ctx", "tp"), route(op)) for op in range(n)])

    halves = [
        lax.ppermute(squares[op * per : (op + 1) * per], ("ctx", "tp"), route(op)) for op in range(n)
    ]
    joined = [sum(halves[op + k * stride] for k in range(t)) for op in range(stride)]

    unit = quarter * 128
    shape = (tokens // t, features)
    out = None
    for (lo, count), received in zip(groups, pieces):
        for op in range(n):
            lane = jnp.mod(ctx - op, stride)
            source = tp * stride + lane
            half = jnp.mod(ctx - op - source, n) // stride
            position = jnp.stack([lane * per, (half * width + lo * 128) // unit]).astype(jnp.int32)
            out = place(position, received[op], joined[op % stride], out, shape, features, unit)
    return out


def solution(mesh):
    return jax.shard_map(
        local,
        mesh=mesh,
        in_specs=(
            P(("dp", "ctx"), "tp"),
            P(("dp", "ctx"), "tp"),
            P(("dp", "ctx"), "tp"),
            P(("dp", "ctx"), "tp"),
            P("tp", ("dp", "ctx")),
            P(),
            P("dp"),
            P("dp"),
        ),
        out_specs=P(("dp", "ctx", "tp"), None),
        check_vma=False,
    )
```

time: 565 us -> 306 us (0.54)
  the two profiles are of different devices: /device:TPU:9 before, /device:TPU:0 now
where the time goes in v1:
time: 306 us; the launch traced here: 303 us
  starting transfers between devices  163 us (53%)
  Pallas kernels  111 us (36%)
  other arithmetic  13.6 us (4%)
  waiting for transfers between devices  10.5 us (3%)
  local copies, waits for them, and re-layouts  4.02 us (1%)
    ppermute x16, starting transfers between devices, local(): lax.ppermute(outs[op], ('ctx', 'tp'), route(op))  134 us
    pallas_call x4, Pallas kernels, attend(): pl.pallas_call(functools.partial(attend_kernel, lo, hp, count, ops), grid...  47.8 us
    pallas_call x16, Pallas kernels, place(): pl.pallas_call(functools.partial(place_kernel, features), grid_spec=pltpu...  41.8 us
    pallas_call x4, Pallas kernels, totals(): pl.pallas_call(functools.partial(totals_kernel, lo, hp, count), grid=(tok...  17.8 us
    ppermute x4, starting transfers between devices, local(): entering = lax.ppermute(low, 'ctx', hop)  13.9 us
    ppermute x16, waiting for transfers between devices, local(): lax.ppermute(outs[op], ('ctx', 'tp'), route(op))  10.5 us
    another operation x15, other arithmetic, local(): jnp.stack([lane * per, (half * width + lo * 128) // unit]).astype(jnp.int32)  9.24 us
    ppermute x4, starting transfers between devices, local(): lax.ppermute((carry * entering.astype(F32) + full).astype(BF16), 'ctx', hop)  7.68 us
  transfers between devices with their start and end apart: 28, of which 2 were waited for; matrix products, arithmetic and copies ran while one was open for 5% of the time, Pallas kernels for 33%

profile of v1, /device:TPU:0, one launch (start us, length us, event | category | flops | bytes accessed | tf_op | source)
XLA Modules:
  0.0 303.0 jit_solution(10183763904401166318)
XLA Ops:
  0.0 3.6 %gates.1 = (f32[64,2048]{1,0:T(8,128)}, f32[2048,128]{1,0:T(8,128)}, f32[8,2048]{1,0:T(8,128)}, f32[16,128]{1,0:T(8,128)}) custom-call(s32[1]{0:T(128)} %bitcast.3.base_ref, s32[16]{0:T(128)} %len_ref.1, f32[16,2048]{1,0:T(8,128)} %decay_ref.1), custom_call_target="tpu_custom_call" | custom-call | tf_op jit(solution)/shard_map/gates/pallas_call | solution.py:91
  3.6 4.4 %totals.6 = (bf16[4,128,128]{2,1,0:T(8,128)(2,1)}, f32[4,128,128]{2,1,0:T(8,128)}) custom-call(bf16[2048,2048]{1,0:T(8,128)(2,1)} %refs_4_.7, bf16[2048,2048]{1,0:T(8,128)(2,1)} %refs_5_.7, f32[64,2048]{1,0:T(8,128)} %get-tuple-element.37.rows_ref.refs_8_), custom_call_target="tpu_custom_call" | custom-call | flops 268435456 | bytes 4194304 | tf_op jit(solution)/shard_map/totals/pallas_call | solution.py:132
  8.0 4.9 %collective-permute-start.5 = (bf16[4,128,128]{2,1,0:T(8,128)(2,1)}, bf16[4,128,128]{2,1,0:T(8,128)(2,1)S(1)}, u32[]{:S(2)}, u32[]{:S(2)}) collective-permute-start(bf16[4,128,128]{2,1,0:T(8,128)(2,1)} %get-tuple-element.47), channel_id=1, source_target_pairs={{0,2},{2,4},{4,6},{1,3},{3,5},{5,7},{8,10},{10,12},{12,14},{9,11},... | collective-permute-start | bytes 393224 | tf_op jit(solution)/shard_map/ppermute | solution.py:324
  12.9 4.4 %totals.5 = (bf16[4,128,128]{2,1,0:T(8,128)(2,1)}, f32[4,128,128]{2,1,0:T(8,128)}) custom-call(bf16[2048,2048]{1,0:T(8,128)(2,1)} %refs_4_.7, bf16[2048,2048]{1,0:T(8,128)(2,1)} %refs_5_.7, f32[64,2048]{1,0:T(8,128)} %get-tuple-element.37.rows_ref.refs_8_), custom_call_target="tpu_custom_call" | custom-call | flops 268435456 | bytes 4194304 | tf_op jit(solution)/shard_map/totals/pallas_call | solution.py:132
  17.4 3.5 %collective-permute-start.3 = (bf16[4,128,128]{2,1,0:T(8,128)(2,1)}, bf16[4,128,128]{2,1,0:T(8,128)(2,1)S(1)}, u32[]{:S(2)}, u32[]{:S(2)}) collective-permute-start(bf16[4,128,128]{2,1,0:T(8,128)(2,1)} %get-tuple-element.44), channel_id=1, source_target_pairs={{0,2},{2,4},{4,6},{1,3},{3,5},{5,7},{8,10},{10,12},{12,14},{9,11},... | collective-permute-start | bytes 393224 | tf_op jit(solution)/shard_map/ppermute | solution.py:324
  20.9 4.4 %totals.7 = (bf16[4,128,128]{2,1,0:T(8,128)(2,1)}, f32[4,128,128]{2,1,0:T(8,128)}) custom-call(bf16[2048,2048]{1,0:T(8,128)(2,1)} %refs_4_.7, bf16[2048,2048]{1,0:T(8,128)(2,1)} %refs_5_.7, f32[64,2048]{1,0:T(8,128)} %get-tuple-element.37.rows_ref.refs_8_), custom_call_target="tpu_custom_call" | custom-call | flops 268435456 | bytes 4194304 | tf_op jit(solution)/shard_map/totals/pallas_call | solution.py:132
  25.3 3.6 %collective-permute-start.7 = (bf16[4,128,128]{2,1,0:T(8,128)(2,1)}, bf16[4,128,128]{2,1,0:T(8,128)(2,1)S(1)}, u32[]{:S(2)}, u32[]{:S(2)}) collective-permute-start(bf16[4,128,128]{2,1,0:T(8,128)(2,1)} %get-tuple-element.50), channel_id=1, source_target_pairs={{0,2},{2,4},{4,6},{1,3},{3,5},{5,7},{8,10},{10,12},{12,14},{9,11},... | collective-permute-start | bytes 393224 | tf_op jit(solution)/shard_map/ppermute | solution.py:324
  29.0 4.5 %totals.4 = (bf16[4,128,128]{2,1,0:T(8,128)(2,1)}, f32[4,128,128]{2,1,0:T(8,128)}) custom-call(bf16[2048,2048]{1,0:T(8,128)(2,1)} %refs_4_.7, bf16[2048,2048]{1,0:T(8,128)(2,1)} %refs_5_.7, f32[64,2048]{1,0:T(8,128)} %get-tuple-element.37.rows_ref.refs_8_), custom_call_target="tpu_custom_call" | custom-call | flops 268435456 | bytes 4194304 | tf_op jit(solution)/shard_map/totals/pallas_call | solution.py:132
  48.1 12.0 %attend.5 = (bf16[2,256,512]{2,1,0:T(8,128)(2,1)}, bf16[2,256,512]{2,1,0:T(8,128)(2,1)}, bf16[2,256,512]{2,1,0:T(8,128)(2,1)}, bf16[2,256,512]{2,1,0:T(8,128)(2,1)}, f32[8,1,256]{2,1,0:T(1,128)}) custom-call(s32[8]{0:T(128)} %copy-done.13, s32[32]{0:T(128)} %min.15.refs_1_, s32[8]{0:T(128)} %minimum_add_fusion.refs_2_, bf16[2048,2048]{1,0:T(8,128)(2,1)} %refs_3_.7, ...), custom_call_target="tpu_custom_call" | custom-call | flops 1610612736 | bytes 10485760 | tf_op jit(solution)/shard_map/attend/pallas_call | solution.py:209
  62.4 11.9 %attend.6 = (bf16[2,256,512]{2,1,0:T(8,128)(2,1)}, bf16[2,256,512]{2,1,0:T(8,128)(2,1)}, bf16[2,256,512]{2,1,0:T(8,128)(2,1)}, bf16[2,256,512]{2,1,0:T(8,128)(2,1)}, f32[8,1,256]{2,1,0:T(1,128)}) custom-call(s32[8]{0:T(128)} %copy-done.13, s32[32]{0:T(128)} %min.15.refs_1_, s32[8]{0:T(128)} %minimum_add_fusion.refs_2_, bf16[2048,2048]{1,0:T(8,128)(2,1)} %refs_3_.7, ...), custom_call_target="tpu_custom_call" | custom-call | flops 1610612736 | bytes 10485760 | tf_op jit(solution)/shard_map/attend/pallas_call | solution.py:209
  75.0 12.0 %attend.7 = (bf16[2,256,512]{2,1,0:T(8,128)(2,1)}, bf16[2,256,512]{2,1,0:T(8,128)(2,1)}, bf16[2,256,512]{2,1,0:T(8,128)(2,1)}, bf16[2,256,512]{2,1,0:T(8,128)(2,1)}, f32[8,1,256]{2,1,0:T(1,128)}) custom-call(s32[8]{0:T(128)} %copy-done.13, s32[32]{0:T(128)} %min.15.refs_1_, s32[8]{0:T(128)} %minimum_add_fusion.refs_2_, bf16[2048,2048]{1,0:T(8,128)(2,1)} %refs_3_.7, ...), custom_call_target="tpu_custom_call" | custom-call | flops 1610612736 | bytes 10485760 | tf_op jit(solution)/shard_map/attend/pallas_call | solution.py:209
  87.7 11.9 %attend.4 = (bf16[2,256,512]{2,1,0:T(8,128)(2,1)}, bf16[2,256,512]{2,1,0:T(8,128)(2,1)}, bf16[2,256,512]{2,1,0:T(8,128)(2,1)}, bf16[2,256,512]{2,1,0:T(8,128)(2,1)}, f32[8,1,256]{2,1,0:T(1,128)}) custom-call(s32[8]{0:T(128)} %copy-done.13, s32[32]{0:T(128)} %min.15.refs_1_, s32[8]{0:T(128)} %minimum_add_fusion.refs_2_, bf16[2048,2048]{1,0:T(8,128)(2,1)} %refs_3_.7, ...), custom_call_target="tpu_custom_call" | custom-call | flops 1610612736 | bytes 10485760 | tf_op jit(solution)/shard_map/attend/pallas_call | solution.py:209
  101.0 4.8 %collective-permute-start.13 = (f32[2,1,256]{2,1,0:T(1,128)S(1)}, f32[2,1,256]{2,1,0:T(1,128)S(1)}, u32[]{:S(2)}, u32[]{:S(2)}) collective-permute-start(f32[2,1,256]{2,1,0:T(1,128)S(1)} %get-tuple-element.73), channel_id=1, source_target_pairs={{0,4},{1,0},{2,6},{3,2},{4,1},{5,5},{6,3},{7,7},{8,12},{9,8},{10,1... | collective-permute-start | bytes 6152 | tf_op jit(solution)/shard_map/ppermute | solution.py:334
  108.6 3.6 %collective-permute-start.25 = (bf16[2,256,512]{2,1,0:T(8,128)(2,1)}, bf16[2,256,512]{2,1,0:T(8,128)(2,1)S(1)}, u32[]{:S(2)}, u32[]{:S(2)}) collective-permute-start(bf16[2,256,512]{2,1,0:T(8,128)(2,1)} %get-tuple-element.66), channel_id=1, source_target_pairs={{0,4},{1,0},{2,6},{3,2},{4,1},{5,5},{6,3},{7,7},{8,12},{9,8},{10,1... | collective-permute-start | bytes 1572872 | tf_op jit(solution)/shard_map/ppermute | solution.py:331
  119.2 10.4 %collective-permute-done.26.piece_ref = bf16[2,256,512]{2,1,0:T(8,128)(2,1)S(1)} collective-permute-done((bf16[2,256,512]{2,1,0:T(8,128)(2,1)}, bf16[2,256,512]{2,1,0:T(8,128)(2,1)S(1)}, u32[]{:S(2)}, u32[]{:S(2)}) %collective-permute-start.26) | collective-permute-done | bytes 524320 | tf_op jit(solution)/shard_map/ppermute | solution.py:331
  131.6 35.3 %collective-permute-start.20 = (bf16[2,256,512]{2,1,0:T(8,128)(2,1)}, bf16[2,256,512]{2,1,0:T(8,128)(2,1)}, u32[]{:S(2)}, u32[]{:S(2)}) collective-permute-start(bf16[2,256,512]{2,1,0:T(8,128)(2,1)} %get-tuple-element.61), channel_id=1, source_target_pairs={{0,6},{1,2},{2,0},{3,4},{4,3},{5,7},{6,5},{7,1},{8,14},{9,10},{10,... | collective-permute-start | bytes 1572872 | tf_op jit(solution)/shard_map/ppermute | solution.py:331
  166.8 5.4 %collective-permute-start.19 = (bf16[2,256,512]{2,1,0:T(8,128)(2,1)}, bf16[2,256,512]{2,1,0:T(8,128)(2,1)}, u32[]{:S(2)}, u32[]{:S(2)}) collective-permute-start(bf16[2,256,512]{2,1,0:T(8,128)(2,1)} %get-tuple-element.60), channel_id=1, source_target_pairs={{0,0},{1,4},{2,2},{3,6},{4,5},{5,1},{6,7},{7,3},{8,8},{9,12},{10,1... | collective-permute-start | bytes 1572872 | tf_op jit(solution)/shard_map/ppermute | solution.py:331
  172.3 12.9 %collective-permute-start.17 = (bf16[2,256,512]{2,1,0:T(8,128)(2,1)}, bf16[2,256,512]{2,1,0:T(8,128)(2,1)}, u32[]{:S(2)}, u32[]{:S(2)}) collective-permute-start(bf16[2,256,512]{2,1,0:T(8,128)(2,1)} %get-tuple-element.58), channel_id=1, source_target_pairs={{0,4},{1,0},{2,6},{3,2},{4,1},{5,5},{6,3},{7,7},{8,12},{9,8},{10,1... | collective-permute-start | bytes 1572872 | tf_op jit(solution)/shard_map/ppermute | solution.py:331
  188.1 23.8 %collective-permute-start.16 = (bf16[2,256,512]{2,1,0:T(8,128)(2,1)}, bf16[2,256,512]{2,1,0:T(8,128)(2,1)}, u32[]{:S(2)}, u32[]{:S(2)}) collective-permute-start(bf16[2,256,512]{2,1,0:T(8,128)(2,1)} %get-tuple-element.57), channel_id=1, source_target_pairs={{0,6},{1,2},{2,0},{3,4},{4,3},{5,7},{6,5},{7,1},{8,14},{9,10},{10,... | collective-permute-start | bytes 1572872 | tf_op jit(solution)/shard_map/ppermute | solution.py:331
  211.9 5.4 %collective-permute-start.15 = (bf16[2,256,512]{2,1,0:T(8,128)(2,1)}, bf16[2,256,512]{2,1,0:T(8,128)(2,1)}, u32[]{:S(2)}, u32[]{:S(2)}) collective-permute-start(bf16[2,256,512]{2,1,0:T(8,128)(2,1)} %get-tuple-element.56), channel_id=1, source_target_pairs={{0,0},{1,4},{2,2},{3,6},{4,5},{5,1},{6,7},{7,3},{8,8},{9,12},{10,1... | collective-permute-start | bytes 1572872 | tf_op jit(solution)/shard_map/ppermute | solution.py:331
  217.3 12.9 %collective-permute-start.11 = (bf16[2,256,512]{2,1,0:T(8,128)(2,1)}, bf16[2,256,512]{2,1,0:T(8,128)(2,1)}, u32[]{:S(2)}, u32[]{:S(2)}) collective-permute-start(bf16[2,256,512]{2,1,0:T(8,128)(2,1)} %get-tuple-element.54), channel_id=1, source_target_pairs={{0,4},{1,0},{2,6},{3,2},{4,1},{5,5},{6,3},{7,7},{8,12},{9,8},{10,1... | collective-permute-start | bytes 1572872 | tf_op jit(solution)/shard_map/ppermute | solution.py:331
  230.2 26.7 %collective-permute-start.2 = (bf16[2,256,512]{2,1,0:T(8,128)(2,1)}, bf16[2,256,512]{2,1,0:T(8,128)(2,1)}, u32[]{:S(2)}, u32[]{:S(2)}) collective-permute-start(bf16[2,256,512]{2,1,0:T(8,128)(2,1)} %get-tuple-element.43), channel_id=1, source_target_pairs={{0,6},{1,2},{2,0},{3,4},{4,3},{5,7},{6,5},{7,1},{8,14},{9,10},{10,... | collective-permute-start | bytes 1572872 | tf_op jit(solution)/shard_map/ppermute | solution.py:331
  265.7 2.6 place.18.refs_0_
  289.9 2.6 place.27.refs_0_
  (130 shorter events, 74.7 us)
Async XLA Ops:
  8.0 30.3 %collective-permute-start.5 = (bf16[4,128,128]{2,1,0:T(8,128)(2,1)}, bf16[4,128,128]{2,1,0:T(8,128)(2,1)S(1)}, u32[]{:S(2)}, u32[]{:S(2)}) collective-permute-start(bf16[4,128,128]{2,1,0:T(8,128)(2,1)} %get-tuple-element.47), channel_id=1, source_target_pairs={{0,2},{2,4},{4,6},{1,3},{3,5},{5,7},{8,10},{10,12},{12,14},{9,11},... | collective-permute-start | bytes 393224 | tf_op jit(solution)/shard_map/ppermute | solution.py:324
  17.4 23.0 %collective-permute-start.3 = (bf16[4,128,128]{2,1,0:T(8,128)(2,1)}, bf16[4,128,128]{2,1,0:T(8,128)(2,1)S(1)}, u32[]{:S(2)}, u32[]{:S(2)}) collective-permute-start(bf16[4,128,128]{2,1,0:T(8,128)(2,1)} %get-tuple-element.44), channel_id=1, source_target_pairs={{0,2},{2,4},{4,6},{1,3},{3,5},{5,7},{8,10},{10,12},{12,14},{9,11},... | collective-permute-start | bytes 393224 | tf_op jit(solution)/shard_map/ppermute | solution.py:324
  25.3 17.0 %collective-permute-start.7 = (bf16[4,128,128]{2,1,0:T(8,128)(2,1)}, bf16[4,128,128]{2,1,0:T(8,128)(2,1)S(1)}, u32[]{:S(2)}, u32[]{:S(2)}) collective-permute-start(bf16[4,128,128]{2,1,0:T(8,128)(2,1)} %get-tuple-element.50), channel_id=1, source_target_pairs={{0,2},{2,4},{4,6},{1,3},{3,5},{5,7},{8,10},{10,12},{12,14},{9,11},... | collective-permute-start | bytes 393224 | tf_op jit(solution)/shard_map/ppermute | solution.py:324
  33.4 11.0 %collective-permute-start = (bf16[4,128,128]{2,1,0:T(8,128)(2,1)}, bf16[4,128,128]{2,1,0:T(8,128)(2,1)S(1)}, u32[]{:S(2)}, u32[]{:S(2)}) collective-permute-start(bf16[4,128,128]{2,1,0:T(8,128)(2,1)} %get-tuple-element.41), channel_id=1, source_target_pairs={{0,2},{2,4},{4,6},{1,3},{3,5},{5,7},{8,10},{10,12},{12,14},{9,11},... | collective-permute-start | bytes 393224 | tf_op jit(solution)/shard_map/ppermute | solution.py:324
  38.4 23.4 %collective-permute-start.6 = (bf16[4,128,128]{2,1,0:T(8,128)(2,1)S(1)}, bf16[4,128,128]{2,1,0:T(8,128)(2,1)S(1)}, u32[]{:S(2)}, u32[]{:S(2)}) collective-permute-start(bf16[4,128,128]{2,1,0:T(8,128)(2,1)S(1)} %add_convert_fusion.1), channel_id=1, source_target_pairs={{0,2},{2,4},{4,6},{1,3},{3,5},{5,7},{8,10},{10,12},{12,14},{9,11},... | collective-permute-start | bytes 393224 | tf_op jit(solution)/shard_map/ppermute | solution.py:326
  42.5 31.9 %collective-permute-start.8 = (bf16[4,128,128]{2,1,0:T(8,128)(2,1)S(1)}, bf16[4,128,128]{2,1,0:T(8,128)(2,1)S(1)}, u32[]{:S(2)}, u32[]{:S(2)}) collective-permute-start(bf16[4,128,128]{2,1,0:T(8,128)(2,1)S(1)} %add_convert_fusion), channel_id=1, source_target_pairs={{0,2},{2,4},{4,6},{1,3},{3,5},{5,7},{8,10},{10,12},{12,14},{9,11},... | collective-permute-start | bytes 393224 | tf_op jit(solution)/shard_map/ppermute | solution.py:326
  45.5 41.5 %collective-permute-start.1 = (bf16[4,128,128]{2,1,0:T(8,128)(2,1)S(1)}, bf16[4,128,128]{2,1,0:T(8,128)(2,1)S(1)}, u32[]{:S(2)}, u32[]{:S(2)}) collective-permute-start(bf16[4,128,128]{2,1,0:T(8,128)(2,1)S(1)} %add_convert_fusion.3), channel_id=1, source_target_pairs={{0,2},{2,4},{4,6},{1,3},{3,5},{5,7},{8,10},{10,12},{12,14},{9,11},... | collective-permute-start | bytes 393224 | tf_op jit(solution)/shard_map/ppermute | solution.py:326
  60.1 55.6 %collective-permute-start.27 = (bf16[2,256,512]{2,1,0:T(8,128)(2,1)}, bf16[2,256,512]{2,1,0:T(8,128)(2,1)S(1)}, u32[]{:S(2)}, u32[]{:S(2)}) collective-permute-start(bf16[2,256,512]{2,1,0:T(8,128)(2,1)} %get-tuple-element.68), channel_id=1, source_target_pairs={{0,0},{1,4},{2,2},{3,6},{4,5},{5,1},{6,7},{7,3},{8,8},{9,12},{10,1... | collective-permute-start | bytes 1572872 | tf_op jit(solution)/shard_map/ppermute | solution.py:331
  101.0 7.6 %collective-permute-start.13 = (f32[2,1,256]{2,1,0:T(1,128)S(1)}, f32[2,1,256]{2,1,0:T(1,128)S(1)}, u32[]{:S(2)}, u32[]{:S(2)}) collective-permute-start(f32[2,1,256]{2,1,0:T(1,128)S(1)} %get-tuple-element.73), channel_id=1, source_target_pairs={{0,4},{1,0},{2,6},{3,2},{4,1},{5,5},{6,3},{7,7},{8,12},{9,8},{10,1... | collective-permute-start | bytes 6152 | tf_op jit(solution)/shard_map/ppermute | solution.py:334
  107.9 21.7 %collective-permute-start.26 = (bf16[2,256,512]{2,1,0:T(8,128)(2,1)}, bf16[2,256,512]{2,1,0:T(8,128)(2,1)S(1)}, u32[]{:S(2)}, u32[]{:S(2)}) collective-permute-start(bf16[2,256,512]{2,1,0:T(8,128)(2,1)} %get-tuple-element.67), channel_id=1, source_target_pairs={{0,2},{1,6},{2,4},{3,0},{4,7},{5,3},{6,1},{7,5},{8,10},{9,14},{10,... | collective-permute-start | bytes 1572872 | tf_op jit(solution)/shard_map/ppermute | solution.py:331
  108.6 23.0 %collective-permute-start.25 = (bf16[2,256,512]{2,1,0:T(8,128)(2,1)}, bf16[2,256,512]{2,1,0:T(8,128)(2,1)S(1)}, u32[]{:S(2)}, u32[]{:S(2)}) collective-permute-start(bf16[2,256,512]{2,1,0:T(8,128)(2,1)} %get-tuple-element.66), channel_id=1, source_target_pairs={{0,4},{1,0},{2,6},{3,2},{4,1},{5,5},{6,3},{7,7},{8,12},{9,8},{10,1... | collective-permute-start | bytes 1572872 | tf_op jit(solution)/shard_map/ppermute | solution.py:331
  112.2 54.6 %collective-permute-start.24 = (bf16[2,256,512]{2,1,0:T(8,128)(2,1)}, bf16[2,256,512]{2,1,0:T(8,128)(2,1)S(1)}, u32[]{:S(2)}, u32[]{:S(2)}) collective-permute-start(bf16[2,256,512]{2,1,0:T(8,128)(2,1)} %get-tuple-element.65), channel_id=1, source_target_pairs={{0,6},{1,2},{2,0},{3,4},{4,3},{5,7},{6,5},{7,1},{8,14},{9,10},{10,... | collective-permute-start | bytes 1572872 | tf_op jit(solution)/shard_map/ppermute | solution.py:331
  114.0 58.2 %collective-permute-start.23 = (bf16[2,256,512]{2,1,0:T(8,128)(2,1)}, bf16[2,256,512]{2,1,0:T(8,128)(2,1)S(1)}, u32[]{:S(2)}, u32[]{:S(2)}) collective-permute-start(bf16[2,256,512]{2,1,0:T(8,128)(2,1)} %get-tuple-element.64), channel_id=1, source_target_pairs={{0,0},{1,4},{2,2},{3,6},{4,5},{5,1},{6,7},{7,3},{8,8},{9,12},{10,1... | collective-permute-start | bytes 1572872 | tf_op jit(solution)/shard_map/ppermute | solution.py:331
  115.7 56.5 %collective-permute-start.22 = (bf16[2,256,512]{2,1,0:T(8,128)(2,1)}, bf16[2,256,512]{2,1,0:T(8,128)(2,1)S(1)}, u32[]{:S(2)}, u32[]{:S(2)}) collective-permute-start(bf16[2,256,512]{2,1,0:T(8,128)(2,1)} %get-tuple-element.63), channel_id=1, source_target_pairs={{0,2},{1,6},{2,4},{3,0},{4,7},{5,3},{6,1},{7,5},{8,10},{9,14},{10,... | collective-permute-start | bytes 1572872 | tf_op jit(solution)/shard_map/ppermute | solution.py:331
  129.6 58.5 %collective-permute-start.21 = (bf16[2,256,512]{2,1,0:T(8,128)(2,1)}, bf16[2,256,512]{2,1,0:T(8,128)(2,1)}, u32[]{:S(2)}, u32[]{:S(2)}) collective-permute-start(bf16[2,256,512]{2,1,0:T(8,128)(2,1)} %get-tuple-element.62), channel_id=1, source_target_pairs={{0,4},{1,0},{2,6},{3,2},{4,1},{5,5},{6,3},{7,7},{8,12},{9,8},{10,1... | collective-permute-start | bytes 1572872 | tf_op jit(solution)/shard_map/ppermute | solution.py:331
  131.6 80.3 %collective-permute-start.20 = (bf16[2,256,512]{2,1,0:T(8,128)(2,1)}, bf16[2,256,512]{2,1,0:T(8,128)(2,1)}, u32[]{:S(2)}, u32[]{:S(2)}) collective-permute-start(bf16[2,256,512]{2,1,0:T(8,128)(2,1)} %get-tuple-element.61), channel_id=1, source_target_pairs={{0,6},{1,2},{2,0},{3,4},{4,3},{5,7},{6,5},{7,1},{8,14},{9,10},{10,... | collective-permute-start | bytes 1572872 | tf_op jit(solution)/shard_map/ppermute | solution.py:331
  166.8 50.4 %collective-permute-start.19 = (bf16[2,256,512]{2,1,0:T(8,128)(2,1)}, bf16[2,256,512]{2,1,0:T(8,128)(2,1)}, u32[]{:S(2)}, u32[]{:S(2)}) collective-permute-start(bf16[2,256,512]{2,1,0:T(8,128)(2,1)} %get-tuple-element.60), channel_id=1, source_target_pairs={{0,0},{1,4},{2,2},{3,6},{4,5},{5,1},{6,7},{7,3},{8,8},{9,12},{10,1... | collective-permute-start | bytes 1572872 | tf_op jit(solution)/shard_map/ppermute | solution.py:331
  172.2 45.0 %collective-permute-start.18 = (bf16[2,256,512]{2,1,0:T(8,128)(2,1)}, bf16[2,256,512]{2,1,0:T(8,128)(2,1)}, u32[]{:S(2)}, u32[]{:S(2)}) collective-permute-start(bf16[2,256,512]{2,1,0:T(8,128)(2,1)} %get-tuple-element.59), channel_id=1, source_target_pairs={{0,2},{1,6},{2,4},{3,0},{4,7},{5,3},{6,1},{7,5},{8,10},{9,14},{10,... | collective-permute-start | bytes 1572872 | tf_op jit(solution)/shard_map/ppermute | solution.py:331
  172.3 57.9 %collective-permute-start.17 = (bf16[2,256,512]{2,1,0:T(8,128)(2,1)}, bf16[2,256,512]{2,1,0:T(8,128)(2,1)}, u32[]{:S(2)}, u32[]{:S(2)}) collective-permute-start(bf16[2,256,512]{2,1,0:T(8,128)(2,1)} %get-tuple-element.58), channel_id=1, source_target_pairs={{0,4},{1,0},{2,6},{3,2},{4,1},{5,5},{6,3},{7,7},{8,12},{9,8},{10,1... | collective-permute-start | bytes 1572872 | tf_op jit(solution)/shard_map/ppermute | solution.py:331
  188.1 101.8 %collective-permute-start.16 = (bf16[2,256,512]{2,1,0:T(8,128)(2,1)}, bf16[2,256,512]{2,1,0:T(8,128)(2,1)}, u32[]{:S(2)}, u32[]{:S(2)}) collective-permute-start(bf16[2,256,512]{2,1,0:T(8,128)(2,1)} %get-tuple-element.57), channel_id=1, source_target_pairs={{0,6},{1,2},{2,0},{3,4},{4,3},{5,7},{6,5},{7,1},{8,14},{9,10},{10,... | collective-permute-start | bytes 1572872 | tf_op jit(solution)/shard_map/ppermute | solution.py:331
  211.9 80.6 %collective-permute-start.15 = (bf16[2,256,512]{2,1,0:T(8,128)(2,1)}, bf16[2,256,512]{2,1,0:T(8,128)(2,1)}, u32[]{:S(2)}, u32[]{:S(2)}) collective-permute-start(bf16[2,256,512]{2,1,0:T(8,128)(2,1)} %get-tuple-element.56), channel_id=1, source_target_pairs={{0,0},{1,4},{2,2},{3,6},{4,5},{5,1},{6,7},{7,3},{8,8},{9,12},{10,1... | collective-permute-start | bytes 1572872 | tf_op jit(solution)/shard_map/ppermute | solution.py:331
  217.3 77.9 %collective-permute-start.14 = (bf16[2,256,512]{2,1,0:T(8,128)(2,1)}, bf16[2,256,512]{2,1,0:T(8,128)(2,1)}, u32[]{:S(2)}, u32[]{:S(2)}) collective-permute-start(bf16[2,256,512]{2,1,0:T(8,128)(2,1)} %get-tuple-element.55), channel_id=1, source_target_pairs={{0,2},{1,6},{2,4},{3,0},{4,7},{5,3},{6,1},{7,5},{8,10},{9,14},{10,... | collective-permute-start | bytes 1572872 | tf_op jit(solution)/shard_map/ppermute | solution.py:331
  217.3 80.5 %collective-permute-start.11 = (bf16[2,256,512]{2,1,0:T(8,128)(2,1)}, bf16[2,256,512]{2,1,0:T(8,128)(2,1)}, u32[]{:S(2)}, u32[]{:S(2)}) collective-permute-start(bf16[2,256,512]{2,1,0:T(8,128)(2,1)} %get-tuple-element.54), channel_id=1, source_target_pairs={{0,4},{1,0},{2,6},{3,2},{4,1},{5,5},{6,3},{7,7},{8,12},{9,8},{10,1... | collective-permute-start | bytes 1572872 | tf_op jit(solution)/shard_map/ppermute | solution.py:331
  230.2 70.2 %collective-permute-start.2 = (bf16[2,256,512]{2,1,0:T(8,128)(2,1)}, bf16[2,256,512]{2,1,0:T(8,128)(2,1)}, u32[]{:S(2)}, u32[]{:S(2)}) collective-permute-start(bf16[2,256,512]{2,1,0:T(8,128)(2,1)} %get-tuple-element.43), channel_id=1, source_target_pairs={{0,6},{1,2},{2,0},{3,4},{4,3},{5,7},{6,5},{7,1},{8,14},{9,10},{10,... | collective-permute-start | bytes 1572872 | tf_op jit(solution)/shard_map/ppermute | solution.py:331
  (24 other events, 858.0 us)

commit v2 on v1

--- a/solution.py
+++ b/solution.py
@@ -26,11 +26,53 @@
     return -(-count // 8) * 8
 
 
-def gates_kernel(base_ref, len_ref, decay_ref, rows_ref, cols_ref, docs_ref, total_ref, scr):
+class Table:
+    def __init__(self, n, t, chunks):
+        self.n, self.t, self.chunks = n, t, chunks
+        self.stride, self.per = n // t, chunks // n
+        self.half = 0
+        self.which = 1
+        self.slot = self.which + chunks
+        self.place = self.slot + chunks
+        self.row = self.place + n * chunks
+        self.side = self.row + n
+        self.source = self.side + n
+        self.square = self.source + n
+        self.size = self.square + n * t
+
+
+def fill_table(tab, shard_ref, table_ref):
+    n, t, per, chunks = tab.n, tab.t, tab.per, tab.chunks
+    ctx, tp = lax.axis_index("ctx"), lax.axis_index("tp")
+    table_ref[tab.half] = tp
+    seen = [jnp.int32(0)] * n
+    for c in range(chunks):
+        shard = shard_ref[ctx * chunks + c]
+        op = lax.rem(shard - ctx - tp * tab.stride + 2 * n, n)
+        table_ref[tab.which + c] = op
+        rank = jnp.int32(0)
+        for k in range(n):
+            table_ref[tab.place + k * chunks + c] = jnp.minimum(seen[k], per - 1)
+            here = (op == k).astype(jnp.int32)
+            rank = rank + here * seen[k]
+            seen[k] = seen[k] + here
+        table_ref[tab.slot + c] = op * per + jnp.minimum(rank, per - 1)
+    for op in range(n):
+        lane = lax.rem(ctx - op + n, tab.stride)
+        source = tp * tab.stride + lane
+        table_ref[tab.row + op] = lane * per
+        table_ref[tab.side + op] = lax.rem(ctx - op - source + 2 * n, n) // tab.stride
+        table_ref[tab.source + op] = source
+        for k in range(t):
+            table_ref[tab.square + op * t + k] = lax.rem(ctx - source - k * tab.stride + 2 * n, n) * per
+
+
+def gates_kernel(tab, len_ref, shard_ref, decay_ref, rows_ref, cols_ref, docs_ref, total_ref, table_ref, scr):
+    fill_table(tab, shard_ref, table_ref)
     heads, tokens = decay_ref.shape
     hp = pad8(heads)
     chunks = tokens // BLK
-    base = base_ref[0]
+    base = lax.axis_index("ctx") * tokens
     starts, run = [], jnp.int32(0)
     for i in range(len_ref.shape[0]):
         starts.append(run)
@@ -83,25 +125,26 @@
     total_ref[...] = jnp.where(edges[-1] == edges[0], jnp.exp(run[:, :128]), 0.0)
 
 
-def gates(base, doc_lengths, decay):
+def gates(tab, doc_lengths, block_shard, decay):
     heads, tokens = decay.shape
     hp = pad8(heads)
     smem = pl.BlockSpec(memory_space=pltpu.SMEM)
     vmem = pl.BlockSpec(memory_space=pltpu.VMEM)
     return pl.pallas_call(
-        gates_kernel,
+        functools.partial(gates_kernel, tab),
         in_specs=[smem, smem, vmem],
-        out_specs=[vmem] * 4,
+        out_specs=[vmem] * 4 + [smem],
         out_shape=[
             jax.ShapeDtypeStruct((4 * hp, tokens), F32),
             jax.ShapeDtypeStruct((tokens, 128), F32),
             jax.ShapeDtypeStruct((8, tokens), F32),
             jax.ShapeDtypeStruct((heads, 128), F32),
+            jax.ShapeDtypeStruct((tab.size,), jnp.int32),
         ],
         scratch_shapes=[pltpu.VMEM((128, tokens), F32)],
         compiler_params=params(),
         name="gates",
-    )(base, doc_lengths, decay)
+    )(doc_lengths, block_shard, decay)
 
 
 def totals_kernel(lo, hp, count, key_ref, value_ref, rows_ref, low_ref, full_ref, acc):
@@ -151,10 +194,11 @@
     )(key_rows, value_rows, rows)
 
 
-def attend_kernel(lo, hp, count, ops, *refs):
-    (which_ref, _, _, query_ref, key_ref, value_ref, gate_ref, gain_ref, rows_ref, cols_ref, docs_ref, state_ref) = refs[:12]
-    outs = refs[12 : 12 + ops]
-    square_ref, state, gated, squares = refs[12 + ops :]
+def attend_kernel(tab, lo, hp, count, chain, *refs):
+    ops = tab.n
+    (table_ref, query_ref, key_ref, value_ref, gate_ref, gain_ref, rows_ref, cols_ref, docs_ref, state_ref) = refs[:10]
+    outs = refs[10 + chain : 10 + chain + ops]
+    square_ref, state, gated = refs[10 + chain + ops :]
     step = pl.program_id(0)
 
     @pl.when(step == 0)
@@ -184,52 +228,53 @@
         gated[:, cols] = (
             attended * gain_ref[0:1, cols] * jax.nn.sigmoid(gate_ref[:, cols].astype(F32))
         ).astype(BF16)
-    square_ref[0] = jnp.sum(square.T, axis=0, keepdims=True)
+    total = jnp.sum(square.T, axis=0, keepdims=True)
+    square_ref[0] = total + refs[10][0] if chain else total
+    which = table_ref[tab.which + step]
     for op in range(ops):
 
-        @pl.when(which_ref[step] == op)
+        @pl.when(which == op)
         def _():
             outs[op][0] = gated[...]
 
 
-def attend(tables, query, key, value, gate, gain, rows, cols, docs, entering, lo, count):
-    tokens = query.shape[0]
-    chunks = tokens // BLK
+def attend(tab, table, query, key, value, gate, gain, rows, cols, docs, entering, base, lo, count, squares):
+    tokens, local_width = query.shape
+    chunks, ops, per = tab.chunks, tab.n, tab.per
     hp = rows.shape[0] // 4
     width = count * 128
     at = lo * 128 // width
-    which, place, slot = tables
-    ops = place.shape[0] // chunks
-    per = chunks // ops
-    wide = pl.BlockSpec((BLK, width), lambda c, *_: (c, at))
-
-    def out_map(op, c, which_ref, place_ref, slot_ref):
-        return (place_ref[op * chunks + c], 0, 0)
+    chain = squares is not None
+    wide = pl.BlockSpec((BLK, width), lambda c, tbl: (c, at))
+    square_spec = pl.BlockSpec((1, 1, BLK), lambda c, tbl: (tbl[tab.slot + c], 0, 0))
+
+    def out_map(op, c, tbl):
+        return (tbl[tab.place + op * chunks + c], 0, 0)
 
     out = pl.pallas_call(
-        functools.partial(attend_kernel, lo, hp, count, ops),
+        functools.partial(attend_kernel, tab, lo, hp, count, int(chain)),
         grid_spec=pltpu.PrefetchScalarGridSpec(
-            num_scalar_prefetch=3,
+            num_scalar_prefetch=1,
             grid=(chunks,),
             in_specs=[
                 wide,
                 wide,
                 wide,
                 wide,
-                pl.BlockSpec((1, width), lambda c, *_: (0, at)),
-                pl.BlockSpec((rows.shape[0], BLK), lambda c, *_: (0, c)),
-                pl.BlockSpec((BLK, 128), lambda c, *_: (c, 0)),
-                pl.BlockSpec((8, BLK), lambda c, *_: (0, c)),
-                whole((count, 128, 128)),
-            ],
+                pl.BlockSpec((1, width), lambda c, tbl: (0, tbl[tab.half] * (local_width // width) + at)),
+                pl.BlockSpec((rows.shape[0], BLK), lambda c, tbl: (0, c)),
+                pl.BlockSpec((BLK, 128), lambda c, tbl: (c, 0)),
+                pl.BlockSpec((8, BLK), lambda c, tbl: (0, c)),
+                pl.BlockSpec((count, 128, 128), lambda c, tbl: ((lo - base) // count, 0, 0)),
+            ]
+            + [square_spec] * chain,
             out_specs=[
                 pl.BlockSpec((1, BLK, width), functools.partial(out_map, op)) for op in range(ops)
             ]
-            + [pl.BlockSpec((1, 1, BLK), lambda c, which_ref, place_ref, slot_ref: (slot_ref[c], 0, 0))],
+            + [square_spec],
             scratch_shapes=[
                 pltpu.VMEM((count, 128, 128), F32),
                 pltpu.VMEM((BLK, width), BF16),
-                pltpu.VMEM((8, 128), F32),
             ],
         ),
         out_shape=[jax.ShapeDtypeStruct((per, BLK, width), BF16)] * ops
@@ -241,38 +286,47 @@
             transcendentals=tokens * count * (BLK + 128),
         ),
         name="attend",
-    )(which, place, slot, query, key, value, gate, gain, rows, cols, docs, entering)
+    )(table, query, key, value, gate, gain, rows, cols, docs, entering, *([squares] if chain else []))
     return out[:ops], out[ops]
 
 
-def place_kernel(features, pos_ref, piece_ref, square_ref, *refs):
+def place_kernel(features, t, table_ref, piece_ref, *refs):
     out_ref = refs[-1]
-    scale = lax.rsqrt(square_ref[0] / features + norm_eps)
+    square = refs[0][0, 0]
+    for k in range(1, t):
+        square = square + refs[k][0, 0]
+    scale = lax.rsqrt(square / features + norm_eps)
     scale = jnp.broadcast_to(scale, (128, BLK)).T
     for c in range(out_ref.shape[1] // 128):
         cols = slice(c * 128, (c + 1) * 128)
         out_ref[:, cols] = (piece_ref[0, :, cols].astype(F32) * scale).astype(BF16)
 
 
-def place(position, piece, square, out, shape, features, unit):
+def place(tab, table, op, lo, piece, squares, out, shape, local_width, features, unit):
     per, _, width = piece.shape
-    in_specs = [
-        pl.BlockSpec((1, BLK, unit), lambda k, j, pos: (k, 0, j)),
-        pl.BlockSpec((1, 1, BLK), lambda k, j, pos: (k, 0, 0)),
-    ]
-    operands = [position, piece, square]
+    t = tab.t
+
+    def square_map(k, c, j, tbl):
+        return (tbl[tab.source + op] * t + k, tbl[tab.square + op * t + k] + c, 0, 0)
+
+    def out_map(c, j, tbl):
+        return (tbl[tab.row + op] + c, (tbl[tab.side + op] * local_width + lo * 128) // unit + j)
+
+    in_specs = [pl.BlockSpec((1, BLK, unit), lambda c, j, tbl: (c, 0, j))]
+    in_specs += [pl.BlockSpec((1, 1, 1, BLK), functools.partial(square_map, k)) for k in range(t)]
+    operands = [table, piece] + [squares] * t
     aliases = {}
     if out is not None:
         in_specs.append(pl.BlockSpec(memory_space=pl.ANY))
         operands.append(out)
-        aliases = {3: 0}
+        aliases = {len(operands) - 1: 0}
     return pl.pallas_call(
-        functools.partial(place_kernel, features),
+        functools.partial(place_kernel, features, t),
         grid_spec=pltpu.PrefetchScalarGridSpec(
             num_scalar_prefetch=1,
             grid=(per, width // unit),
             in_specs=in_specs,
-            out_specs=pl.BlockSpec((BLK, unit), lambda k, j, pos: (pos[0] + k, pos[1] + j)),
+            out_specs=pl.BlockSpec((BLK, unit), out_map),
         ),
         out_shape=jax.ShapeDtypeStruct(shape, BF16),
         input_output_aliases=aliases,
@@ -287,64 +341,55 @@
 def local(query_rows, key_rows, value_rows, gate_rows, decay_log, norm_gain, doc_lengths, block_shard):
     tokens, width = query_rows.shape
     heads = decay_log.shape[0]
-    chunks = tokens // BLK
     features = norm_gain.shape[0]
     n, t = lax.axis_size("ctx"), lax.axis_size("tp")
-    stride = n // t
-    per = chunks // n
-    ctx, tp = lax.axis_index("ctx"), lax.axis_index("tp")
+    tab = Table(n, t, tokens // BLK)
     quarter = max(1, heads // 4)
-    groups = [(lo, quarter) for lo in range(0, heads, quarter)]
-
-    base = (ctx * tokens).astype(jnp.int32).reshape(1)
-    rows, cols, docs, total_gate = gates(base, doc_lengths, decay_log)
-
-    shards = lax.dynamic_slice_in_dim(block_shard, ctx * chunks, chunks)
-    which = jnp.mod(shards - ctx - tp * stride, n).astype(jnp.int32)
-    index = jnp.arange(chunks)
-    earlier = index[None, :] < index[:, None]
-    ranks = jnp.sum((earlier & (which[None, :] == which[:, None])).astype(jnp.int32), axis=1)
-    seen = jnp.sum(
-        (earlier[None] & (which[None, None, :] == jnp.arange(n)[:, None, None])).astype(jnp.int32), axis=2
-    )
-    tables = (which, jnp.minimum(seen, per - 1).reshape(-1), which * per + jnp.minimum(ranks, per - 1))
-    gain = lax.dynamic_slice_in_dim(norm_gain, tp * width, width).reshape(1, width)
-
+
+    rows, cols, docs, total_gate, table = gates(tab, doc_lengths, block_shard, decay_log)
+    gain = norm_gain.reshape(1, features)
     hop = [(i, i + 1) for i in range(n - 1)]
 
     def route(op):
         return [
-            (d * t + k, (d + op + k * stride) % n * t + d // stride) for d in range(n) for k in range(t)
+            (d * t + k, (d + op + k * tab.stride) % n * t + d // tab.stride)
+            for d in range(n)
+            for k in range(t)
         ]
 
-    pieces, squares = [], None
-    for lo, count in groups:
+    def enter(lo, count):
         low, full = totals(key_rows, value_rows, rows, lo, count)
         carry = total_gate[lo : lo + count, :1, None]
         entering = lax.ppermute(low, "ctx", hop)
         for _ in range(max(1, n // 2) - 1):
             entering = lax.ppermute((carry * entering.astype(F32) + full).astype(BF16), "ctx", hop)
-        outs, square = attend(
-            tables, query_rows, key_rows, value_rows, gate_rows, gain, rows, cols, docs, entering, lo, count
+        return entering
+
+    rest = heads - quarter
+    entering = {rest: enter(rest, quarter), 0: enter(0, rest)}
+    groups = [(rest, quarter, rest), (0, 2 * quarter, 0), (2 * quarter, quarter, 0)]
+    gated, squares = [], None
+    for lo, count, base in groups:
+        outs, squares = attend(
+            tab, table, query_rows, key_rows, value_rows, gate_rows, gain, rows, cols, docs,
+            entering[base], base, lo, count, squares,
         )
-        squares = square if squares is None else squares + square
-        pieces.append([lax.ppermute(outs[op], ("ctx", "tp"), route(op)) for op in range(n)])
-
-    halves = [
-        lax.ppermute(squares[op * per : (op + 1) * per], ("ctx", "tp"), route(op)) for op in range(n)
-    ]
-    joined = [sum(halves[op + k * stride] for k in range(t)) for op in range(stride)]
+        gated.append(outs)
+    squares = lax.all_gather(squares, ("ctx", "tp"))
 
     unit = quarter * 128
     shape = (tokens // t, features)
     out = None
-    for (lo, count), received in zip(groups, pieces):
+    pieces = [[lax.ppermute(gated[g][op], ("ctx", "tp"), route(op)) for op in range(n)] for g in range(2)]
+    for g in range(3):
+        if g == 1:
+            sent = []
+            for op in range(n):
+                ready, out = lax.optimization_barrier((gated[2][op], out))
+                sent.append(lax.ppermute(ready, ("ctx", "tp"), route(op)))
+            pieces.append(sent)
         for op in range(n):
-            lane = jnp.mod(ctx - op, stride)
-            source = tp * stride + lane
-            half = jnp.mod(ctx - op - source, n) // stride
-            position = jnp.stack([lane * per, (half * width + lo * 128) // unit]).astype(jnp.int32)
-            out = place(position, received[op], joined[op % stride], out, shape, features, unit)
+            out = place(tab, table, op, groups[g][0], pieces[g][op], squares, out, shape, width, features, unit)
     return out
 
 

time: 306 us -> 267 us (0.87)
  the two profiles are of different devices: /device:TPU:0 before, /device:TPU:1 now
where the time goes in v2:
time: 267 us; the launch traced here: 265 us
  Pallas kernels  94.9 us (36%)
  starting transfers between devices  78.2 us (29%)
  blocking collectives  51.2 us (19%)
  waiting for transfers between devices  32.4 us (12%)
  local copies, waits for them, and re-layouts  6.63 us (2%)
    ppermute x8, starting transfers between devices, local(): lax.ppermute(gated[g][op], ('ctx', 'tp'), route(op))  55.6 us
    all_gather x1, blocking collectives, local(): squares = lax.all_gather(squares, ('ctx', 'tp'))  51.2 us
    pallas_call x3, Pallas kernels, attend(): pl.pallas_call(functools.partial(attend_kernel, tab, lo, hp, count, int(c...  41.1 us
    pallas_call x12, Pallas kernels, place(): pl.pallas_call(functools.partial(place_kernel, features, t), grid_spec=pl...  38.4 us
    ppermute x4, waiting for transfers between devices, local(): sent.append(lax.ppermute(ready, ('ctx', 'tp'), route(op)))  15.5 us
    ppermute x8, waiting for transfers between devices, local(): lax.ppermute(gated[g][op], ('ctx', 'tp'), route(op))  12.7 us
    pallas_call x2, Pallas kernels, totals(): pl.pallas_call(functools.partial(totals_kernel, lo, hp, count), grid=(tok...  11.9 us
    ppermute x4, starting transfers between devices, local(): sent.append(lax.ppermute(ready, ('ctx', 'tp'), route(op)))  7.98 us
  transfers between devices with their start and end apart: 16, of which 4 were waited for; matrix products, arithmetic and copies ran while one was open for 1% of the time, Pallas kernels for 32%

profile of v2, /device:TPU:1, one launch (start us, length us, event | category | flops | bytes accessed | tf_op | source)
XLA Modules:
  0.0 265.0 jit_solution(2997209041016081012)
XLA Ops:
  0.0 3.6 %gates.1 = (f32[64,2048]{1,0:T(8,128)}, f32[2048,128]{1,0:T(8,128)}, f32[8,2048]{1,0:T(8,128)}, f32[16,128]{1,0:T(8,128)}, s32[69]{0:T(128)}) custom-call(s32[16]{0:T(128)} %len_ref.1, s32[32]{0:T(128)} %shard_ref.1, f32[16,2048]{1,0:T(8,128)} %decay_ref.1), custom_call_target="tpu_custom_call" | custom-call | tf_op jit(solution)/shard_map/gates/pallas_call | solution.py:133
  3.6 4.4 %totals.3 = (bf16[4,128,128]{2,1,0:T(8,128)(2,1)}, f32[4,128,128]{2,1,0:T(8,128)}) custom-call(bf16[2048,2048]{1,0:T(8,128)(2,1)} %refs_2_.5, bf16[2048,2048]{1,0:T(8,128)(2,1)} %refs_3_.5, f32[64,2048]{1,0:T(8,128)} %get-tuple-element.38.rows_ref.refs_6_), custom_call_target="tpu_custom_call" | custom-call | flops 268435456 | bytes 4194304 | tf_op jit(solution)/shard_map/totals/pallas_call | solution.py:175
  8.0 4.2 %collective-permute-start.2 = (bf16[4,128,128]{2,1,0:T(8,128)(2,1)}, bf16[4,128,128]{2,1,0:T(8,128)(2,1)S(1)}, u32[]{:S(2)}, u32[]{:S(2)}) collective-permute-start(bf16[4,128,128]{2,1,0:T(8,128)(2,1)} %get-tuple-element.44), channel_id=1, source_target_pairs={{0,2},{2,4},{4,6},{1,3},{3,5},{5,7},{8,10},{10,12},{12,14},{9,11},... | collective-permute-start | bytes 393224 | tf_op jit(solution)/shard_map/ppermute | solution.py:363
  12.2 7.4 %totals.2 = (bf16[12,128,128]{2,1,0:T(8,128)(2,1)}, f32[12,128,128]{2,1,0:T(8,128)}) custom-call(bf16[2048,2048]{1,0:T(8,128)(2,1)} %refs_2_.5, bf16[2048,2048]{1,0:T(8,128)(2,1)} %refs_3_.5, f32[64,2048]{1,0:T(8,128)} %get-tuple-element.38.rows_ref.refs_6_), custom_call_target="tpu_custom_call" | custom-call | flops 805306368 | bytes 12582912 | tf_op jit(solution)/shard_map/totals/pallas_call | solution.py:175
  19.6 3.2 %collective-permute-start = (bf16[12,128,128]{2,1,0:T(8,128)(2,1)}, bf16[12,128,128]{2,1,0:T(8,128)(2,1)S(1)}, u32[]{:S(2)}, u32[]{:S(2)}) collective-permute-start(bf16[12,128,128]{2,1,0:T(8,128)(2,1)} %get-tuple-element.42), channel_id=1, source_target_pairs={{0,2},{2,4},{4,6},{1,3},{3,5},{5,7},{8,10},{10,12},{12,14},{9,11},... | collective-permute-start | bytes 1179656 | tf_op jit(solution)/shard_map/ppermute | solution.py:363
  23.2 3.2 %collective-permute-start.3 = (bf16[4,128,128]{2,1,0:T(8,128)(2,1)S(1)}, bf16[4,128,128]{2,1,0:T(8,128)(2,1)S(1)}, u32[]{:S(2)}, u32[]{:S(2)}) collective-permute-start(bf16[4,128,128]{2,1,0:T(8,128)(2,1)S(1)} %add_convert_fusion.1), channel_id=1, source_target_pairs={{0,2},{2,4},{4,6},{1,3},{3,5},{5,7},{8,10},{10,12},{12,14},{9,11},... | collective-permute-start | bytes 393224 | tf_op jit(solution)/shard_map/ppermute | solution.py:365
  26.4 4.2 %collective-permute-done = bf16[12,128,128]{2,1,0:T(8,128)(2,1)S(1)} collective-permute-done((bf16[12,128,128]{2,1,0:T(8,128)(2,1)}, bf16[12,128,128]{2,1,0:T(8,128)(2,1)S(1)}, u32[]{:S(2)}, u32[]{:S(2)}) %collective-permute-start) | collective-permute-done | bytes 393248 | tf_op jit(solution)/shard_map/ppermute | solution.py:363
  31.9 4.0 %collective-permute-start.1 = (bf16[12,128,128]{2,1,0:T(8,128)(2,1)S(1)}, bf16[12,128,128]{2,1,0:T(8,128)(2,1)S(1)}, u32[]{:S(2)}, u32[]{:S(2)}) collective-permute-start(bf16[12,128,128]{2,1,0:T(8,128)(2,1)S(1)} %add_convert_fusion), channel_id=1, source_target_pairs={{0,2},{2,4},{4,6},{1,3},{3,5},{5,7},{8,10},{10,12},{12,14},{9,11},... | collective-permute-start | bytes 1179656 | tf_op jit(solution)/shard_map/ppermute | solution.py:365
  36.6 11.8 %attend.3 = (bf16[2,256,512]{2,1,0:T(8,128)(2,1)}, bf16[2,256,512]{2,1,0:T(8,128)(2,1)}, bf16[2,256,512]{2,1,0:T(8,128)(2,1)}, bf16[2,256,512]{2,1,0:T(8,128)(2,1)}, f32[8,1,256]{2,1,0:T(1,128)}) custom-call(s32[69]{0:T(128)} %get-tuple-element.37.refs_0_.table_ref, bf16[2048,2048]{1,0:T(8,128)(2,1)} %refs_1_.5, bf16[2048,2048]{1,0:T(8,128)(2,1)} %refs_2_.5, ...), custom_call_target="tpu_custom_call" | custom-call | flops 1610612736 | bytes 10485760 | tf_op jit(solution)/shard_map/attend/pallas_call | solution.py:254
  48.4 5.5 %collective-permute-start.5 = (bf16[2,256,512]{2,1,0:T(8,128)(2,1)}, bf16[2,256,512]{2,1,0:T(8,128)(2,1)S(1)}, u32[]{:S(2)}, u32[]{:S(2)}) collective-permute-start(bf16[2,256,512]{2,1,0:T(8,128)(2,1)} %get-tuple-element.54), channel_id=1, source_target_pairs={{0,4},{1,0},{2,6},{3,2},{4,1},{5,5},{6,3},{7,7},{8,12},{9,8},{10,1... | collective-permute-start | bytes 1572872 | tf_op jit(solution)/shard_map/ppermute | solution.py:383
  57.4 17.3 %attend.4 = (bf16[2,256,1024]{2,1,0:T(8,128)(2,1)}, bf16[2,256,1024]{2,1,0:T(8,128)(2,1)}, bf16[2,256,1024]{2,1,0:T(8,128)(2,1)}, bf16[2,256,1024]{2,1,0:T(8,128)(2,1)}, f32[8,1,256]{2,1,0:T(1,128)}) custom-call(s32[69]{0:T(128)} %get-tuple-element.37.refs_0_.table_ref, bf16[2048,2048]{1,0:T(8,128)(2,1)} %refs_1_.5, bf16[2048,2048]{1,0:T(8,128)(2,1)} %refs_2_.5, ...), custom_call_target="tpu_custom_call" | custom-call | flops 3221225472 | bytes 20971520 | tf_op jit(solution)/shard_map/attend/pallas_call | solution.py:254
  77.3 4.8 %collective-permute-start.14 = (bf16[2,256,1024]{2,1,0:T(8,128)(2,1)}, bf16[2,256,1024]{2,1,0:T(8,128)(2,1)S(1)}, u32[]{:S(2)}, u32[]{:S(2)}) collective-permute-start(bf16[2,256,1024]{2,1,0:T(8,128)(2,1)} %get-tuple-element.66), channel_id=1, source_target_pairs={{0,2},{1,6},{2,4},{3,0},{4,7},{5,3},{6,1},{7,5},{8,10},{9,14},{10,... | collective-permute-start | bytes 3145736 | tf_op jit(solution)/shard_map/ppermute | solution.py:383
  84.9 38.1 %collective-permute-start.4 = (bf16[2,256,512]{2,1,0:T(8,128)(2,1)S(1)}, bf16[2,256,512]{2,1,0:T(8,128)(2,1)S(1)}, u32[]{:S(2)}, u32[]{:S(2)}) collective-permute-start(bf16[2,256,512]{2,1,0:T(8,128)(2,1)S(1)} %copy-done.18), channel_id=1, source_target_pairs={{0,6},{1,2},{2,0},{3,4},{4,3},{5,7},{6,5},{7,1},{8,14},{9,10},{10,... | collective-permute-start | bytes 1572872 | tf_op jit(solution)/shard_map/ppermute | solution.py:383
  123.1 11.8 %collective-permute-done.7.piece_ref = bf16[2,256,512]{2,1,0:T(8,128)(2,1)S(1)} collective-permute-done((bf16[2,256,512]{2,1,0:T(8,128)(2,1)}, bf16[2,256,512]{2,1,0:T(8,128)(2,1)S(1)}, u32[]{:S(2)}, u32[]{:S(2)}) %collective-permute-start.7) | collective-permute-done | bytes 524320 | tf_op jit(solution)/shard_map/ppermute | solution.py:383
  134.9 11.9 %attend.5 = (bf16[2,256,512]{2,1,0:T(8,128)(2,1)}, bf16[2,256,512]{2,1,0:T(8,128)(2,1)}, bf16[2,256,512]{2,1,0:T(8,128)(2,1)}, bf16[2,256,512]{2,1,0:T(8,128)(2,1)}, f32[8,1,256]{2,1,0:T(1,128)}) custom-call(s32[69]{0:T(128)} %get-tuple-element.37.refs_0_.table_ref, bf16[2048,2048]{1,0:T(8,128)(2,1)} %refs_1_.5, bf16[2048,2048]{1,0:T(8,128)(2,1)} %refs_2_.5, ...), custom_call_target="tpu_custom_call" | custom-call | flops 1610612736 | bytes 10485760 | tf_op jit(solution)/shard_map/attend/pallas_call | solution.py:254
  146.9 51.2 %all-gather = f32[64,1,256]{2,1,0:T(1,128)} all-gather(f32[8,1,256]{2,1,0:T(1,128)} %get-tuple-element.53), channel_id=2, replica_groups=mesh['dp'=4,'ctx'=4,'tp'=2] {'ctx','tp'}, dimensions={0}, use_global_device_ids=true | all-gather | bytes 73728 | tf_op jit(solution)/shard_map/all_gather | solution.py:378
  198.1 2.7 %place.12.refs_2_ = bf16[1024,4096]{1,0:T(8,128)(2,1)} custom-call(s32[69]{0:T(128)} %get-tuple-element.37.refs_0_.table_ref, bf16[2,256,512]{2,1,0:T(8,128)(2,1)} %copy-done.7, f32[8,8,1,256]{3,2,1,0:T(1,128)} %bitcast.2, f32[8,8,1,256]{3,2,1,0:T(1,128)} %bitcast.3), custom_call_target="tpu_custom_call" | custom-call | flops 262144 | bytes 1048576 | tf_op jit(solution)/shard_map/place/pallas_call | solution.py:323
  200.7 2.7 %place.13.refs_2_ = bf16[1024,4096]{1,0:T(8,128)(2,1)} custom-call(s32[69]{0:T(128)} %get-tuple-element.37.refs_0_.table_ref, bf16[2,256,512]{2,1,0:T(8,128)(2,1)} %copy-done.6, f32[8,8,1,256]{3,2,1,0:T(1,128)} %bitcast.4, f32[8,8,1,256]{3,2,1,0:T(1,128)} %bitcast.5, bf16[1024,4096]{1,0:T(8,128)(2,1)} %place.12.refs_2_), custom_call_target="tpu_custom_call", output_to_operand_aliasing={{}: (4, {})} | custom-call | flops 262144 | bytes 1048576 | tf_op jit(solution)/shard_map/place/pallas_call | solution.py:323
  206.9 2.7 %place.15.refs_2_ = bf16[1024,4096]{1,0:T(8,128)(2,1)} custom-call(s32[69]{0:T(128)} %get-tuple-element.37.refs_0_.table_ref, bf16[2,256,512]{2,1,0:T(8,128)(2,1)} %copy-done.12, f32[8,8,1,256]{3,2,1,0:T(1,128)} %bitcast.8, f32[8,8,1,256]{3,2,1,0:T(1,128)} %bitcast.9, bf16[1024,4096]{1,0:T(8,128)(2,1)} %place.14.refs_2_), custom_call_target="tpu_custom_call", output_to_operand_aliasing={{}: (4, {})} | custom-call | flops 262144 | bytes 1048576 | tf_op jit(solution)/shard_map/place/pallas_call | solution.py:323
  217.6 4.3 %place.16.refs_2_ = bf16[1024,4096]{1,0:T(8,128)(2,1)} custom-call(s32[69]{0:T(128)} %get-tuple-element.37.refs_0_.table_ref, bf16[2,256,1024]{2,1,0:T(8,128)(2,1)} %copy-done.3, f32[8,8,1,256]{3,2,1,0:T(1,128)} %bitcast.10, f32[8,8,1,256]{3,2,1,0:T(1,128)} %bitcast.11, bf16[1024,4096]{1,0:T(8,128)(2,1)} %place.15.refs_2_), custom_call_target="tpu_custom_call", output_to_operand_aliasing={{}: (4, {})} | custom-call | flops 524288 | bytes 2097152 | tf_op jit(solution)/shard_map/place/pallas_call | solution.py:323
  221.9 4.3 %place.17.refs_2_ = bf16[1024,4096]{1,0:T(8,128)(2,1)} custom-call(s32[69]{0:T(128)} %get-tuple-element.37.refs_0_.table_ref, bf16[2,256,1024]{2,1,0:T(8,128)(2,1)} %copy-done.2, f32[8,8,1,256]{3,2,1,0:T(1,128)} %bitcast.13, f32[8,8,1,256]{3,2,1,0:T(1,128)} %bitcast.12, bf16[1024,4096]{1,0:T(8,128)(2,1)} %place.16.refs_2_), custom_call_target="tpu_custom_call", output_to_operand_aliasing={{}: (4, {})} | custom-call | flops 524288 | bytes 2097152 | tf_op jit(solution)/shard_map/place/pallas_call | solution.py:323
  226.2 4.3 %place.18.refs_2_ = bf16[1024,4096]{1,0:T(8,128)(2,1)} custom-call(s32[69]{0:T(128)} %get-tuple-element.37.refs_0_.table_ref, bf16[2,256,1024]{2,1,0:T(8,128)(2,1)} %copy-done.1, f32[8,8,1,256]{3,2,1,0:T(1,128)} %bitcast.14, f32[8,8,1,256]{3,2,1,0:T(1,128)} %bitcast.15, bf16[1024,4096]{1,0:T(8,128)(2,1)} %place.17.refs_2_), custom_call_target="tpu_custom_call", output_to_operand_aliasing={{}: (4, {})} | custom-call | flops 524288 | bytes 2097152 | tf_op jit(solution)/shard_map/place/pallas_call | solution.py:323
  231.4 4.3 %place.19.refs_2_ = bf16[1024,4096]{1,0:T(8,128)(2,1)} custom-call(s32[69]{0:T(128)} %get-tuple-element.37.refs_0_.table_ref, bf16[2,256,1024]{2,1,0:T(8,128)(2,1)} %copy-done.4, f32[8,8,1,256]{3,2,1,0:T(1,128)} %bitcast.16, f32[8,8,1,256]{3,2,1,0:T(1,128)} %bitcast.17, bf16[1024,4096]{1,0:T(8,128)(2,1)} %place.18.refs_2_), custom_call_target="tpu_custom_call", output_to_operand_aliasing={{}: (4, {})} | custom-call | flops 524288 | bytes 2097152 | tf_op jit(solution)/shard_map/place/pallas_call | solution.py:323
  235.7 15.5 %collective-permute-done.11.piece_ref = bf16[2,256,512]{2,1,0:T(8,128)(2,1)S(1)} collective-permute-done((bf16[2,256,512]{2,1,0:T(8,128)(2,1)}, bf16[2,256,512]{2,1,0:T(8,128)(2,1)S(1)}, u32[]{:S(2)}, u32[]{:S(2)}) %collective-permute-start.11) | collective-permute-done | bytes 524320 | tf_op jit(solution)/shard_map/ppermute | solution.py:389
  (69 shorter events, 37.4 us)
Async XLA Ops:
  8.0 14.8 %copy-start.15 = (f32[16,128]{1,0:T(8,128)S(1)}, f32[16,128]{1,0:T(8,128)}, u32[]{:S(2)}) copy-start(f32[16,128]{1,0:T(8,128)} %get-tuple-element.41) | copy-start | bytes 24580
  8.0 15.1 %copy-start.13 = (f32[4,128,128]{2,1,0:T(8,128)S(1)}, f32[4,128,128]{2,1,0:T(8,128)}, u32[]{:S(2)}) copy-start(f32[4,128,128]{2,1,0:T(8,128)} %get-tuple-element.45) | copy-start | bytes 786436
  8.0 15.0 %collective-permute-start.2 = (bf16[4,128,128]{2,1,0:T(8,128)(2,1)}, bf16[4,128,128]{2,1,0:T(8,128)(2,1)S(1)}, u32[]{:S(2)}, u32[]{:S(2)}) collective-permute-start(bf16[4,128,128]{2,1,0:T(8,128)(2,1)} %get-tuple-element.44), channel_id=1, source_target_pairs={{0,2},{2,4},{4,6},{1,3},{3,5},{5,7},{8,10},{10,12},{12,14},{9,11},... | collective-permute-start | bytes 393224 | tf_op jit(solution)/shard_map/ppermute | solution.py:363
  19.6 11.0 %collective-permute-start = (bf16[12,128,128]{2,1,0:T(8,128)(2,1)}, bf16[12,128,128]{2,1,0:T(8,128)(2,1)S(1)}, u32[]{:S(2)}, u32[]{:S(2)}) collective-permute-start(bf16[12,128,128]{2,1,0:T(8,128)(2,1)} %get-tuple-element.42), channel_id=1, source_target_pairs={{0,2},{2,4},{4,6},{1,3},{3,5},{5,7},{8,10},{10,12},{12,14},{9,11},... | collective-permute-start | bytes 1179656 | tf_op jit(solution)/shard_map/ppermute | solution.py:363
  23.2 12.7 %collective-permute-start.3 = (bf16[4,128,128]{2,1,0:T(8,128)(2,1)S(1)}, bf16[4,128,128]{2,1,0:T(8,128)(2,1)S(1)}, u32[]{:S(2)}, u32[]{:S(2)}) collective-permute-start(bf16[4,128,128]{2,1,0:T(8,128)(2,1)S(1)} %add_convert_fusion.1), channel_id=1, source_target_pairs={{0,2},{2,4},{4,6},{1,3},{3,5},{5,7},{8,10},{10,12},{12,14},{9,11},... | collective-permute-start | bytes 393224 | tf_op jit(solution)/shard_map/ppermute | solution.py:365
  31.9 24.7 %collective-permute-start.1 = (bf16[12,128,128]{2,1,0:T(8,128)(2,1)S(1)}, bf16[12,128,128]{2,1,0:T(8,128)(2,1)S(1)}, u32[]{:S(2)}, u32[]{:S(2)}) collective-permute-start(bf16[12,128,128]{2,1,0:T(8,128)(2,1)S(1)} %add_convert_fusion), channel_id=1, source_target_pairs={{0,2},{2,4},{4,6},{1,3},{3,5},{5,7},{8,10},{10,12},{12,14},{9,11},... | collective-permute-start | bytes 1179656 | tf_op jit(solution)/shard_map/ppermute | solution.py:365
  48.4 34.6 %collective-permute-start.5 = (bf16[2,256,512]{2,1,0:T(8,128)(2,1)}, bf16[2,256,512]{2,1,0:T(8,128)(2,1)S(1)}, u32[]{:S(2)}, u32[]{:S(2)}) collective-permute-start(bf16[2,256,512]{2,1,0:T(8,128)(2,1)} %get-tuple-element.54), channel_id=1, source_target_pairs={{0,4},{1,0},{2,6},{3,2},{4,1},{5,5},{6,3},{7,7},{8,12},{9,8},{10,1... | collective-permute-start | bytes 1572872 | tf_op jit(solution)/shard_map/ppermute | solution.py:383
  53.9 31.1 %collective-permute-start.6 = (bf16[2,256,512]{2,1,0:T(8,128)(2,1)}, bf16[2,256,512]{2,1,0:T(8,128)(2,1)S(1)}, u32[]{:S(2)}, u32[]{:S(2)}) collective-permute-start(bf16[2,256,512]{2,1,0:T(8,128)(2,1)} %get-tuple-element.55), channel_id=1, source_target_pairs={{0,2},{1,6},{2,4},{3,0},{4,7},{5,3},{6,1},{7,5},{8,10},{9,14},{10,... | collective-permute-start | bytes 1572872 | tf_op jit(solution)/shard_map/ppermute | solution.py:383
  54.1 80.8 %collective-permute-start.7 = (bf16[2,256,512]{2,1,0:T(8,128)(2,1)}, bf16[2,256,512]{2,1,0:T(8,128)(2,1)S(1)}, u32[]{:S(2)}, u32[]{:S(2)}) collective-permute-start(bf16[2,256,512]{2,1,0:T(8,128)(2,1)} %get-tuple-element.56), channel_id=1, source_target_pairs={{0,0},{1,4},{2,2},{3,6},{4,5},{5,1},{6,7},{7,3},{8,8},{9,12},{10,1... | collective-permute-start | bytes 1572872 | tf_op jit(solution)/shard_map/ppermute | solution.py:383
  57.4 27.6 %copy-start.18 = (bf16[2,256,512]{2,1,0:T(8,128)(2,1)S(1)}, bf16[2,256,512]{2,1,0:T(8,128)(2,1)}, u32[]{:S(2)}) copy-start(bf16[2,256,512]{2,1,0:T(8,128)(2,1)} %get-tuple-element.52) | copy-start | bytes 1572868
  74.7 136.5 %collective-permute-start.13 = (bf16[2,256,1024]{2,1,0:T(8,128)(2,1)}, bf16[2,256,1024]{2,1,0:T(8,128)(2,1)S(1)}, u32[]{:S(2)}, u32[]{:S(2)}) collective-permute-start(bf16[2,256,1024]{2,1,0:T(8,128)(2,1)} %get-tuple-element.65), channel_id=1, source_target_pairs={{0,4},{1,0},{2,6},{3,2},{4,1},{5,5},{6,3},{7,7},{8,12},{9,8},{10,1... | collective-permute-start | bytes 3145736 | tf_op jit(solution)/shard_map/ppermute | solution.py:383
  77.3 136.4 %collective-permute-start.14 = (bf16[2,256,1024]{2,1,0:T(8,128)(2,1)}, bf16[2,256,1024]{2,1,0:T(8,128)(2,1)S(1)}, u32[]{:S(2)}, u32[]{:S(2)}) collective-permute-start(bf16[2,256,1024]{2,1,0:T(8,128)(2,1)} %get-tuple-element.66), channel_id=1, source_target_pairs={{0,2},{1,6},{2,4},{3,0},{4,7},{5,3},{6,1},{7,5},{8,10},{9,14},{10,... | collective-permute-start | bytes 3145736 | tf_op jit(solution)/shard_map/ppermute | solution.py:383
  83.0 63.8 %copy-start.5 = (bf16[2,256,512]{2,1,0:T(8,128)(2,1)}, bf16[2,256,512]{2,1,0:T(8,128)(2,1)S(1)}, u32[]{:S(2)}) copy-start(bf16[2,256,512]{2,1,0:T(8,128)(2,1)S(1)} %collective-permute-done.5.piece_ref) | copy-start | bytes 1572868
  83.0 132.6 %collective-permute-start.15 = (bf16[2,256,1024]{2,1,0:T(8,128)(2,1)}, bf16[2,256,1024]{2,1,0:T(8,128)(2,1)S(1)}, u32[]{:S(2)}, u32[]{:S(2)}) collective-permute-start(bf16[2,256,1024]{2,1,0:T(8,128)(2,1)} %get-tuple-element.67), channel_id=1, source_target_pairs={{0,0},{1,4},{2,2},{3,6},{4,5},{5,1},{6,7},{7,3},{8,8},{9,12},{10,1... | collective-permute-start | bytes 3145736 | tf_op jit(solution)/shard_map/ppermute | solution.py:383
  84.9 61.9 %copy-start.6 = (bf16[2,256,512]{2,1,0:T(8,128)(2,1)}, bf16[2,256,512]{2,1,0:T(8,128)(2,1)S(1)}, u32[]{:S(2)}) copy-start(bf16[2,256,512]{2,1,0:T(8,128)(2,1)S(1)} %collective-permute-done.6.piece_ref) | copy-start | bytes 1572868
  84.9 121.1 %collective-permute-start.4 = (bf16[2,256,512]{2,1,0:T(8,128)(2,1)S(1)}, bf16[2,256,512]{2,1,0:T(8,128)(2,1)S(1)}, u32[]{:S(2)}, u32[]{:S(2)}) collective-permute-start(bf16[2,256,512]{2,1,0:T(8,128)(2,1)S(1)} %copy-done.18), channel_id=1, source_target_pairs={{0,6},{1,2},{2,0},{3,4},{4,3},{5,7},{6,5},{7,1},{8,14},{9,10},{10,... | collective-permute-start | bytes 1572872 | tf_op jit(solution)/shard_map/ppermute | solution.py:383
  134.9 12.0 %copy-start.7 = (bf16[2,256,512]{2,1,0:T(8,128)(2,1)}, bf16[2,256,512]{2,1,0:T(8,128)(2,1)S(1)}, u32[]{:S(2)}) copy-start(bf16[2,256,512]{2,1,0:T(8,128)(2,1)S(1)} %collective-permute-done.7.piece_ref) | copy-start | bytes 1572868
  134.9 95.6 %collective-permute-start.12 = (bf16[2,256,1024]{2,1,0:T(8,128)(2,1)}, bf16[2,256,1024]{2,1,0:T(8,128)(2,1)S(1)}, u32[]{:S(2)}, u32[]{:S(2)}) collective-permute-start(bf16[2,256,1024]{2,1,0:T(8,128)(2,1)} %get-tuple-element.64), channel_id=1, source_target_pairs={{0,6},{1,2},{2,0},{3,4},{4,3},{5,7},{6,5},{7,1},{8,14},{9,10},{10,... | collective-permute-start | bytes 3145736 | tf_op jit(solution)/shard_map/ppermute | solution.py:383
  206.0 9.5 %copy-start.16 = (bf16[2,256,512]{2,1,0:T(8,128)(2,1)S(1)}, bf16[2,256,512]{2,1,0:T(8,128)(2,1)}, u32[]{:S(2)}) copy-start(bf16[2,256,512]{2,1,0:T(8,128)(2,1)} %get-tuple-element.60) | copy-start | bytes 1572868
  209.5 45.1 %collective-permute-start.10 = (bf16[2,256,512]{2,1,0:T(8,128)(2,1)}, bf16[2,256,512]{2,1,0:T(8,128)(2,1)S(1)}, u32[]{:S(2)}, u32[]{:S(2)}) collective-permute-start(bf16[2,256,512]{2,1,0:T(8,128)(2,1)} %get-tuple-element.62), channel_id=1, source_target_pairs={{0,2},{1,6},{2,4},{3,0},{4,7},{5,3},{6,1},{7,5},{8,10},{9,14},{10,... | collective-permute-start | bytes 1572872 | tf_op jit(solution)/shard_map/ppermute | solution.py:389
  211.2 10.7 %copy-start.1 = (bf16[2,256,1024]{2,1,0:T(8,128)(2,1)}, bf16[2,256,1024]{2,1,0:T(8,128)(2,1)S(1)}, u32[]{:S(2)}) copy-start(bf16[2,256,1024]{2,1,0:T(8,128)(2,1)S(1)} %collective-permute-done.13.piece_ref) | copy-start | bytes 3145732
  211.2 40.0 %collective-permute-start.11 = (bf16[2,256,512]{2,1,0:T(8,128)(2,1)}, bf16[2,256,512]{2,1,0:T(8,128)(2,1)S(1)}, u32[]{:S(2)}, u32[]{:S(2)}) collective-permute-start(bf16[2,256,512]{2,1,0:T(8,128)(2,1)} %get-tuple-element.63), channel_id=1, source_target_pairs={{0,0},{1,4},{2,2},{3,6},{4,5},{5,1},{6,7},{7,3},{8,8},{9,12},{10,1... | collective-permute-start | bytes 1572872 | tf_op jit(solution)/shard_map/ppermute | solution.py:389
  213.6 44.5 %collective-permute-start.9 = (bf16[2,256,512]{2,1,0:T(8,128)(2,1)S(1)}, bf16[2,256,512]{2,1,0:T(8,128)(2,1)S(1)}, u32[]{:S(2)}, u32[]{:S(2)}) collective-permute-start(bf16[2,256,512]{2,1,0:T(8,128)(2,1)S(1)} %copy-done.17), channel_id=1, source_target_pairs={{0,4},{1,0},{2,6},{3,2},{4,1},{5,5},{6,3},{7,7},{8,12},{9,8},{10,1... | collective-permute-start | bytes 1572872 | tf_op jit(solution)/shard_map/ppermute | solution.py:389
  215.6 45.9 %collective-permute-start.8 = (bf16[2,256,512]{2,1,0:T(8,128)(2,1)S(1)}, bf16[2,256,512]{2,1,0:T(8,128)(2,1)S(1)}, u32[]{:S(2)}, u32[]{:S(2)}) collective-permute-start(bf16[2,256,512]{2,1,0:T(8,128)(2,1)S(1)} %copy-done.16), channel_id=1, source_target_pairs={{0,6},{1,2},{2,0},{3,4},{4,3},{5,7},{6,5},{7,1},{8,14},{9,10},{10,... | collective-permute-start | bytes 1572872 | tf_op jit(solution)/shard_map/ppermute | solution.py:389
  (11 other events, 24.2 us)

commit v3 on v2

v3 whole, which is shorter than its diff:
```python
import functools

import jax
import jax.numpy as jnp
from jax import lax
from jax.experimental import pallas as pl
from jax.experimental.pallas import tpu as pltpu
from jax.sharding import PartitionSpec as P

BLK = 256
norm_eps = 1e-05
VMEM_LIMIT = 56 * 2**20
F32 = jnp.float32
BF16 = jnp.bfloat16


def params(limit=VMEM_LIMIT):
    return pltpu.CompilerParams(vmem_limit_bytes=limit)


def whole(shape):
    return pl.BlockSpec(shape, lambda *_: (0,) * len(shape))


def extra_rows(width):
    lanes = min(width, BLK)
    return lanes, BLK // lanes


def pad8(count):
    return -(-count // 8) * 8


class Table:
    def __init__(self, n, t, chunks):
        self.n, self.t, self.chunks = n, t, chunks
        self.stride, self.per = n // t, chunks // n
        self.half = 0
        self.which = 1
        self.slot = self.which + chunks
        self.place = self.slot + chunks
        self.row = self.place + n * chunks
        self.side = self.row + n
        self.shard = self.side + n
        self.size = self.shard + chunks


def fill_table(tab, shard_ref, table_ref):
    n, per, chunks = tab.n, tab.per, tab.chunks
    ctx, tp = lax.axis_index("ctx"), lax.axis_index("tp")
    table_ref[tab.half] = tp
    seen = [jnp.int32(0)] * n
    for c in range(chunks):
        shard = shard_ref[ctx * chunks + c]
        op = lax.rem(shard - ctx - tp * tab.stride + 2 * n, n)
        table_ref[tab.which + c] = op
        rank = jnp.int32(0)
        for k in range(n):
            table_ref[tab.place + k * chunks + c] = jnp.minimum(seen[k], per - 1)
            here = (op == k).astype(jnp.int32)
            rank = rank + here * seen[k]
            seen[k] = seen[k] + here
        table_ref[tab.slot + c] = op * per + jnp.minimum(rank, per - 1)
        table_ref[tab.shard + c] = shard * per + jnp.minimum(rank, per - 1)
    for op in range(n):
        lane = lax.rem(ctx - op + n, tab.stride)
        source = tp * tab.stride + lane
        table_ref[tab.row + op] = lane * per
        table_ref[tab.side + op] = lax.rem(ctx - op - source + 2 * n, n) // tab.stride


def fill_gates(len_ref, decay_ref, rows_ref, cols_ref, docs_ref, total_ref, tail_ref, scr):
    heads, tokens = decay_ref.shape
    hp = pad8(heads)
    chunks = tokens // BLK
    base = lax.axis_index("ctx") * tokens
    starts, run = [], jnp.int32(0)
    for i in range(len_ref.shape[0]):
        starts.append(run)
        run = run + len_ref[i]

    def doc_at(position):
        found = jnp.int32(0)
        for start in starts:
            found = found + (position >= start).astype(jnp.int32)
        return found - 1

    position = base + lax.broadcasted_iota(jnp.int32, (8, tokens), 1)
    doc = jnp.zeros((8, tokens), jnp.int32) - 1
    for start in starts:
        doc = doc + (position >= start).astype(jnp.int32)
    docs_ref[...] = doc.astype(F32)
    edges = [doc_at(base - 1)] + [doc_at(base + (c + 1) * BLK - 1) for c in range(chunks)]

    first = lax.broadcasted_iota(jnp.int32, (BLK, BLK), 0)
    second = lax.broadcasted_iota(jnp.int32, (BLK, BLK), 1)
    upto = jnp.where(first <= second, 1.0, 0.0).astype(F32)
    every = jnp.ones((BLK, BLK), F32)
    scr[...] = jnp.zeros_like(scr)
    cums, sums = [], []
    for c in range(chunks):
        part = decay_ref[:, c * BLK : (c + 1) * BLK]
        cums.append(jnp.dot(part, upto, precision=lax.Precision.HIGHEST, preferred_element_type=F32))
        sums.append(jnp.dot(part, every, precision=lax.Precision.HIGHEST, preferred_element_type=F32))
    before, after = [], [None] * chunks
    run = jnp.zeros_like(sums[0])
    for c in range(chunks):
        before.append(run)
        run = run + sums[c]
    run = jnp.zeros_like(sums[0])
    for c in reversed(range(chunks)):
        after[c] = run
        run = run + sums[c]
    for c in range(chunks):
        span = slice(c * BLK, (c + 1) * BLK)
        doc_c = doc[:1, span]
        cum, total = cums[c], sums[c]
        rows_ref[0:heads, span] = cum
        rows_ref[hp : hp + heads, span] = jnp.where(doc_c == edges[c + 1], jnp.exp(total - cum), 0.0)
        tail_ref[0:heads, span] = jnp.where(doc_c == edges[-1], jnp.exp(total - cum + after[c]), 0.0)
        rows_ref[2 * hp : 2 * hp + heads, span] = jnp.where(
            edges[c + 1] == edges[c], jnp.exp(total), 0.0
        )
        scr[0:heads, span] = cum
        scr[hp : hp + heads, span] = jnp.where(doc_c == edges[c], jnp.exp(cum), 0.0)
        scr[2 * hp + 8 : 2 * hp + 8 + heads, span] = jnp.where(
            doc_c == edges[0], jnp.exp(before[c] + cum), 0.0
        )
    scr[2 * hp : 2 * hp + 8, :] = doc.astype(F32)
    cols_ref[...] = scr[...].T
    total_ref[...] = jnp.where(edges[-1] == edges[0], jnp.exp(run[:, :128]), 0.0)


def prelude_kernel(tab, splits, len_ref, shard_ref, decay_ref, key_ref, value_ref, *refs):
    rows_ref, cols_ref, docs_ref, total_ref, table_ref = refs[:5]
    lows, fulls = refs[5 : 5 + len(splits)], refs[5 + len(splits) : 5 + 2 * len(splits)]
    tail_ref, scr, acc = refs[5 + 2 * len(splits) :]
    step = pl.program_id(0)
    tile = key_ref.shape[0]

    @pl.when(step == 0)
    def _():
        fill_table(tab, shard_ref, table_ref)
        fill_gates(len_ref, decay_ref, rows_ref, cols_ref, docs_ref, total_ref, tail_ref, scr)
        acc[...] = jnp.zeros_like(acc)

    tails = tail_ref[:, pl.ds(pl.multiple_of(step * tile, tile), tile)]
    for h in range(acc.shape[0]):
        cols = slice(h * 128, (h + 1) * 128)
        scaled = (key_ref[:, cols].T.astype(F32) * tails[h : h + 1, :]).astype(BF16)
        acc[h] += jnp.dot(scaled, value_ref[:, cols], preferred_element_type=F32)

    @pl.when(step == pl.num_programs(0) - 1)
    def _():
        for (lo, count), low_ref, full_ref in zip(splits, lows, fulls):
            low_ref[...] = acc[lo : lo + count].astype(BF16)
            full_ref[...] = acc[lo : lo + count]


def prelude(tab, splits, doc_lengths, block_shard, decay, key, value):
    heads, tokens = decay.shape
    hp = pad8(heads)
    tile = 2 * BLK
    smem = pl.BlockSpec(memory_space=pltpu.SMEM)
    shapes = [(3 * hp, tokens), (tokens, 128), (8, tokens), (heads, 128)]
    states = [(count, 128, 128) for _, count in splits]
    wide = pl.BlockSpec((tile, key.shape[1]), lambda c: (c, 0))
    return pl.pallas_call(
        functools.partial(prelude_kernel, tab, splits),
        grid=(tokens // tile,),
        in_specs=[smem, smem, whole(decay.shape), wide, wide],
        out_specs=[whole(shape) for shape in shapes] + [smem] + [whole(shape) for shape in states * 2],
        out_shape=[jax.ShapeDtypeStruct(shape, F32) for shape in shapes]
        + [jax.ShapeDtypeStruct((tab.size,), jnp.int32)]
        + [jax.ShapeDtypeStruct(shape, BF16) for shape in states]
        + [jax.ShapeDtypeStruct(shape, F32) for shape in states],
        scratch_shapes=[
            pltpu.VMEM((hp, tokens), F32),
            pltpu.VMEM((128, tokens), F32),
            pltpu.VMEM((heads, 128, 128), F32),
        ],
        compiler_params=params(),
        name="prelude",
    )(doc_lengths, block_shard, decay, key, value)


def barred_pairs(hp, cols_ref, docs_ref):
    first = lax.broadcasted_iota(jnp.int32, (BLK, BLK), 0)
    second = lax.broadcasted_iota(jnp.int32, (BLK, BLK), 1)
    same = cols_ref[:, 2 * hp : 2 * hp + 1] == docs_ref[0:1, :]
    return jnp.where((first >= second) & same, 0.0, -1e30).astype(F32)


def chunk_of_head(h, head, hp, barred, query_ref, key_ref, value_ref, rows_ref, cols_ref, state):
    cols = slice(h * 128, (h + 1) * 128)
    query, value = query_ref[:, cols], value_ref[:, cols]
    key_t = key_ref[:, cols].T
    scores = jnp.dot(query, key_t, preferred_element_type=F32)
    gap = cols_ref[:, head : head + 1] - rows_ref[head : head + 1, :] + barred
    weights = (scores * jnp.exp(gap)).astype(BF16)
    intra = jnp.dot(weights, value, preferred_element_type=F32)
    reached = jnp.dot(query, state[h].astype(BF16), preferred_element_type=F32)
    scaled = (key_t.astype(F32) * rows_ref[hp + head : hp + head + 1, :]).astype(BF16)
    carry = rows_ref[2 * hp + head : 2 * hp + head + 1, :128]
    state[h] = carry * state[h] + jnp.dot(scaled, value, preferred_element_type=F32)
    return intra + cols_ref[:, hp + head : hp + head + 1] * reached


def gate_head(h, attended, square, gain_ref, gate_ref, gated):
    cols = slice(h * 128, (h + 1) * 128)
    attended = attended.astype(BF16).astype(F32)
    gated[:BLK, cols] = (
        attended * gain_ref[0:1, cols] * jax.nn.sigmoid(gate_ref[:, cols].astype(F32))
    ).astype(BF16)
    return square + attended * attended


def own_kernel(lo, hp, count, query_ref, key_ref, value_ref, rows_ref, cols_ref, docs_ref, own_ref, state):
    @pl.when(pl.program_id(0) == 0)
    def _():
        state[...] = jnp.zeros_like(state)

    barred = barred_pairs(hp, cols_ref, docs_ref)
    for h in range(count):
        own_ref[:, h * 128 : (h + 1) * 128] = chunk_of_head(
            h, lo + h, hp, barred, query_ref, key_ref, value_ref, rows_ref, cols_ref, state
        )


def attend_own(query, key, value, rows, cols, docs, lo, count):
    tokens = query.shape[0]
    hp = rows.shape[0] // 3
    width = count * 128
    at = lo * 128 // width
    wide = pl.BlockSpec((BLK, width), lambda c: (c, at))
    return pl.pallas_call(
        functools.partial(own_kernel, lo, hp, count),
        grid=(tokens // BLK,),
        in_specs=[
            wide,
            wide,
            wide,
            pl.BlockSpec((rows.shape[0], BLK), lambda c: (0, c)),
            pl.BlockSpec((BLK, 128), lambda c: (c, 0)),
            pl.BlockSpec((8, BLK), lambda c: (0, c)),
        ],
        out_specs=pl.BlockSpec((BLK, width), lambda c: (c, 0)),
        out_shape=jax.ShapeDtypeStruct((tokens, width), F32),
        scratch_shapes=[pltpu.VMEM((count, 128, 128), F32)],
        compiler_params=params(),
        cost_estimate=pl.CostEstimate(
            flops=8 * tokens * width * BLK, bytes_accessed=10 * tokens * width, transcendentals=0
        ),
        name="attend_own",
    )(query, key, value, rows, cols, docs)


def enter_kernel(tab, lo, hp, count, table_ref, query_ref, own_ref, gate_ref, gain_ref, cols_ref, state_ref, out_ref, square_ref):
    square = jnp.zeros((BLK, 128), F32)
    for h in range(count):
        cols = slice(h * 128, (h + 1) * 128)
        reached = jnp.dot(query_ref[:, cols], state_ref[h], preferred_element_type=F32)
        column = 2 * hp + 8 + lo + h
        attended = own_ref[:, cols] + cols_ref[:, column : column + 1] * reached
        square = gate_head(h, attended, square, gain_ref, gate_ref, out_ref.at[0])
    square_ref[0] = jnp.sum(square.T, axis=0, keepdims=True)


def attend_entered(tab, table, query, own, gate, gain, cols, entering, lo, count, hp):
    tokens, local_width = query.shape
    width = count * 128
    at = lo * 128 // width
    wide = pl.BlockSpec((BLK, width), lambda c, tbl: (c, at))
    return pl.pallas_call(
        functools.partial(enter_kernel, tab, lo, hp, count),
        grid_spec=pltpu.PrefetchScalarGridSpec(
            num_scalar_prefetch=1,
            grid=(tab.chunks,),
            in_specs=[
                wide,
                pl.BlockSpec((BLK, width), lambda c, tbl: (c, 0)),
                wide,
                pl.BlockSpec((1, width), lambda c, tbl: (0, tbl[tab.half] * (local_width // width) + at)),
                pl.BlockSpec((BLK, 128), lambda c, tbl: (c, 0)),
                whole((count, 128, 128)),
            ],
            out_specs=[
                pl.BlockSpec((1, BLK, width), lambda c, tbl: (tbl[tab.shard + c], 0, 0)),
                pl.BlockSpec((1, 1, BLK), lambda c, tbl: (tbl[tab.slot + c], 0, 0)),
            ],
        ),
        out_shape=[
            jax.ShapeDtypeStruct((tab.chunks, BLK, width), BF16),
            jax.ShapeDtypeStruct((tab.chunks, 1, BLK), F32),
        ],
        compiler_params=params(),
        cost_estimate=pl.CostEstimate(flops=width, bytes_accessed=width, transcendentals=0),
        name="attend_entered",
    )(table, query, own, gate, gain, cols, entering)


def attend_kernel(tab, lo, hp, count, last, *refs):
    ops = tab.n
    (table_ref, query_ref, key_ref, value_ref, gate_ref, gain_ref, rows_ref, cols_ref, docs_ref, state_ref, squares_ref) = refs[:11]
    outs = refs[11 : 11 + ops]
    state, gated = refs[-2:]
    step = pl.program_id(0)

    @pl.when(step == 0)
    def _():
        state[...] = state_ref[...].astype(F32)
        if last:
            gated[BLK:, :] = jnp.zeros((16, gated.shape[1]), BF16)

    barred = barred_pairs(hp, cols_ref, docs_ref)
    square = jnp.zeros((BLK, 128), F32)
    for h in range(count):
        attended = chunk_of_head(
            h, lo + h, hp, barred, query_ref, key_ref, value_ref, rows_ref, cols_ref, state
        )
        square = gate_head(h, attended, square, gain_ref, gate_ref, gated)
    total = jnp.sum(square.T, axis=0, keepdims=True) + squares_ref[0]
    if last:
        lanes, lines = extra_rows(gated.shape[1])
        row = lax.broadcasted_iota(jnp.int32, (16, lanes), 0)
        extra, left = jnp.zeros((16, lanes), F32), total
        for term in range(3):
            part = left.astype(BF16).astype(F32)
            left = left - part
            for line in range(lines):
                piece = part[:, line * lanes : (line + 1) * lanes]
                extra = jnp.where(row == term * lines + line, piece, extra)
        gated[BLK:, :lanes] = extra.astype(BF16)
    else:
        refs[11 + ops][0] = total
    which = table_ref[tab.which + step]
    for op in range(ops):

        @pl.when(which == op)
        def _():
            outs[op][0] = gated[...]


def attend(tab, table, query, key, value, gate, gain, rows, cols, docs, entering, base, lo, count, squares, last):
    tokens, local_width = query.shape
    chunks, per = tab.chunks, tab.per
    ops = tab.n
    hp = rows.shape[0] // 3
    width = count * 128
    at = lo * 128 // width
    height = BLK + 16 * last
    wide = pl.BlockSpec((BLK, width), lambda c, tbl: (c, at))
    square_spec = pl.BlockSpec((1, 1, BLK), lambda c, tbl: (tbl[tab.slot + c], 0, 0))

    def out_map(op, c, tbl):
        return (tbl[tab.place + op * chunks + c], 0, 0)

    out = pl.pallas_call(
        functools.partial(attend_kernel, tab, lo, hp, count, last),
        grid_spec=pltpu.PrefetchScalarGridSpec(
            num_scalar_prefetch=1,
            grid=(chunks,),
            in_specs=[
                wide,
                wide,
                wide,
                wide,
                pl.BlockSpec((1, width), lambda c, tbl: (0, tbl[tab.half] * (local_width // width) + at)),
                pl.BlockSpec((rows.shape[0], BLK), lambda c, tbl: (0, c)),
                pl.BlockSpec((BLK, 128), lambda c, tbl: (c, 0)),
                pl.BlockSpec((8, BLK), lambda c, tbl: (0, c)),
                pl.BlockSpec((count, 128, 128), lambda c, tbl: ((lo - base) // count, 0, 0)),
            ]
            + [square_spec],
            out_specs=[
                pl.BlockSpec((1, height, width), functools.partial(out_map, op)) for op in range(ops)
            ]
            + [square_spec] * (not last),
            scratch_shapes=[
                pltpu.VMEM((count, 128, 128), F32),
                pltpu.VMEM((height, width), BF16),
            ],
        ),
        out_shape=[jax.ShapeDtypeStruct((chunks // ops, height, width), BF16)] * ops
        + [jax.ShapeDtypeStruct((chunks, 1, BLK), F32)] * (not last),
        compiler_params=params(),
        cost_estimate=pl.CostEstimate(flops=width, bytes_accessed=width, transcendentals=0),
        name="attend",
    )(table, query, key, value, gate, gain, rows, cols, docs, entering, squares)
    return out[:ops], None if last else out[ops]


def place_kernel(features, t, count, lanes, lines, table_ref, *refs):
    out_ref = refs[-1]
    square = []
    for line in range(lines):
        parts = [refs[k][0, term * lines + line : term * lines + line + 1, :] for k in range(t) for term in range(3)]
        square.append(sum(part.astype(F32) for part in parts))
    scale = [lax.rsqrt(row / features + norm_eps) for row in square]
    scale = jnp.concatenate([jnp.broadcast_to(row, (128, lanes)).T for row in scale], axis=0)
    done = 0
    for piece_ref in refs[t : t + count]:
        for c in range(piece_ref.shape[2] // 128):
            piece = piece_ref[0, :BLK, c * 128 : (c + 1) * 128].astype(F32)
            out_ref[:, done : done + 128] = (piece * scale).astype(BF16)
            done += 128


def place(tab, table, op, lo, pieces, extras, out, shape, local_width, features):
    def piece_map(all_blocks, c, tbl):
        block = tbl[tab.side + op] * tab.stride * tab.per + tbl[tab.row + op] if all_blocks else 0
        return (block + c, 0, 0)

    lanes, lines = extra_rows(extras[0].shape[2])
    unit = sum(piece.shape[2] for piece in pieces)

    def out_map(c, tbl):
        return (tbl[tab.row + op] + c, tbl[tab.side + op] * (local_width // unit) + lo * 128 // unit)

    in_specs = [pl.BlockSpec((1, 16, lanes), lambda c, tbl: (c, BLK // 16, 0))] * tab.t
    in_specs += [
        pl.BlockSpec((1, *piece.shape[1:]), functools.partial(piece_map, piece.shape[0] > tab.per))
        for piece in pieces
    ]
    operands = [table, *extras, *pieces]
    aliases = {}
    if out is not None:
        in_specs.append(pl.BlockSpec(memory_space=pl.ANY))
        operands.append(out)
        aliases = {len(operands) - 1: 0}
    return pl.pallas_call(
        functools.partial(place_kernel, features, tab.t, len(pieces), lanes, lines),
        grid_spec=pltpu.PrefetchScalarGridSpec(
            num_scalar_prefetch=1,
            grid=(tab.per,),
            in_specs=in_specs,
            out_specs=pl.BlockSpec((BLK, unit), out_map),
        ),
        out_shape=jax.ShapeDtypeStruct(shape, BF16),
        input_output_aliases=aliases,
        compiler_params=params(63 * 2**20),
        cost_estimate=pl.CostEstimate(flops=unit, bytes_accessed=unit, transcendentals=0),
        name="place",
    )(*operands)


def local(query_rows, key_rows, value_rows, gate_rows, decay_log, norm_gain, doc_lengths, block_shard):
    tokens, width = query_rows.shape
    heads = decay_log.shape[0]
    features = norm_gain.shape[0]
    n, t = lax.axis_size("ctx"), lax.axis_size("tp")
    tab = Table(n, t, tokens // BLK)
    quarter = max(1, heads // 4)

    rest = heads - quarter
    splits = ((rest, quarter), (0, rest))
    (rows, cols, docs, total_gate, table, *states) = prelude(
        tab, splits, doc_lengths, block_shard, decay_log, key_rows, value_rows
    )
    gain = norm_gain.reshape(1, features)
    hop = [(i, i + 1) for i in range(n - 1)]

    def route(op):
        return [
            (d * t + k, (d + op + k * tab.stride) % n * t + d // tab.stride)
            for d in range(n)
            for k in range(t)
        ]

    def relay(lo, count, low, full):
        carry = total_gate[lo : lo + count, :1, None]
        for _ in range(max(1, n // 2) - 1):
            low = (carry * lax.ppermute(low, "ctx", hop).astype(F32) + full).astype(BF16)
        return low

    early, later = (relay(*split, low, full) for split, low, full in zip(splits, states[:2], states[2:]))
    own = attend_own(query_rows, key_rows, value_rows, rows, cols, docs, rest, quarter)
    early, own = lax.optimization_barrier((early, own))
    early = lax.ppermute(early, "ctx", hop)
    early, later = lax.optimization_barrier((early, later))
    entering = lax.ppermute(later, "ctx", hop)
    ready, squares = attend_entered(
        tab, table, query_rows, own, gate_rows, gain, cols, early, rest, quarter, rows.shape[0] // 3
    )
    ready, entering = lax.optimization_barrier((ready, entering))
    gated = [None]
    for lo, count in ((0, 2 * quarter), (2 * quarter, quarter)):
        outs, squares = attend(
            tab, table, query_rows, key_rows, value_rows, gate_rows, gain, rows, cols, docs,
            entering, 0, lo, count, squares, lo > 0,
        )
        gated.append(outs)
    head = lax.all_to_all(ready, "ctx", split_axis=0, concat_axis=0, tiled=True)
    head = lax.all_to_all(head, "tp", split_axis=0, concat_axis=0, tiled=True)
    tail = [lax.ppermute(gated[2][op], ("ctx", "tp"), route(op)) for op in range(n)]
    middle = []
    for op in range(n):
        ready = gated[1][op]
        for before in ([], [0, n - 1])[op] if op < 2 else [op - 1]:
            ready, tail[before] = lax.optimization_barrier((ready, tail[before]))
        middle.append(lax.ppermute(ready, ("ctx", "tp"), route(op)))

    shape = (tokens // t, features)
    out = None
    for pieces, lo in ((lambda op: [tail[op], head], 2 * quarter), (lambda op: [middle[op]], 0)):
        for op in range(n):
            extras = [tail[(op + k * tab.stride) % n] for k in range(t)]
            out = place(tab, table, op, lo, pieces(op), extras, out, shape, width, features)
    return out


def solution(mesh):
    return jax.shard_map(
        local,
        mesh=mesh,
        in_specs=(
            P(("dp", "ctx"), "tp"),
            P(("dp", "ctx"), "tp"),
            P(("dp", "ctx"), "tp"),
            P(("dp", "ctx"), "tp"),
            P("tp", ("dp", "ctx")),
            P(),
            P("dp"),
            P("dp"),
        ),
        out_specs=P(("dp", "ctx", "tp"), None),
        check_vma=False,
    )
```

time: 267 us -> 242 us (0.906)
  the two profiles are of different devices: /device:TPU:1 before, /device:TPU:9 now
where the time goes in v3:
time: 242 us; the launch traced here: 238 us
  waiting for transfers between devices  107 us (44%)
  Pallas kernels  83.6 us (35%)
  starting transfers between devices  40.7 us (17%)
  blocking collectives  5.93 us (2%)
    ppermute x4, waiting for transfers between devices, local(): lax.ppermute(gated[2][op], ('ctx', 'tp'), route(op))  61 us
    ppermute x4, waiting for transfers between devices, local(): middle.append(lax.ppermute(ready, ('ctx', 'tp'), route(op)))  42.6 us
    pallas_call x2, Pallas kernels, attend(): pl.pallas_call(functools.partial(attend_kernel, tab, lo, hp, count, last)...  29.5 us
    pallas_call x8, Pallas kernels, place(): pl.pallas_call(functools.partial(place_kernel, features, tab.t, len(piece...  23.6 us
    ppermute x4, starting transfers between devices, local(): middle.append(lax.ppermute(ready, ('ctx', 'tp'), route(op)))  14.5 us
    pallas_call x1, Pallas kernels, prelude(): pl.pallas_call(functools.partial(prelude_kernel, tab, splits), grid=(toke...  11.5 us
    ppermute x4, starting transfers between devices, local(): lax.ppermute(gated[2][op], ('ctx', 'tp'), route(op))  10.9 us
    pallas_call x1, Pallas kernels, attend_own(): pl.pallas_call(functools.partial(own_kernel, lo, hp, count), grid=(tokens...  10 us
  transfers between devices with their start and end apart: 13, of which 7 were waited for; matrix products, arithmetic and copies ran while one was open for 0% of the time, Pallas kernels for 29%

profile of v3, /device:TPU:9, one launch (start us, length us, event | category | flops | bytes accessed | tf_op | source)
XLA Modules:
  0.0 238.1 jit_solution(1441607161430723053)
XLA Ops:
  0.0 11.5 %prelude.1 = (f32[48,2048]{1,0:T(8,128)}, f32[2048,128]{1,0:T(8,128)}, f32[8,2048]{1,0:T(8,128)}, f32[16,128]{1,0:T(8,128)}, s32[65]{0:T(128)}, /*index=5*/bf16[...) custom-call(s32[16]{0:T(128)} %len_ref.1, s32[32]{0:T(128)} %shard_ref.1, ...), custom_call_target="tpu_custom_call" | custom-call | tf_op jit(solution)/shard_map/prelude/pallas_call | solution.py:168
  11.5 3.2 %collective-permute-start = (bf16[4,128,128]{2,1,0:T(8,128)(2,1)}, bf16[4,128,128]{2,1,0:T(8,128)(2,1)S(1)}, u32[]{:S(2)}, u32[]{:S(2)}) collective-permute-start(bf16[4,128,128]{2,1,0:T(8,128)(2,1)} %get-tuple-element.44), channel_id=1, source_target_pairs={{0,2},{2,4},{4,6},{1,3},{3,5},{5,7},{8,10},{10,12},{12,14},{9,11},... | collective-permute-start | bytes 393224 | tf_op jit(solution)/shard_map/ppermute | solution.py:473
  14.7 3.2 %collective-permute-start.2 = (bf16[12,128,128]{2,1,0:T(8,128)(2,1)}, bf16[12,128,128]{2,1,0:T(8,128)(2,1)S(1)}, u32[]{:S(2)}, u32[]{:S(2)}) collective-permute-start(bf16[12,128,128]{2,1,0:T(8,128)(2,1)} %get-tuple-element.48), channel_id=1, source_target_pairs={{0,2},{2,4},{4,6},{1,3},{3,5},{5,7},{8,10},{10,12},{12,14},{9,11},... | collective-permute-start | bytes 1179656 | tf_op jit(solution)/shard_map/ppermute | solution.py:473
  17.9 10.0 %attend_own.1.own_ref = f32[2048,512]{1,0:T(8,128)} custom-call(bf16[2048,2048]{1,0:T(8,128)(2,1)} %refs_1_.3, bf16[2048,2048]{1,0:T(8,128)(2,1)} %refs_2_.3, bf16[2048,2048]{1,0:T(8,128)(2,1)} %refs_3_.3, f32[48,2048]{1,0:T(8,128)} %get-tuple-element.40.rows_ref.refs_6_, f32[2048,128]{1,0:T(8,128)} %get-tuple-element.41.cols_ref.refs_7_, ...), custom_call_target="tpu_custom_call" | custom-call | flops 2147483648 | bytes 10485760 | tf_op jit(solution)/shard_map/attend_own/pallas_call | solution.py:236
  30.4 3.6 %collective-permute-done.1.state_ref = bf16[4,128,128]{2,1,0:T(8,128)(2,1)S(1)} collective-permute-done((bf16[4,128,128]{2,1,0:T(8,128)(2,1)S(1)}, bf16[4,128,128]{2,1,0:T(8,128)(2,1)S(1)}, u32[]{:S(2)}, u32[]{:S(2)}) %collective-permute-start.1) | collective-permute-done | bytes 131104 | tf_op jit(solution)/shard_map/ppermute | solution.py:479
  36.0 9.0 %attend_entered.1 = (bf16[8,256,512]{2,1,0:T(8,128)(2,1)}, f32[8,1,256]{2,1,0:T(1,128)}) custom-call(s32[65]{0:T(128)} %get-tuple-element.39.table_ref.refs_0_, bf16[2048,2048]{1,0:T(8,128)(2,1)} %refs_1_.3, f32[2048,512]{1,0:T(8,128)} %attend_own.1.own_ref, bf16[2048,2048]{1,0:T(8,128)(2,1)} %refs_4_.3, f32[1,4096]{1,0:T(1,128)} %bitcast.1, ...), custom_call_target="tpu_custom_call" | custom-call | flops 512 | bytes 512 | tf_op jit(solution)/shard_map/attend_entered/pallas_call | solution.py:274
  45.0 5.0 %all-to-all-start = ((bf16[8,256,512]{2,1,0:T(8,128)(2,1)}), bf16[8,256,512]{2,1,0:T(8,128)(2,1)S(1)}, u32[]{:S(2)}, u32[]{:S(2)}) async-start(bf16[8,256,512]{2,1,0:T(8,128)(2,1)} %get-tuple-element.72), calls=%async_computation | async-start | bytes 4194304 | tf_op jit(solution)/shard_map/all_to_all | solution.py:493
  50.0 17.4 %attend.2 = (bf16[2,256,1024]{2,1,0:T(8,128)(2,1)}, bf16[2,256,1024]{2,1,0:T(8,128)(2,1)}, bf16[2,256,1024]{2,1,0:T(8,128)(2,1)}, bf16[2,256,1024]{2,1,0:T(8,128)(2,1)}, f32[8,1,256]{2,1,0:T(1,128)}) custom-call(s32[65]{0:T(128)} %get-tuple-element.39.table_ref.refs_0_, bf16[2048,2048]{1,0:T(8,128)(2,1)} %refs_1_.3, bf16[2048,2048]{1,0:T(8,128)(2,1)} %refs_2_.3, ...), custom_call_target="tpu_custom_call" | custom-call | flops 1024 | bytes 1024 | tf_op jit(solution)/shard_map/attend/pallas_call | solution.py:358
  67.5 12.1 %attend.3 = (bf16[2,272,512]{2,1,0:T(8,128)(2,1)}, bf16[2,272,512]{2,1,0:T(8,128)(2,1)}, bf16[2,272,512]{2,1,0:T(8,128)(2,1)}, bf16[2,272,512]{2,1,0:T(8,128)(2,1)}) custom-call(s32[65]{0:T(128)} %get-tuple-element.39.table_ref.refs_0_, bf16[2048,2048]{1,0:T(8,128)(2,1)} %refs_1_.3, bf16[2048,2048]{1,0:T(8,128)(2,1)} %refs_2_.3, bf16[2048,2048]{1,0:T(8,128)(2,1)} %refs_3_.3, ...), custom_call_target="tpu_custom_call" | custom-call | flops 512 | bytes 512 | tf_op jit(solution)/shard_map/attend/pallas_call | solution.py:358
  79.5 6.8 %collective-permute-start.4 = (bf16[2,272,512]{2,1,0:T(8,128)(2,1)}, bf16[2,272,512]{2,1,0:T(8,128)(2,1)S(1)}, u32[]{:S(2)}, u32[]{:S(2)}) collective-permute-start(bf16[2,272,512]{2,1,0:T(8,128)(2,1)} %get-tuple-element.57), channel_id=1, source_target_pairs={{0,0},{1,4},{2,2},{3,6},{4,5},{5,1},{6,7},{7,3},{8,8},{9,12},{10,1... | collective-permute-start | bytes 1671176 | tf_op jit(solution)/shard_map/ppermute | solution.py:495
  90.5 3.9 %collective-permute-start.11 = (bf16[2,256,1024]{2,1,0:T(8,128)(2,1)}, bf16[2,256,1024]{2,1,0:T(8,128)(2,1)}, u32[]{:S(2)}, u32[]{:S(2)}) collective-permute-start(bf16[2,256,1024]{2,1,0:T(8,128)(2,1)} %get-tuple-element.71), channel_id=1, source_target_pairs={{0,0},{1,4},{2,2},{3,6},{4,5},{5,1},{6,7},{7,3},{8,8},{9,12},{10,1... | collective-permute-start | bytes 3145736 | tf_op jit(solution)/shard_map/ppermute | solution.py:501
  94.4 45.3 %collective-permute-done.4.refs_0_.refs_2_.refs_1_ = bf16[2,272,512]{2,1,0:T(8,128)(2,1)S(1)} collective-permute-done((bf16[2,272,512]{2,1,0:T(8,128)(2,1)}, bf16[2,272,512]{2,1,0:T(8,128)(2,1)S(1)}, u32[]{:S(2)}, u32[]{:S(2)}) %collective-permute-start.4) | collective-permute-done | bytes 557088 | tf_op jit(solution)/shard_map/ppermute | solution.py:495
  139.7 11.9 %collective-permute-done.5.refs_1_.refs_0_.refs_2_ = bf16[2,272,512]{2,1,0:T(8,128)(2,1)S(1)} collective-permute-done((bf16[2,272,512]{2,1,0:T(8,128)(2,1)}, bf16[2,272,512]{2,1,0:T(8,128)(2,1)S(1)}, u32[]{:S(2)}, u32[]{:S(2)}) %collective-permute-start.5) | collective-permute-done | bytes 557088 | tf_op jit(solution)/shard_map/ppermute | solution.py:495
  151.6 3.8 %collective-permute-done.6.refs_0_.refs_2_.refs_1_ = bf16[2,272,512]{2,1,0:T(8,128)(2,1)} collective-permute-done((bf16[2,272,512]{2,1,0:T(8,128)(2,1)}, bf16[2,272,512]{2,1,0:T(8,128)(2,1)}, u32[]{:S(2)}, u32[]{:S(2)}) %collective-permute-start.6) | collective-permute-done | bytes 557088 | tf_op jit(solution)/shard_map/ppermute | solution.py:495
  155.4 4.9 %collective-permute-start.9 = (bf16[2,256,1024]{2,1,0:T(8,128)(2,1)}, bf16[2,256,1024]{2,1,0:T(8,128)(2,1)}, u32[]{:S(2)}, u32[]{:S(2)}) collective-permute-start(bf16[2,256,1024]{2,1,0:T(8,128)(2,1)} %get-tuple-element.69), channel_id=1, source_target_pairs={{0,4},{1,0},{2,6},{3,2},{4,1},{5,5},{6,3},{7,7},{8,12},{9,8},{10,1... | collective-permute-start | bytes 3145736 | tf_op jit(solution)/shard_map/ppermute | solution.py:501
  160.3 5.8 %collective-permute-start.8 = (bf16[2,256,1024]{2,1,0:T(8,128)(2,1)}, bf16[2,256,1024]{2,1,0:T(8,128)(2,1)}, u32[]{:S(2)}, u32[]{:S(2)}) collective-permute-start(bf16[2,256,1024]{2,1,0:T(8,128)(2,1)} %get-tuple-element.66), channel_id=1, source_target_pairs={{0,6},{1,2},{2,0},{3,4},{4,3},{5,7},{6,5},{7,1},{8,14},{9,10},{10,... | collective-permute-start | bytes 3145736 | tf_op jit(solution)/shard_map/ppermute | solution.py:501
  166.0 5.9 %all_to_all.10.refs_3_ = bf16[8,256,512]{2,1,0:T(8,128)(2,1)} all-to-all(bf16[8,256,512]{2,1,0:T(8,128)(2,1)S(1)} %all-to-all-done), channel_id=1, replica_groups=mesh['dp'=4,'ctx'=4,'tp'=2] {'tp'}, dimensions={0} | all-to-all | bytes 4194304 | tf_op jit(solution)/shard_map/all_to_all | solution.py:494
  172.0 3.0 %place.8.refs_4_ = bf16[1024,4096]{1,0:T(8,128)(2,1)} custom-call(s32[65]{0:T(128)} %get-tuple-element.39.table_ref.refs_0_, bf16[2,272,512]{2,1,0:T(8,128)(2,1)} %copy-done.1, bf16[2,272,512]{2,1,0:T(8,128)(2,1)} %collective-permute-done.7.refs_1_.refs_0_.refs_2_, bf16[2,272,512]{2,1,0:T(8,128)(2,1)} %copy-done.1, bf16[8,256,512]{2,1,0:T(8,128)(2,1)} %all_to_all.10.refs_3_), custom_call_target="tpu_custom_call" | custom-call | flops 1024 | bytes 1024 | tf_op jit(solution)/shard_map/place/pallas_call | solution.py:431
  174.9 3.0 %place.9.refs_4_ = bf16[1024,4096]{1,0:T(8,128)(2,1)} custom-call(s32[65]{0:T(128)} %get-tuple-element.39.table_ref.refs_0_, bf16[2,272,512]{2,1,0:T(8,128)(2,1)} %collective-permute-done.6.refs_0_.refs_2_.refs_1_, bf16[2,272,512]{2,1,0:T(8,128)(2,1)} %copy-done, ...), custom_call_target="tpu_custom_call", output_to_operand_aliasing={{}: (5, {})} | custom-call | flops 1024 | bytes 1024 | tf_op jit(solution)/shard_map/place/pallas_call | solution.py:431
  186.4 3.0 %place.12.refs_3_ = bf16[1024,4096]{1,0:T(8,128)(2,1)} custom-call(s32[65]{0:T(128)} %get-tuple-element.39.table_ref.refs_0_, bf16[2,272,512]{2,1,0:T(8,128)(2,1)} %copy-done.1, bf16[2,272,512]{2,1,0:T(8,128)(2,1)} %collective-permute-done.7.refs_1_.refs_0_.refs_2_, ...), custom_call_target="tpu_custom_call", output_to_operand_aliasing={{}: (4, {})} | custom-call | flops 1024 | bytes 1024 | tf_op jit(solution)/shard_map/place/pallas_call | solution.py:431
  189.3 37.0 %collective-permute-done.10.refs_2_ = bf16[2,256,1024]{2,1,0:T(8,128)(2,1)} collective-permute-done((bf16[2,256,1024]{2,1,0:T(8,128)(2,1)}, bf16[2,256,1024]{2,1,0:T(8,128)(2,1)}, u32[]{:S(2)}, u32[]{:S(2)}) %collective-permute-start.10) | collective-permute-done | bytes 1048608 | tf_op jit(solution)/shard_map/ppermute | solution.py:501
  226.3 3.0 %place.13.refs_3_ = bf16[1024,4096]{1,0:T(8,128)(2,1)} custom-call(s32[65]{0:T(128)} %get-tuple-element.39.table_ref.refs_0_, bf16[2,272,512]{2,1,0:T(8,128)(2,1)} %collective-permute-done.6.refs_0_.refs_2_.refs_1_, bf16[2,272,512]{2,1,0:T(8,128)(2,1)} %copy-done, ...), custom_call_target="tpu_custom_call", output_to_operand_aliasing={{}: (4, {})} | custom-call | flops 1024 | bytes 1024 | tf_op jit(solution)/shard_map/place/pallas_call | solution.py:431
  229.3 3.0 %place.14.refs_3_ = bf16[1024,4096]{1,0:T(8,128)(2,1)} custom-call(s32[65]{0:T(128)} %get-tuple-element.39.table_ref.refs_0_, bf16[2,272,512]{2,1,0:T(8,128)(2,1)} %collective-permute-done.7.refs_1_.refs_0_.refs_2_, bf16[2,272,512]{2,1,0:T(8,128)(2,1)} %copy-done.1, ...), custom_call_target="tpu_custom_call", output_to_operand_aliasing={{}: (4, {})} | custom-call | flops 1024 | bytes 1024 | tf_op jit(solution)/shard_map/place/pallas_call | solution.py:431
  235.2 3.0 %place.15 = bf16[1024,4096]{1,0:T(8,128)(2,1)} custom-call(s32[65]{0:T(128)} %get-tuple-element.39.table_ref.refs_0_, bf16[2,272,512]{2,1,0:T(8,128)(2,1)} %copy-done, bf16[2,272,512]{2,1,0:T(8,128)(2,1)} %collective-permute-done.6.refs_0_.refs_2_.refs_1_, bf16[2,256,1024]{2,1,0:T(8,128)(2,1)} %collective-permute-done.8.refs_2_, ...), custom_call_target="tpu_custom_call", output_to_operand_aliasing={{}: (4, {})} | custom-call | flops 1024 | bytes 1024 | tf_op jit(solution)/shard_map/place/pallas_call | solution.py:431
  (34 shorter events, 19.9 us)
Async XLA Ops:
  11.5 16.7 %collective-permute-start = (bf16[4,128,128]{2,1,0:T(8,128)(2,1)}, bf16[4,128,128]{2,1,0:T(8,128)(2,1)S(1)}, u32[]{:S(2)}, u32[]{:S(2)}) collective-permute-start(bf16[4,128,128]{2,1,0:T(8,128)(2,1)} %get-tuple-element.44), channel_id=1, source_target_pairs={{0,2},{2,4},{4,6},{1,3},{3,5},{5,7},{8,10},{10,12},{12,14},{9,11},... | collective-permute-start | bytes 393224 | tf_op jit(solution)/shard_map/ppermute | solution.py:473
  14.7 15.5 %collective-permute-start.2 = (bf16[12,128,128]{2,1,0:T(8,128)(2,1)}, bf16[12,128,128]{2,1,0:T(8,128)(2,1)S(1)}, u32[]{:S(2)}, u32[]{:S(2)}) collective-permute-start(bf16[12,128,128]{2,1,0:T(8,128)(2,1)} %get-tuple-element.48), channel_id=1, source_target_pairs={{0,2},{2,4},{4,6},{1,3},{3,5},{5,7},{8,10},{10,12},{12,14},{9,11},... | collective-permute-start | bytes 1179656 | tf_op jit(solution)/shard_map/ppermute | solution.py:473
  17.9 10.0 %copy-start.6 = (f32[16,128]{1,0:T(8,128)S(1)}, f32[16,128]{1,0:T(8,128)}, u32[]{:S(2)}) copy-start(f32[16,128]{1,0:T(8,128)} %get-tuple-element.43) | copy-start | bytes 24580
  17.9 10.3 %copy-start.4 = (f32[4,128,128]{2,1,0:T(8,128)S(1)}, f32[4,128,128]{2,1,0:T(8,128)}, u32[]{:S(2)}) copy-start(f32[4,128,128]{2,1,0:T(8,128)} %get-tuple-element.45) | copy-start | bytes 786436
  17.9 12.3 %copy-start.3 = (f32[12,128,128]{2,1,0:T(8,128)S(1)}, f32[12,128,128]{2,1,0:T(8,128)}, u32[]{:S(2)}) copy-start(f32[12,128,128]{2,1,0:T(8,128)} %get-tuple-element.49) | copy-start | bytes 2359300
  28.3 5.7 %collective-permute-start.1 = (bf16[4,128,128]{2,1,0:T(8,128)(2,1)S(1)}, bf16[4,128,128]{2,1,0:T(8,128)(2,1)S(1)}, u32[]{:S(2)}, u32[]{:S(2)}) collective-permute-start(bf16[4,128,128]{2,1,0:T(8,128)(2,1)S(1)} %add_convert_fusion.1), channel_id=1, source_target_pairs={{0,2},{2,4},{4,6},{1,3},{3,5},{5,7},{8,10},{10,12},{12,14},{9,11},... | collective-permute-start | bytes 393224 | tf_op jit(solution)/shard_map/ppermute | solution.py:479
  34.0 1.9 copy-start.5
  34.0 11.0 %collective-permute-start.3 = (bf16[12,128,128]{2,1,0:T(8,128)(2,1)S(1)}, bf16[12,128,128]{2,1,0:T(8,128)(2,1)S(1)}, u32[]{:S(2)}, u32[]{:S(2)}) collective-permute-start(bf16[12,128,128]{2,1,0:T(8,128)(2,1)S(1)} %add_convert_fusion), channel_id=1, source_target_pairs={{0,2},{2,4},{4,6},{1,3},{3,5},{5,7},{8,10},{10,12},{12,14},{9,11},... | collective-permute-start | bytes 1179656 | tf_op jit(solution)/shard_map/ppermute | solution.py:481
  45.0 5.1 %copy-start.2 = (bf16[12,128,128]{2,1,0:T(8,128)(2,1)}, bf16[12,128,128]{2,1,0:T(8,128)(2,1)S(1)}, u32[]{:S(2)}) copy-start(bf16[12,128,128]{2,1,0:T(8,128)(2,1)S(1)} %collective-permute-done.3.refs_9_) | copy-start | bytes 1179652
  45.0 121.0 %all-to-all-start = ((bf16[8,256,512]{2,1,0:T(8,128)(2,1)}), bf16[8,256,512]{2,1,0:T(8,128)(2,1)S(1)}, u32[]{:S(2)}, u32[]{:S(2)}) async-start(bf16[8,256,512]{2,1,0:T(8,128)(2,1)} %get-tuple-element.72), calls=%async_computation | async-start | bytes 4194304 | tf_op jit(solution)/shard_map/all_to_all | solution.py:493
  79.5 60.1 %collective-permute-start.4 = (bf16[2,272,512]{2,1,0:T(8,128)(2,1)}, bf16[2,272,512]{2,1,0:T(8,128)(2,1)S(1)}, u32[]{:S(2)}, u32[]{:S(2)}) collective-permute-start(bf16[2,272,512]{2,1,0:T(8,128)(2,1)} %get-tuple-element.57), channel_id=1, source_target_pairs={{0,0},{1,4},{2,2},{3,6},{4,5},{5,1},{6,7},{7,3},{8,8},{9,12},{10,1... | collective-permute-start | bytes 1671176 | tf_op jit(solution)/shard_map/ppermute | solution.py:495
  86.4 65.2 %collective-permute-start.5 = (bf16[2,272,512]{2,1,0:T(8,128)(2,1)}, bf16[2,272,512]{2,1,0:T(8,128)(2,1)S(1)}, u32[]{:S(2)}, u32[]{:S(2)}) collective-permute-start(bf16[2,272,512]{2,1,0:T(8,128)(2,1)} %get-tuple-element.59), channel_id=1, source_target_pairs={{0,6},{1,2},{2,0},{3,4},{4,3},{5,7},{6,5},{7,1},{8,14},{9,10},{10,... | collective-permute-start | bytes 1671176 | tf_op jit(solution)/shard_map/ppermute | solution.py:495
  86.4 69.0 %collective-permute-start.6 = (bf16[2,272,512]{2,1,0:T(8,128)(2,1)}, bf16[2,272,512]{2,1,0:T(8,128)(2,1)}, u32[]{:S(2)}, u32[]{:S(2)}) collective-permute-start(bf16[2,272,512]{2,1,0:T(8,128)(2,1)} %get-tuple-element.62), channel_id=1, source_target_pairs={{0,2},{1,6},{2,4},{3,0},{4,7},{5,3},{6,1},{7,5},{8,10},{9,14},{10,... | collective-permute-start | bytes 1671176 | tf_op jit(solution)/shard_map/ppermute | solution.py:495
  87.9 67.5 %collective-permute-start.7 = (bf16[2,272,512]{2,1,0:T(8,128)(2,1)}, bf16[2,272,512]{2,1,0:T(8,128)(2,1)}, u32[]{:S(2)}, u32[]{:S(2)}) collective-permute-start(bf16[2,272,512]{2,1,0:T(8,128)(2,1)} %get-tuple-element.65), channel_id=1, source_target_pairs={{0,4},{1,0},{2,6},{3,2},{4,1},{5,5},{6,3},{7,7},{8,12},{9,8},{10,1... | collective-permute-start | bytes 1671176 | tf_op jit(solution)/shard_map/ppermute | solution.py:495
  90.5 95.9 %collective-permute-start.11 = (bf16[2,256,1024]{2,1,0:T(8,128)(2,1)}, bf16[2,256,1024]{2,1,0:T(8,128)(2,1)}, u32[]{:S(2)}, u32[]{:S(2)}) collective-permute-start(bf16[2,256,1024]{2,1,0:T(8,128)(2,1)} %get-tuple-element.71), channel_id=1, source_target_pairs={{0,0},{1,4},{2,2},{3,6},{4,5},{5,1},{6,7},{7,3},{8,8},{9,12},{10,1... | collective-permute-start | bytes 3145736 | tf_op jit(solution)/shard_map/ppermute | solution.py:501
  139.7 11.9 %copy-start.1 = (bf16[2,272,512]{2,1,0:T(8,128)(2,1)}, bf16[2,272,512]{2,1,0:T(8,128)(2,1)S(1)}, u32[]{:S(2)}) copy-start(bf16[2,272,512]{2,1,0:T(8,128)(2,1)S(1)} %collective-permute-done.4.refs_0_.refs_2_.refs_1_) | copy-start | bytes 1671172
  151.6 23.3 %copy-start = (bf16[2,272,512]{2,1,0:T(8,128)(2,1)}, bf16[2,272,512]{2,1,0:T(8,128)(2,1)S(1)}, u32[]{:S(2)}) copy-start(bf16[2,272,512]{2,1,0:T(8,128)(2,1)S(1)} %collective-permute-done.5.refs_1_.refs_0_.refs_2_) | copy-start | bytes 1671172
  155.4 71.0 %collective-permute-start.10 = (bf16[2,256,1024]{2,1,0:T(8,128)(2,1)}, bf16[2,256,1024]{2,1,0:T(8,128)(2,1)}, u32[]{:S(2)}, u32[]{:S(2)}) collective-permute-start(bf16[2,256,1024]{2,1,0:T(8,128)(2,1)} %get-tuple-element.70), channel_id=1, source_target_pairs={{0,2},{1,6},{2,4},{3,0},{4,7},{5,3},{6,1},{7,5},{8,10},{9,14},{10,... | collective-permute-start | bytes 3145736 | tf_op jit(solution)/shard_map/ppermute | solution.py:501
  155.4 73.9 %collective-permute-start.9 = (bf16[2,256,1024]{2,1,0:T(8,128)(2,1)}, bf16[2,256,1024]{2,1,0:T(8,128)(2,1)}, u32[]{:S(2)}, u32[]{:S(2)}) collective-permute-start(bf16[2,256,1024]{2,1,0:T(8,128)(2,1)} %get-tuple-element.69), channel_id=1, source_target_pairs={{0,4},{1,0},{2,6},{3,2},{4,1},{5,5},{6,3},{7,7},{8,12},{9,8},{10,1... | collective-permute-start | bytes 3145736 | tf_op jit(solution)/shard_map/ppermute | solution.py:501
  160.3 74.9 %collective-permute-start.8 = (bf16[2,256,1024]{2,1,0:T(8,128)(2,1)}, bf16[2,256,1024]{2,1,0:T(8,128)(2,1)}, u32[]{:S(2)}, u32[]{:S(2)}) collective-permute-start(bf16[2,256,1024]{2,1,0:T(8,128)(2,1)} %get-tuple-element.66), channel_id=1, source_target_pairs={{0,6},{1,2},{2,0},{3,4},{4,3},{5,7},{6,5},{7,1},{8,14},{9,10},{10,... | collective-permute-start | bytes 3145736 | tf_op jit(solution)/shard_map/ppermute | solution.py:501

commit v4 on v3

--- a/solution.py
+++ b/solution.py
@@ -16,6 +16,10 @@
 
 def params(limit=VMEM_LIMIT):
     return pltpu.CompilerParams(vmem_limit_bytes=limit)
+
+
+def in_hbm(array):
+    return pltpu.with_memory_space_constraint(array, pltpu.HBM)
 
 
 def whole(shape):
@@ -179,9 +183,9 @@
             pltpu.VMEM((128, tokens), F32),
             pltpu.VMEM((heads, 128, 128), F32),
         ],
-        compiler_params=params(),
+        compiler_params=params(24 * 2**20),
         name="prelude",
-    )(doc_lengths, block_shard, decay, key, value)
+    )(doc_lengths, block_shard, decay, in_hbm(key), in_hbm(value))
 
 
 def barred_pairs(hp, cols_ref, docs_ref):
@@ -215,7 +219,10 @@
     return square + attended * attended
 
 
-def own_kernel(lo, hp, count, query_ref, key_ref, value_ref, rows_ref, cols_ref, docs_ref, own_ref, state):
+def own_kernel(lo, hp, count, *refs):
+    (_, query_ref, key_ref, value_ref, gate_ref, gain_ref, rows_ref, cols_ref, docs_ref) = refs[:9]
+    own_ref, same_ref, factor_ref, state = refs[9:]
+
     @pl.when(pl.program_id(0) == 0)
     def _():
         state[...] = jnp.zeros_like(state)
@@ -225,78 +232,75 @@
         own_ref[:, h * 128 : (h + 1) * 128] = chunk_of_head(
             h, lo + h, hp, barred, query_ref, key_ref, value_ref, rows_ref, cols_ref, state
         )
-
-
-def attend_own(query, key, value, rows, cols, docs, lo, count):
-    tokens = query.shape[0]
+    same_ref[...] = query_ref[...]
+    factor_ref[...] = gain_ref[0:1, :] * jax.nn.sigmoid(gate_ref[...].astype(F32))
+
+
+def attend_own(tab, table, query, key, value, gate, gain, rows, cols, docs, lo, count):
+    tokens, local_width = query.shape
     hp = rows.shape[0] // 3
     width = count * 128
     at = lo * 128 // width
-    wide = pl.BlockSpec((BLK, width), lambda c: (c, at))
+    wide = pl.BlockSpec((BLK, width), lambda c, tbl: (c, at))
+    narrow = pl.BlockSpec((BLK, width), lambda c, tbl: (c, 0))
     return pl.pallas_call(
         functools.partial(own_kernel, lo, hp, count),
-        grid=(tokens // BLK,),
-        in_specs=[
-            wide,
-            wide,
-            wide,
-            pl.BlockSpec((rows.shape[0], BLK), lambda c: (0, c)),
-            pl.BlockSpec((BLK, 128), lambda c: (c, 0)),
-            pl.BlockSpec((8, BLK), lambda c: (0, c)),
-        ],
-        out_specs=pl.BlockSpec((BLK, width), lambda c: (c, 0)),
-        out_shape=jax.ShapeDtypeStruct((tokens, width), F32),
-        scratch_shapes=[pltpu.VMEM((count, 128, 128), F32)],
-        compiler_params=params(),
+        grid_spec=pltpu.PrefetchScalarGridSpec(
+            num_scalar_prefetch=1,
+            grid=(tokens // BLK,),
+            in_specs=[
+                wide,
+                wide,
+                wide,
+                wide,
+                pl.BlockSpec((1, width), lambda c, tbl: (0, tbl[tab.half] * (local_width // width) + at)),
+                pl.BlockSpec((rows.shape[0], BLK), lambda c, tbl: (0, c)),
+                pl.BlockSpec((BLK, 128), lambda c, tbl: (c, 0)),
+                pl.BlockSpec((8, BLK), lambda c, tbl: (0, c)),
+            ],
+            out_specs=[narrow] * 3,
+            scratch_shapes=[pltpu.VMEM((count, 128, 128), F32)],
+        ),
+        out_shape=[jax.ShapeDtypeStruct((tokens, width), kind) for kind in (F32, BF16, F32)],
+        compiler_params=params(24 * 2**20),
         cost_estimate=pl.CostEstimate(
             flops=8 * tokens * width * BLK, bytes_accessed=10 * tokens * width, transcendentals=0
         ),
         name="attend_own",
-    )(query, key, value, rows, cols, docs)
-
-
-def enter_kernel(tab, lo, hp, count, table_ref, query_ref, own_ref, gate_ref, gain_ref, cols_ref, state_ref, out_ref, square_ref):
-    square = jnp.zeros((BLK, 128), F32)
-    for h in range(count):
-        cols = slice(h * 128, (h + 1) * 128)
-        reached = jnp.dot(query_ref[:, cols], state_ref[h], preferred_element_type=F32)
-        column = 2 * hp + 8 + lo + h
-        attended = own_ref[:, cols] + cols_ref[:, column : column + 1] * reached
-        square = gate_head(h, attended, square, gain_ref, gate_ref, out_ref.at[0])
-    square_ref[0] = jnp.sum(square.T, axis=0, keepdims=True)
-
-
-def attend_entered(tab, table, query, own, gate, gain, cols, entering, lo, count, hp):
-    tokens, local_width = query.shape
+    )(table, *map(in_hbm, (query, key, value, gate)), gain, rows, cols, docs)
+
+
+def enter_kernel(tab, lo, hp, count, table_ref, own_ref, query_ref, factor_ref, cols_ref, state_ref, out_ref, square_ref):
+    for c in range(tab.chunks):
+        span = slice(c * BLK, (c + 1) * BLK)
+        place, slot = table_ref[tab.shard + c], table_ref[tab.slot + c]
+        square = jnp.zeros((BLK, 128), F32)
+        for h in range(count):
+            cols = slice(h * 128, (h + 1) * 128)
+            reached = jnp.dot(query_ref[span, cols], state_ref[h], preferred_element_type=F32)
+            column = 2 * hp + 8 + lo + h
+            attended = own_ref[span, cols] + cols_ref[span, column : column + 1] * reached
+            attended = attended.astype(BF16).astype(F32)
+            out_ref[place, :, cols] = (attended * factor_ref[span, cols]).astype(BF16)
+            square = square + attended * attended
+        square_ref[slot] = jnp.sum(square.T, axis=0, keepdims=True)
+
+
+def attend_entered(tab, table, own, cols, entering, lo, count, hp):
     width = count * 128
-    at = lo * 128 // width
-    wide = pl.BlockSpec((BLK, width), lambda c, tbl: (c, at))
+    vmem = pl.BlockSpec(memory_space=pltpu.VMEM)
     return pl.pallas_call(
         functools.partial(enter_kernel, tab, lo, hp, count),
-        grid_spec=pltpu.PrefetchScalarGridSpec(
-            num_scalar_prefetch=1,
-            grid=(tab.chunks,),
-            in_specs=[
-                wide,
-                pl.BlockSpec((BLK, width), lambda c, tbl: (c, 0)),
-                wide,
-                pl.BlockSpec((1, width), lambda c, tbl: (0, tbl[tab.half] * (local_width // width) + at)),
-                pl.BlockSpec((BLK, 128), lambda c, tbl: (c, 0)),
-                whole((count, 128, 128)),
-            ],
-            out_specs=[
-                pl.BlockSpec((1, BLK, width), lambda c, tbl: (tbl[tab.shard + c], 0, 0)),
-                pl.BlockSpec((1, 1, BLK), lambda c, tbl: (tbl[tab.slot + c], 0, 0)),
-            ],
-        ),
+        in_specs=[pl.BlockSpec(memory_space=pltpu.SMEM)] + [vmem] * 5,
+        out_specs=[vmem] * 2,
         out_shape=[
             jax.ShapeDtypeStruct((tab.chunks, BLK, width), BF16),
             jax.ShapeDtypeStruct((tab.chunks, 1, BLK), F32),
         ],
-        compiler_params=params(),
+        compiler_params=params(24 * 2**20),
         cost_estimate=pl.CostEstimate(flops=width, bytes_accessed=width, transcendentals=0),
         name="attend_entered",
-    )(table, query, own, gate, gain, cols, entering)
+    )(table, *own, cols, entering)
 
 
 def attend_kernel(tab, lo, hp, count, last, *refs):
@@ -384,7 +388,7 @@
         out_shape=[jax.ShapeDtypeStruct((chunks // ops, height, width), BF16)] * ops
         + [jax.ShapeDtypeStruct((chunks, 1, BLK), F32)] * (not last),
         compiler_params=params(),
-        cost_estimate=pl.CostEstimate(flops=width, bytes_accessed=width, transcendentals=0),
+        cost_estimate=pl.CostEstimate(flops=16 * tokens * width * BLK, bytes_accessed=10 * tokens * width, transcendentals=tokens * width),
         name="attend",
     )(table, query, key, value, gate, gain, rows, cols, docs, entering, squares)
     return out[:ops], None if last else out[ops]
@@ -453,7 +457,7 @@
     quarter = max(1, heads // 4)
 
     rest = heads - quarter
-    splits = ((rest, quarter), (0, rest))
+    splits = ((0, heads),)
     (rows, cols, docs, total_gate, table, *states) = prelude(
         tab, splits, doc_lengths, block_shard, decay_log, key_rows, value_rows
     )
@@ -467,22 +471,25 @@
             for k in range(t)
         ]
 
-    def relay(lo, count, low, full):
-        carry = total_gate[lo : lo + count, :1, None]
-        for _ in range(max(1, n // 2) - 1):
-            low = (carry * lax.ppermute(low, "ctx", hop).astype(F32) + full).astype(BF16)
-        return low
-
-    early, later = (relay(*split, low, full) for split, low, full in zip(splits, states[:2], states[2:]))
-    own = attend_own(query_rows, key_rows, value_rows, rows, cols, docs, rest, quarter)
-    early, own = lax.optimization_barrier((early, own))
-    early = lax.ppermute(early, "ctx", hop)
-    early, later = lax.optimization_barrier((early, later))
-    entering = lax.ppermute(later, "ctx", hop)
-    ready, squares = attend_entered(
-        tab, table, query_rows, own, gate_rows, gain, cols, early, rest, quarter, rows.shape[0] // 3
+    low, full = states
+    carry = total_gate[:, :1, None]
+
+    def merge(arrived, part):
+        return (carry[part] * arrived[part].astype(F32) + full[part]).astype(BF16)
+
+    first, others = slice(rest, heads), slice(0, rest)
+    for _ in range(max(1, n // 2) - 2):
+        low = merge(lax.ppermute(low, "ctx", hop), slice(0, heads))
+    parts = [low[first], low[others]]
+    if n // 2 > 1:
+        arrived = lax.ppermute(low, "ctx", hop)
+        parts = [merge(arrived, first), merge(arrived, others)]
+    own = attend_own(
+        tab, table, query_rows, key_rows, value_rows, gate_rows, gain, rows, cols, docs, rest, quarter
     )
-    ready, entering = lax.optimization_barrier((ready, entering))
+    parts, own = lax.optimization_barrier((parts, own))
+    early, entering = (lax.ppermute(part, "ctx", hop) for part in parts)
+    ready, squares = attend_entered(tab, table, own, cols, early, rest, quarter, rows.shape[0] // 3)
     gated = [None]
     for lo, count in ((0, 2 * quarter), (2 * quarter, quarter)):
         outs, squares = attend(

time: 242 us -> 235 us (0.971)
  Pallas kernels: 83.6 us -> 77.3 us
  waiting for transfers between devices: 107 us -> 101 us
  local copies, waits for them, and re-layouts: 0.26 us -> 3.8 us
    pallas_call x2, Pallas kernels: 19 us -> 13.8 us  [the longest x1 9.44 us: attend_own(): pl.pallas_call(functools.partial(own_kernel, lo, hp, count), grid_spec=pl...]
    unnamed x14 -> x24, local copies, waits for them, and re-layouts: 0.03 us -> 3.58 us
    ppermute x4, waiting for transfers between devices: 61 us -> 58.5 us  [local(): lax.ppermute(gated[2][op], ('ctx', 'tp'), route(op))]
    ppermute x4 -> x3, starting transfers between devices: 10.2 us -> 9.62 us  [the longest x2 6.41 us: local(): early, entering = (lax.ppermute(part, 'ctx', hop) for part in parts)]
  transfers between devices with their start and end apart: 13 -> 12, of which waited for: 7 -> 6; matrix products, arithmetic and copies ran while one was open for 0% -> 0% of each run, Pallas kernels for 29% -> 28%
where the time goes in v4:
time: 235 us; the launch traced here: 231 us
  waiting for transfers between devices  101 us (43%)
  Pallas kernels  77.3 us (33%)
  starting transfers between devices  42.5 us (18%)
  blocking collectives  5.92 us (3%)
  local copies, waits for them, and re-layouts  3.8 us (2%)
    ppermute x4, waiting for transfers between devices, local(): lax.ppermute(gated[2][op], ('ctx', 'tp'), route(op))  58.5 us
    ppermute x4, waiting for transfers between devices, local(): middle.append(lax.ppermute(ready, ('ctx', 'tp'), route(op)))  40.7 us
    pallas_call x2, Pallas kernels, attend(): pl.pallas_call(functools.partial(attend_kernel, tab, lo, hp, count, last)...  29.5 us
    pallas_call x8, Pallas kernels, place(): pl.pallas_call(functools.partial(place_kernel, features, tab.t, len(piece...  23.6 us
    ppermute x4, starting transfers between devices, local(): middle.append(lax.ppermute(ready, ('ctx', 'tp'), route(op)))  16.3 us
    ppermute x4, starting transfers between devices, local(): lax.ppermute(gated[2][op], ('ctx', 'tp'), route(op))  12.6 us
    pallas_call x1, Pallas kernels, prelude(): pl.pallas_call(functools.partial(prelude_kernel, tab, splits), grid=(toke...  10.4 us
    pallas_call x1, Pallas kernels, attend_own(): pl.pallas_call(functools.partial(own_kernel, lo, hp, count), grid_spec=pl...  9.44 us
  transfers between devices with their start and end apart: 12, of which 6 were waited for; matrix products, arithmetic and copies ran while one was open for 0% of the time, Pallas kernels for 28%

profile of v4, /device:TPU:9, one launch (start us, length us, event | category | flops | bytes accessed | tf_op | source)
XLA Modules:
  0.0 231.1 jit_solution(6676833125678472693)
XLA Ops:
  2.2 10.4 %prelude.1 = (f32[48,2048]{1,0:T(8,128)S(1)}, f32[2048,128]{1,0:T(8,128)S(1)}, f32[8,2048]{1,0:T(8,128)S(1)}, f32[16,128]{1,0:T(8,128)S(1)}, s32[65]{0:T(128)S(1...) custom-call(s32[16]{0:T(128)S(1)} %copy-done.7, s32[32]{0:T(128)S(1)} %copy-done.8, ...), custom_call_target="tpu_custom_call" | custom-call | tf_op jit(solution)/shard_map/prelude/pallas_call | solution.py:172
  12.7 3.2 %collective-permute-start = (bf16[16,128,128]{2,1,0:T(8,128)(2,1)S(1)}, bf16[16,128,128]{2,1,0:T(8,128)(2,1)S(1)}, u32[]{:S(2)}, u32[]{:S(2)}) collective-permute-start(bf16[16,128,128]{2,1,0:T(8,128)(2,1)S(1)} %get-tuple-element.44), channel_id=1, source_target_pairs={{0,2},{2,4},{4,6},{1,3},{3,5},{5,7},{8,10},{10,12},{12,14},{9,11},... | collective-permute-start | bytes 1572872 | tf_op jit(solution)/shard_map/ppermute | solution.py:485
  16.1 9.4 %attend_own.1 = (f32[2048,512]{1,0:T(8,128)S(1)}, bf16[2048,512]{1,0:T(8,128)(2,1)S(1)}, f32[2048,512]{1,0:T(8,128)S(1)}) custom-call(s32[65]{0:T(128)S(1)} %get-tuple-element.39.refs_0_.table_ref, bf16[2048,2048]{1,0:T(8,128)(2,1)} %refs_1_.5, bf16[2048,2048]{1,0:T(8,128)(2,1)} %refs_2_.5, bf16[2048,2048]{1,0:T(8,128)(2,1)} %refs_3_.5, ...), custom_call_target="tpu_custom_call" | custom-call | flops 2147483648 | bytes 10485760 | tf_op jit(solution)/shard_map/attend_own/pallas_call | solution.py:246
  27.6 3.2 %collective-permute-start.2 = (bf16[4,128,128]{2,1,0:T(8,128)(2,1)S(1)}, bf16[4,128,128]{2,1,0:T(8,128)(2,1)S(1)}, u32[]{:S(2)}, u32[]{:S(2)}) collective-permute-start(bf16[4,128,128]{2,1,0:T(8,128)(2,1)S(1)} %add_convert_fusion.1), channel_id=1, source_target_pairs={{0,2},{2,4},{4,6},{1,3},{3,5},{5,7},{8,10},{10,12},{12,14},{9,11},... | collective-permute-start | bytes 393224 | tf_op jit(solution)/shard_map/ppermute | solution.py:491
  30.8 3.2 %collective-permute-start.1 = (bf16[12,128,128]{2,1,0:T(8,128)(2,1)S(1)}, bf16[12,128,128]{2,1,0:T(8,128)(2,1)S(1)}, u32[]{:S(2)}, u32[]{:S(2)}) collective-permute-start(bf16[12,128,128]{2,1,0:T(8,128)(2,1)S(1)} %add_convert_fusion), channel_id=1, source_target_pairs={{0,2},{2,4},{4,6},{1,3},{3,5},{5,7},{8,10},{10,12},{12,14},{9,11},... | collective-permute-start | bytes 1179656 | tf_op jit(solution)/shard_map/ppermute | solution.py:491
  34.1 4.3 %attend_entered.1 = (bf16[8,256,512]{2,1,0:T(8,128)(2,1)}, f32[8,1,256]{2,1,0:T(1,128)S(1)}) custom-call(s32[65]{0:T(128)S(1)} %get-tuple-element.39.refs_0_.table_ref, f32[2048,512]{1,0:T(8,128)S(1)} %get-tuple-element.50.own_ref, bf16[2048,512]{1,0:T(8,128)(2,1)S(1)} %get-tuple-element.51.query_ref, f32[2048,512]{1,0:T(8,128)S(1)} %get-tuple-element.52.factor_ref, ...), custom_call_target="tpu_custom_call" | custom-call | flops 512 | bytes 512 | tf_op jit(solution)/shard_map/attend_entered/pallas_call | solution.py:292
  39.0 4.0 %all-to-all-start = ((bf16[8,256,512]{2,1,0:T(8,128)(2,1)}), bf16[8,256,512]{2,1,0:T(8,128)(2,1)S(1)}, u32[]{:S(2)}, u32[]{:S(2)}) async-start(bf16[8,256,512]{2,1,0:T(8,128)(2,1)} %get-tuple-element.72), calls=%async_computation | async-start | bytes 4194304 | tf_op jit(solution)/shard_map/all_to_all | solution.py:500
  43.8 17.4 %attend.2 = (bf16[2,256,1024]{2,1,0:T(8,128)(2,1)}, bf16[2,256,1024]{2,1,0:T(8,128)(2,1)}, bf16[2,256,1024]{2,1,0:T(8,128)(2,1)}, bf16[2,256,1024]{2,1,0:T(8,128)(2,1)}, f32[8,1,256]{2,1,0:T(1,128)}) custom-call(s32[65]{0:T(128)} %copy-done.5, bf16[2048,2048]{1,0:T(8,128)(2,1)} %refs_1_.5, bf16[2048,2048]{1,0:T(8,128)(2,1)} %refs_2_.5, ...), custom_call_target="tpu_custom_call" | custom-call | flops 8589934592 | bytes 20971520 | tf_op jit(solution)/shard_map/attend/pallas_call | solution.py:362
  61.2 12.1 %attend.3 = (bf16[2,272,512]{2,1,0:T(8,128)(2,1)}, bf16[2,272,512]{2,1,0:T(8,128)(2,1)}, bf16[2,272,512]{2,1,0:T(8,128)(2,1)}, bf16[2,272,512]{2,1,0:T(8,128)(2,1)}) custom-call(s32[65]{0:T(128)} %copy-done.5, bf16[2048,2048]{1,0:T(8,128)(2,1)} %refs_1_.5, bf16[2048,2048]{1,0:T(8,128)(2,1)} %refs_2_.5, bf16[2048,2048]{1,0:T(8,128)(2,1)} %refs_3_.5, ...), custom_call_target="tpu_custom_call" | custom-call | flops 4294967296 | bytes 10485760 | tf_op jit(solution)/shard_map/attend/pallas_call | solution.py:362
  73.3 8.5 %collective-permute-start.3 = (bf16[2,272,512]{2,1,0:T(8,128)(2,1)}, bf16[2,272,512]{2,1,0:T(8,128)(2,1)S(1)}, u32[]{:S(2)}, u32[]{:S(2)}) collective-permute-start(bf16[2,272,512]{2,1,0:T(8,128)(2,1)} %get-tuple-element.57), channel_id=1, source_target_pairs={{0,0},{1,4},{2,2},{3,6},{4,5},{5,1},{6,7},{7,3},{8,8},{9,12},{10,1... | collective-permute-start | bytes 1671176 | tf_op jit(solution)/shard_map/ppermute | solution.py:502
  85.9 3.9 %collective-permute-start.10 = (bf16[2,256,1024]{2,1,0:T(8,128)(2,1)}, bf16[2,256,1024]{2,1,0:T(8,128)(2,1)}, u32[]{:S(2)}, u32[]{:S(2)}) collective-permute-start(bf16[2,256,1024]{2,1,0:T(8,128)(2,1)} %get-tuple-element.71), channel_id=1, source_target_pairs={{0,0},{1,4},{2,2},{3,6},{4,5},{5,1},{6,7},{7,3},{8,8},{9,12},{10,1... | collective-permute-start | bytes 3145736 | tf_op jit(solution)/shard_map/ppermute | solution.py:508
  89.8 41.1 %collective-permute-done.3.refs_0_.refs_2_.refs_1_ = bf16[2,272,512]{2,1,0:T(8,128)(2,1)S(1)} collective-permute-done((bf16[2,272,512]{2,1,0:T(8,128)(2,1)}, bf16[2,272,512]{2,1,0:T(8,128)(2,1)S(1)}, u32[]{:S(2)}, u32[]{:S(2)}) %collective-permute-start.3) | collective-permute-done | bytes 557088 | tf_op jit(solution)/shard_map/ppermute | solution.py:502
  131.0 11.9 %collective-permute-done.4.refs_1_.refs_0_.refs_2_ = bf16[2,272,512]{2,1,0:T(8,128)(2,1)S(1)} collective-permute-done((bf16[2,272,512]{2,1,0:T(8,128)(2,1)}, bf16[2,272,512]{2,1,0:T(8,128)(2,1)S(1)}, u32[]{:S(2)}, u32[]{:S(2)}) %collective-permute-start.4) | collective-permute-done | bytes 557088 | tf_op jit(solution)/shard_map/ppermute | solution.py:502
  142.9 5.5 %collective-permute-done.5.refs_0_.refs_2_.refs_1_ = bf16[2,272,512]{2,1,0:T(8,128)(2,1)} collective-permute-done((bf16[2,272,512]{2,1,0:T(8,128)(2,1)}, bf16[2,272,512]{2,1,0:T(8,128)(2,1)}, u32[]{:S(2)}, u32[]{:S(2)}) %collective-permute-start.5) | collective-permute-done | bytes 557088 | tf_op jit(solution)/shard_map/ppermute | solution.py:502
  148.4 6.7 %collective-permute-start.8 = (bf16[2,256,1024]{2,1,0:T(8,128)(2,1)}, bf16[2,256,1024]{2,1,0:T(8,128)(2,1)}, u32[]{:S(2)}, u32[]{:S(2)}) collective-permute-start(bf16[2,256,1024]{2,1,0:T(8,128)(2,1)} %get-tuple-element.69), channel_id=1, source_target_pairs={{0,4},{1,0},{2,6},{3,2},{4,1},{5,5},{6,3},{7,7},{8,12},{9,8},{10,1... | collective-permute-start | bytes 3145736 | tf_op jit(solution)/shard_map/ppermute | solution.py:508
  155.1 5.7 %collective-permute-start.7 = (bf16[2,256,1024]{2,1,0:T(8,128)(2,1)}, bf16[2,256,1024]{2,1,0:T(8,128)(2,1)}, u32[]{:S(2)}, u32[]{:S(2)}) collective-permute-start(bf16[2,256,1024]{2,1,0:T(8,128)(2,1)} %get-tuple-element.66), channel_id=1, source_target_pairs={{0,6},{1,2},{2,0},{3,4},{4,3},{5,7},{6,5},{7,1},{8,14},{9,10},{10,... | collective-permute-start | bytes 3145736 | tf_op jit(solution)/shard_map/ppermute | solution.py:508
  160.8 5.9 %all_to_all.10.refs_3_ = bf16[8,256,512]{2,1,0:T(8,128)(2,1)} all-to-all(bf16[8,256,512]{2,1,0:T(8,128)(2,1)S(1)} %all-to-all-done), channel_id=1, replica_groups=mesh['dp'=4,'ctx'=4,'tp'=2] {'tp'}, dimensions={0} | all-to-all | bytes 4194304 | tf_op jit(solution)/shard_map/all_to_all | solution.py:501
  169.7 3.0 %place.9.refs_4_ = bf16[1024,4096]{1,0:T(8,128)(2,1)} custom-call(s32[65]{0:T(128)} %copy-done.5, bf16[2,272,512]{2,1,0:T(8,128)(2,1)} %collective-permute-done.5.refs_0_.refs_2_.refs_1_, bf16[2,272,512]{2,1,0:T(8,128)(2,1)} %copy-done.9, bf16[2,272,512]{2,1,0:T(8,128)(2,1)} %collective-permute-done.5.refs_0_.refs_2_.refs_1_, ...), custom_call_target="tpu_custom_call", output_to_operand_aliasing={{}: (5, {})} | custom-call | flops 1024 | bytes 1024 | tf_op jit(solution)/shard_map/place/pallas_call | solution.py:435
  178.5 3.0 %place.12.refs_3_ = bf16[1024,4096]{1,0:T(8,128)(2,1)} custom-call(s32[65]{0:T(128)} %copy-done.5, bf16[2,272,512]{2,1,0:T(8,128)(2,1)} %copy-done.10, bf16[2,272,512]{2,1,0:T(8,128)(2,1)} %collective-permute-done.6.refs_1_.refs_0_.refs_2_, bf16[2,256,1024]{2,1,0:T(8,128)(2,1)} %collective-permute-done.10.refs_2_, ...), custom_call_target="tpu_custom_call", output_to_operand_aliasing={{}: (4, {})} | custom-call | flops 1024 | bytes 1024 | tf_op jit(solution)/shard_map/place/pallas_call | solution.py:435
  181.5 36.0 %collective-permute-done.9.refs_2_ = bf16[2,256,1024]{2,1,0:T(8,128)(2,1)} collective-permute-done((bf16[2,256,1024]{2,1,0:T(8,128)(2,1)}, bf16[2,256,1024]{2,1,0:T(8,128)(2,1)}, u32[]{:S(2)}, u32[]{:S(2)}) %collective-permute-start.9) | collective-permute-done | bytes 1048608 | tf_op jit(solution)/shard_map/ppermute | solution.py:508
  217.5 3.0 %place.13.refs_3_ = bf16[1024,4096]{1,0:T(8,128)(2,1)} custom-call(s32[65]{0:T(128)} %copy-done.5, bf16[2,272,512]{2,1,0:T(8,128)(2,1)} %collective-permute-done.5.refs_0_.refs_2_.refs_1_, bf16[2,272,512]{2,1,0:T(8,128)(2,1)} %copy-done.9, bf16[2,256,1024]{2,1,0:T(8,128)(2,1)} %collective-permute-done.9.refs_2_, ...), custom_call_target="tpu_custom_call", output_to_operand_aliasing={{}: (4, {})} | custom-call | flops 1024 | bytes 1024 | tf_op jit(solution)/shard_map/place/pallas_call | solution.py:435
  220.5 3.0 %place.14.refs_3_ = bf16[1024,4096]{1,0:T(8,128)(2,1)} custom-call(s32[65]{0:T(128)} %copy-done.5, bf16[2,272,512]{2,1,0:T(8,128)(2,1)} %collective-permute-done.6.refs_1_.refs_0_.refs_2_, bf16[2,272,512]{2,1,0:T(8,128)(2,1)} %copy-done.10, bf16[2,256,1024]{2,1,0:T(8,128)(2,1)} %collective-permute-done.8.refs_2_, ...), custom_call_target="tpu_custom_call", output_to_operand_aliasing={{}: (4, {})} | custom-call | flops 1024 | bytes 1024 | tf_op jit(solution)/shard_map/place/pallas_call | solution.py:435
  223.4 4.7 %collective-permute-done.7.refs_2_ = bf16[2,256,1024]{2,1,0:T(8,128)(2,1)} collective-permute-done((bf16[2,256,1024]{2,1,0:T(8,128)(2,1)}, bf16[2,256,1024]{2,1,0:T(8,128)(2,1)}, u32[]{:S(2)}, u32[]{:S(2)}) %collective-permute-start.7) | collective-permute-done | bytes 1048608 | tf_op jit(solution)/shard_map/ppermute | solution.py:508
  228.1 3.0 %place.15 = bf16[1024,4096]{1,0:T(8,128)(2,1)} custom-call(s32[65]{0:T(128)} %copy-done.5, bf16[2,272,512]{2,1,0:T(8,128)(2,1)} %copy-done.9, bf16[2,272,512]{2,1,0:T(8,128)(2,1)} %collective-permute-done.5.refs_0_.refs_2_.refs_1_, bf16[2,256,1024]{2,1,0:T(8,128)(2,1)} %collective-permute-done.7.refs_2_, ...), custom_call_target="tpu_custom_call", output_to_operand_aliasing={{}: (4, {})} | custom-call | flops 1024 | bytes 1024 | tf_op jit(solution)/shard_map/place/pallas_call | solution.py:435
  (42 shorter events, 18.8 us)
Async XLA Ops:
  0.0 0.9 copy-start.4
  0.9 0.7 copy-start.7
  1.6 0.7 copy-start.8
  2.2 13.9 %copy-start.3 = (f32[4096]{0:T(1024)S(1)}, f32[4096]{0:T(1024)}, u32[]{:S(2)}) copy-start(f32[4096]{0:T(1024)} %param.13) | copy-start | bytes 49156
  12.6 12.9 %copy-start.1 = (f32[48,2048]{1,0:T(8,128)}, f32[48,2048]{1,0:T(8,128)S(1)}, u32[]{:S(2)}) copy-start(f32[48,2048]{1,0:T(8,128)S(1)} %get-tuple-element.40.refs_6_) | copy-start | bytes 1179652
  12.6 12.9 %copy-start.2 = (f32[8,2048]{1,0:T(8,128)}, f32[8,2048]{1,0:T(8,128)S(1)}, u32[]{:S(2)}) copy-start(f32[8,2048]{1,0:T(8,128)S(1)} %get-tuple-element.42.refs_8_) | copy-start | bytes 196612
  12.6 21.4 %copy-start = (f32[2048,128]{1,0:T(8,128)}, f32[2048,128]{1,0:T(8,128)S(1)}, u32[]{:S(2)}) copy-start(f32[2048,128]{1,0:T(8,128)S(1)} %get-tuple-element.41.refs_7_.cols_ref) | copy-start | bytes 3145732
  12.6 21.4 %copy-start.5 = (s32[65]{0:T(128)}, s32[65]{0:T(128)S(1)}, u32[]{:S(2)}) copy-start(s32[65]{0:T(128)S(1)} %get-tuple-element.39.refs_0_.table_ref) | copy-start | bytes 784
  12.7 14.7 %collective-permute-start = (bf16[16,128,128]{2,1,0:T(8,128)(2,1)S(1)}, bf16[16,128,128]{2,1,0:T(8,128)(2,1)S(1)}, u32[]{:S(2)}, u32[]{:S(2)}) collective-permute-start(bf16[16,128,128]{2,1,0:T(8,128)(2,1)S(1)} %get-tuple-element.44), channel_id=1, source_target_pairs={{0,2},{2,4},{4,6},{1,3},{3,5},{5,7},{8,10},{10,12},{12,14},{9,11},... | collective-permute-start | bytes 1572872 | tf_op jit(solution)/shard_map/ppermute | solution.py:485
  27.6 6.4 %collective-permute-start.2 = (bf16[4,128,128]{2,1,0:T(8,128)(2,1)S(1)}, bf16[4,128,128]{2,1,0:T(8,128)(2,1)S(1)}, u32[]{:S(2)}, u32[]{:S(2)}) collective-permute-start(bf16[4,128,128]{2,1,0:T(8,128)(2,1)S(1)} %add_convert_fusion.1), channel_id=1, source_target_pairs={{0,2},{2,4},{4,6},{1,3},{3,5},{5,7},{8,10},{10,12},{12,14},{9,11},... | collective-permute-start | bytes 393224 | tf_op jit(solution)/shard_map/ppermute | solution.py:491
  30.8 12.2 %collective-permute-start.1 = (bf16[12,128,128]{2,1,0:T(8,128)(2,1)S(1)}, bf16[12,128,128]{2,1,0:T(8,128)(2,1)S(1)}, u32[]{:S(2)}, u32[]{:S(2)}) collective-permute-start(bf16[12,128,128]{2,1,0:T(8,128)(2,1)S(1)} %add_convert_fusion), channel_id=1, source_target_pairs={{0,2},{2,4},{4,6},{1,3},{3,5},{5,7},{8,10},{10,12},{12,14},{9,11},... | collective-permute-start | bytes 1179656 | tf_op jit(solution)/shard_map/ppermute | solution.py:491
  38.4 0.6 copy-start.6
  39.0 121.8 %all-to-all-start = ((bf16[8,256,512]{2,1,0:T(8,128)(2,1)}), bf16[8,256,512]{2,1,0:T(8,128)(2,1)S(1)}, u32[]{:S(2)}, u32[]{:S(2)}) async-start(bf16[8,256,512]{2,1,0:T(8,128)(2,1)} %get-tuple-element.72), calls=%async_computation | async-start | bytes 4194304 | tf_op jit(solution)/shard_map/all_to_all | solution.py:500
  43.0 0.7 copy-start.11
  73.3 57.7 %collective-permute-start.3 = (bf16[2,272,512]{2,1,0:T(8,128)(2,1)}, bf16[2,272,512]{2,1,0:T(8,128)(2,1)S(1)}, u32[]{:S(2)}, u32[]{:S(2)}) collective-permute-start(bf16[2,272,512]{2,1,0:T(8,128)(2,1)} %get-tuple-element.57), channel_id=1, source_target_pairs={{0,0},{1,4},{2,2},{3,6},{4,5},{5,1},{6,7},{7,3},{8,8},{9,12},{10,1... | collective-permute-start | bytes 1671176 | tf_op jit(solution)/shard_map/ppermute | solution.py:502
  81.8 61.1 %collective-permute-start.4 = (bf16[2,272,512]{2,1,0:T(8,128)(2,1)}, bf16[2,272,512]{2,1,0:T(8,128)(2,1)S(1)}, u32[]{:S(2)}, u32[]{:S(2)}) collective-permute-start(bf16[2,272,512]{2,1,0:T(8,128)(2,1)} %get-tuple-element.59), channel_id=1, source_target_pairs={{0,6},{1,2},{2,0},{3,4},{4,3},{5,7},{6,5},{7,1},{8,14},{9,10},{10,... | collective-permute-start | bytes 1671176 | tf_op jit(solution)/shard_map/ppermute | solution.py:502
  81.9 66.5 %collective-permute-start.5 = (bf16[2,272,512]{2,1,0:T(8,128)(2,1)}, bf16[2,272,512]{2,1,0:T(8,128)(2,1)}, u32[]{:S(2)}, u32[]{:S(2)}) collective-permute-start(bf16[2,272,512]{2,1,0:T(8,128)(2,1)} %get-tuple-element.62), channel_id=1, source_target_pairs={{0,2},{1,6},{2,4},{3,0},{4,7},{5,3},{6,1},{7,5},{8,10},{9,14},{10,... | collective-permute-start | bytes 1671176 | tf_op jit(solution)/shard_map/ppermute | solution.py:502
  83.4 65.0 %collective-permute-start.6 = (bf16[2,272,512]{2,1,0:T(8,128)(2,1)}, bf16[2,272,512]{2,1,0:T(8,128)(2,1)}, u32[]{:S(2)}, u32[]{:S(2)}) collective-permute-start(bf16[2,272,512]{2,1,0:T(8,128)(2,1)} %get-tuple-element.65), channel_id=1, source_target_pairs={{0,4},{1,0},{2,6},{3,2},{4,1},{5,5},{6,3},{7,7},{8,12},{9,8},{10,1... | collective-permute-start | bytes 1671176 | tf_op jit(solution)/shard_map/ppermute | solution.py:502
  85.9 92.6 %collective-permute-start.10 = (bf16[2,256,1024]{2,1,0:T(8,128)(2,1)}, bf16[2,256,1024]{2,1,0:T(8,128)(2,1)}, u32[]{:S(2)}, u32[]{:S(2)}) collective-permute-start(bf16[2,256,1024]{2,1,0:T(8,128)(2,1)} %get-tuple-element.71), channel_id=1, source_target_pairs={{0,0},{1,4},{2,2},{3,6},{4,5},{5,1},{6,7},{7,3},{8,8},{9,12},{10,1... | collective-permute-start | bytes 3145736 | tf_op jit(solution)/shard_map/ppermute | solution.py:508
  131.0 11.9 %copy-start.10 = (bf16[2,272,512]{2,1,0:T(8,128)(2,1)}, bf16[2,272,512]{2,1,0:T(8,128)(2,1)S(1)}, u32[]{:S(2)}) copy-start(bf16[2,272,512]{2,1,0:T(8,128)(2,1)S(1)} %collective-permute-done.3.refs_0_.refs_2_.refs_1_) | copy-start | bytes 1671172
  142.9 26.8 %copy-start.9 = (bf16[2,272,512]{2,1,0:T(8,128)(2,1)}, bf16[2,272,512]{2,1,0:T(8,128)(2,1)S(1)}, u32[]{:S(2)}) copy-start(bf16[2,272,512]{2,1,0:T(8,128)(2,1)S(1)} %collective-permute-done.4.refs_1_.refs_0_.refs_2_) | copy-start | bytes 1671172
  148.4 69.1 %collective-permute-start.9 = (bf16[2,256,1024]{2,1,0:T(8,128)(2,1)}, bf16[2,256,1024]{2,1,0:T(8,128)(2,1)}, u32[]{:S(2)}, u32[]{:S(2)}) collective-permute-start(bf16[2,256,1024]{2,1,0:T(8,128)(2,1)} %get-tuple-element.70), channel_id=1, source_target_pairs={{0,2},{1,6},{2,4},{3,0},{4,7},{5,3},{6,1},{7,5},{8,10},{9,14},{10,... | collective-permute-start | bytes 3145736 | tf_op jit(solution)/shard_map/ppermute | solution.py:508
  148.4 72.1 %collective-permute-start.8 = (bf16[2,256,1024]{2,1,0:T(8,128)(2,1)}, bf16[2,256,1024]{2,1,0:T(8,128)(2,1)}, u32[]{:S(2)}, u32[]{:S(2)}) collective-permute-start(bf16[2,256,1024]{2,1,0:T(8,128)(2,1)} %get-tuple-element.69), channel_id=1, source_target_pairs={{0,4},{1,0},{2,6},{3,2},{4,1},{5,5},{6,3},{7,7},{8,12},{9,8},{10,1... | collective-permute-start | bytes 3145736 | tf_op jit(solution)/shard_map/ppermute | solution.py:508
  155.1 73.1 %collective-permute-start.7 = (bf16[2,256,1024]{2,1,0:T(8,128)(2,1)}, bf16[2,256,1024]{2,1,0:T(8,128)(2,1)}, u32[]{:S(2)}, u32[]{:S(2)}) collective-permute-start(bf16[2,256,1024]{2,1,0:T(8,128)(2,1)} %get-tuple-element.66), channel_id=1, source_target_pairs={{0,6},{1,2},{2,0},{3,4},{4,3},{5,7},{6,5},{7,1},{8,14},{9,10},{10,... | collective-permute-start | bytes 3145736 | tf_op jit(solution)/shard_map/ppermute | solution.py:508

commit v5 on v4

--- a/solution.py
+++ b/solution.py
@@ -73,7 +73,7 @@
         table_ref[tab.side + op] = lax.rem(ctx - op - source + 2 * n, n) // tab.stride
 
 
-def fill_gates(len_ref, decay_ref, rows_ref, cols_ref, docs_ref, total_ref, tail_ref, scr):
+def fill_gates(len_ref, decay_ref, rows_ref, cols_ref, docs_ref, total_ref, tail_ref, scr, stack):
     heads, tokens = decay_ref.shape
     hp = pad8(heads)
     chunks = tokens // BLK
@@ -98,14 +98,19 @@
 
     first = lax.broadcasted_iota(jnp.int32, (BLK, BLK), 0)
     second = lax.broadcasted_iota(jnp.int32, (BLK, BLK), 1)
-    upto = jnp.where(first <= second, 1.0, 0.0).astype(F32)
-    every = jnp.ones((BLK, BLK), F32)
+    upto = jnp.where(first <= second, 1.0, 0.0).astype(BF16)
+    stack[...] = jnp.zeros_like(stack)
+    for c in range(chunks):
+        stack[c * hp : c * hp + heads, :] = decay_ref[:, c * BLK : (c + 1) * BLK]
+    left, terms = stack[...], []
+    for _ in range(3):
+        terms.append(left.astype(BF16))
+        left = left - terms[-1].astype(F32)
+    high, middle, low = (jnp.dot(term, upto, preferred_element_type=F32) for term in terms)
+    stack[...] = high + (middle + low)
     scr[...] = jnp.zeros_like(scr)
-    cums, sums = [], []
-    for c in range(chunks):
-        part = decay_ref[:, c * BLK : (c + 1) * BLK]
-        cums.append(jnp.dot(part, upto, precision=lax.Precision.HIGHEST, preferred_element_type=F32))
-        sums.append(jnp.dot(part, every, precision=lax.Precision.HIGHEST, preferred_element_type=F32))
+    cums = [stack[c * hp : c * hp + heads, :] for c in range(chunks)]
+    sums = [jnp.broadcast_to(cum[:, BLK - 1 :], cum.shape) for cum in cums]
     before, after = [], [None] * chunks
     run = jnp.zeros_like(sums[0])
     for c in range(chunks):
@@ -135,57 +140,57 @@
     total_ref[...] = jnp.where(edges[-1] == edges[0], jnp.exp(run[:, :128]), 0.0)
 
 
-def prelude_kernel(tab, splits, len_ref, shard_ref, decay_ref, key_ref, value_ref, *refs):
-    rows_ref, cols_ref, docs_ref, total_ref, table_ref = refs[:5]
-    lows, fulls = refs[5 : 5 + len(splits)], refs[5 + len(splits) : 5 + 2 * len(splits)]
-    tail_ref, scr, acc = refs[5 + 2 * len(splits) :]
-    step = pl.program_id(0)
-    tile = key_ref.shape[0]
-
-    @pl.when(step == 0)
-    def _():
-        fill_table(tab, shard_ref, table_ref)
-        fill_gates(len_ref, decay_ref, rows_ref, cols_ref, docs_ref, total_ref, tail_ref, scr)
-        acc[...] = jnp.zeros_like(acc)
-
-    tails = tail_ref[:, pl.ds(pl.multiple_of(step * tile, tile), tile)]
-    for h in range(acc.shape[0]):
-        cols = slice(h * 128, (h + 1) * 128)
-        scaled = (key_ref[:, cols].T.astype(F32) * tails[h : h + 1, :]).astype(BF16)
-        acc[h] += jnp.dot(scaled, value_ref[:, cols], preferred_element_type=F32)
-
-    @pl.when(step == pl.num_programs(0) - 1)
-    def _():
-        for (lo, count), low_ref, full_ref in zip(splits, lows, fulls):
-            low_ref[...] = acc[lo : lo + count].astype(BF16)
-            full_ref[...] = acc[lo : lo + count]
-
-
-def prelude(tab, splits, doc_lengths, block_shard, decay, key, value):
+def prelude_kernel(tab, tile, len_ref, shard_ref, decay_ref, key_hbm, value_hbm, *refs):
+    rows_ref, cols_ref, docs_ref, total_ref, table_ref, low_ref, full_ref = refs[:7]
+    tail_ref, scr, stack, key_ref, value_ref, arrived = refs[7:]
+    tokens = key_ref.shape[0]
+    heads = full_ref.shape[0]
+    copies = []
+    for i in range(tokens // tile):
+        span = pl.ds(i * tile, tile)
+        for k, (source, target) in enumerate(((key_hbm, key_ref), (value_hbm, value_ref))):
+            copies.append(pltpu.make_async_copy(source.at[span], target.at[span], arrived.at[k, i]))
+            copies[-1].start()
+    fill_table(tab, shard_ref, table_ref)
+    fill_gates(len_ref, decay_ref, rows_ref, cols_ref, docs_ref, total_ref, tail_ref, scr, stack)
+    for i in range(tokens // tile):
+        copies[2 * i].wait()
+        copies[2 * i + 1].wait()
+        span = slice(i * tile, (i + 1) * tile)
+        for h in range(heads):
+            cols = slice(h * 128, (h + 1) * 128)
+            scaled = (key_ref[span, cols].T.astype(F32) * tail_ref[h : h + 1, span]).astype(BF16)
+            part = jnp.dot(scaled, value_ref[span, cols], preferred_element_type=F32)
+            full_ref[h] = full_ref[h] + part if i else part
+    low_ref[...] = full_ref[...].astype(BF16)
+
+
+def prelude(tab, doc_lengths, block_shard, decay, key, value):
     heads, tokens = decay.shape
     hp = pad8(heads)
     tile = 2 * BLK
     smem = pl.BlockSpec(memory_space=pltpu.SMEM)
+    vmem = pl.BlockSpec(memory_space=pltpu.VMEM)
+    hbm = pl.BlockSpec(memory_space=pl.ANY)
     shapes = [(3 * hp, tokens), (tokens, 128), (8, tokens), (heads, 128)]
-    states = [(count, 128, 128) for _, count in splits]
-    wide = pl.BlockSpec((tile, key.shape[1]), lambda c: (c, 0))
     return pl.pallas_call(
-        functools.partial(prelude_kernel, tab, splits),
-        grid=(tokens // tile,),
-        in_specs=[smem, smem, whole(decay.shape), wide, wide],
-        out_specs=[whole(shape) for shape in shapes] + [smem] + [whole(shape) for shape in states * 2],
+        functools.partial(prelude_kernel, tab, tile),
+        in_specs=[smem, smem, vmem, hbm, hbm],
+        out_specs=[vmem] * 4 + [smem] + [vmem] * 2,
         out_shape=[jax.ShapeDtypeStruct(shape, F32) for shape in shapes]
         + [jax.ShapeDtypeStruct((tab.size,), jnp.int32)]
-        + [jax.ShapeDtypeStruct(shape, BF16) for shape in states]
-        + [jax.ShapeDtypeStruct(shape, F32) for shape in states],
+        + [jax.ShapeDtypeStruct((heads, 128, 128), kind) for kind in (BF16, F32)],
         scratch_shapes=[
             pltpu.VMEM((hp, tokens), F32),
             pltpu.VMEM((128, tokens), F32),
-            pltpu.VMEM((heads, 128, 128), F32),
+            pltpu.VMEM((tokens // BLK * hp, BLK), F32),
+            pltpu.VMEM(key.shape, BF16),
+            pltpu.VMEM(value.shape, BF16),
+            pltpu.SemaphoreType.DMA((2, tokens // tile)),
         ],
-        compiler_params=params(24 * 2**20),
+        compiler_params=params(32 * 2**20),
         name="prelude",
-    )(doc_lengths, block_shard, decay, in_hbm(key), in_hbm(value))
+    )(doc_lengths, block_shard, in_hbm(decay), in_hbm(key), in_hbm(value))
 
 
 def barred_pairs(hp, cols_ref, docs_ref):
@@ -448,6 +453,80 @@
     )(*operands)
 
 
+def row_scale(extra_ref, features, t, lanes, lines):
+    square = []
+    for line in range(lines):
+        at = [term * lines + line for term in range(3)]
+        parts = [extra_ref[k, row : row + 1, :] for k in range(t) for row in at]
+        square.append(sum(part.astype(F32) for part in parts))
+    scale = [lax.rsqrt(row / features + norm_eps) for row in square]
+    return jnp.concatenate([jnp.broadcast_to(row, (128, lanes)).T for row in scale], axis=0)
+
+
+def place_last_kernel(tab, features, ops, lo, local_width, lanes, lines, table_ref, *refs):
+    t, per, count = tab.t, tab.per, len(ops)
+    extras, pieces = refs[: count * t], refs[count * t : count * (t + 1)]
+    out_ref, extra, block, extra_in, block_in, block_out = refs[-6:]
+    unit = block.shape[2]
+    moves, fetched, stores = [], [], []
+    for j in range(count):
+        for c in range(per):
+            for k in range(t):
+                source = extras[j * t + k].at[c, pl.ds(BLK, 16), pl.ds(0, lanes)]
+                moves.append(pltpu.make_async_copy(source, extra.at[j * per + c, k], extra_in.at[j * per + c, k]))
+                moves[-1].start()
+    for j in range(count):
+        for c in range(per):
+            b = j * per + c
+            fetched.append(pltpu.make_async_copy(pieces[j].at[c], block.at[b], block_in.at[b]))
+            fetched[-1].start()
+    for j, op in enumerate(ops):
+        row = table_ref[tab.row + op] * BLK
+        left = pl.multiple_of(table_ref[tab.side + op] * local_width + lo * 128, 128)
+        for c in range(per):
+            b = j * per + c
+            for k in range(t):
+                moves[b * t + k].wait()
+            scale = row_scale(extra.at[b], features, t, lanes, lines)
+            fetched[b].wait()
+            for col in range(0, unit, 128):
+                cols = slice(col, col + 128)
+                block[b, :, cols] = (block[b, :, cols].astype(F32) * scale).astype(BF16)
+            top = pl.multiple_of(row + c * BLK, BLK)
+            stores.append(
+                pltpu.make_async_copy(
+                    block.at[b], out_ref.at[pl.ds(top, BLK), pl.ds(left, unit)], block_out.at[b]
+                )
+            )
+            stores[-1].start()
+    for store in stores:
+        store.wait()
+
+
+def place_last(tab, table, ops, lo, pieces, extras, out, local_width, features):
+    lanes, lines = extra_rows(extras[0].shape[2])
+    blocks = len(ops) * tab.per
+    hbm = pl.BlockSpec(memory_space=pl.ANY)
+    operands = [table, *extras, *pieces, out]
+    return pl.pallas_call(
+        functools.partial(place_last_kernel, tab, features, ops, lo, local_width, lanes, lines),
+        in_specs=[pl.BlockSpec(memory_space=pltpu.SMEM)] + [hbm] * (len(operands) - 1),
+        out_specs=hbm,
+        out_shape=jax.ShapeDtypeStruct(out.shape, BF16),
+        scratch_shapes=[
+            pltpu.VMEM((blocks, tab.t, 16, lanes), BF16),
+            pltpu.VMEM((blocks, BLK, pieces[0].shape[2]), BF16),
+            pltpu.SemaphoreType.DMA((blocks, tab.t)),
+            pltpu.SemaphoreType.DMA((blocks,)),
+            pltpu.SemaphoreType.DMA((blocks,)),
+        ],
+        input_output_aliases={len(operands) - 1: 0},
+        compiler_params=params(63 * 2**20),
+        cost_estimate=pl.CostEstimate(flops=lanes, bytes_accessed=lanes, transcendentals=0),
+        name="place_last",
+    )(*operands)
+
+
 def local(query_rows, key_rows, value_rows, gate_rows, decay_log, norm_gain, doc_lengths, block_shard):
     tokens, width = query_rows.shape
     heads = decay_log.shape[0]
@@ -457,9 +536,8 @@
     quarter = max(1, heads // 4)
 
     rest = heads - quarter
-    splits = ((0, heads),)
-    (rows, cols, docs, total_gate, table, *states) = prelude(
-        tab, splits, doc_lengths, block_shard, decay_log, key_rows, value_rows
+    rows, cols, docs, total_gate, table, low, full = prelude(
+        tab, doc_lengths, block_shard, decay_log, key_rows, value_rows
     )
     gain = norm_gain.reshape(1, features)
     hop = [(i, i + 1) for i in range(n - 1)]
@@ -471,7 +549,6 @@
             for k in range(t)
         ]
 
-    low, full = states
     carry = total_gate[:, :1, None]
 
     def merge(arrived, part):
@@ -509,11 +586,18 @@
 
     shape = (tokens // t, features)
     out = None
-    for pieces, lo in ((lambda op: [tail[op], head], 2 * quarter), (lambda op: [middle[op]], 0)):
-        for op in range(n):
-            extras = [tail[(op + k * tab.stride) % n] for k in range(t)]
-            out = place(tab, table, op, lo, pieces(op), extras, out, shape, width, features)
-    return out
+
+    def extras(op):
+        return [tail[(op + k * tab.stride) % n] for k in range(t)]
+
+    for op in range(n):
+        out = place(tab, table, op, 2 * quarter, [tail[op], head], extras(op), out, shape, width, features)
+    for op in range(n - 2):
+        out = place(tab, table, op, 0, [middle[op]], extras(op), out, shape, width, features)
+    last = (n - 2, n - 1)
+    return place_last(
+        tab, table, last, 0, middle[n - 2 :], [extra for op in last for extra in extras(op)], out, width, features
+    )
 
 
 def solution(mesh):

time: 235 us -> 231 us (0.983)
  Pallas kernels: 77.3 us -> 73 us
  waiting for transfers between devices: 101 us -> 104 us
    ppermute x4, waiting for transfers between devices: 58.5 us -> 68 us  [local(): lax.ppermute(gated[2][op], ('ctx', 'tp'), route(op))]
    ppermute x4, waiting for transfers between devices: 40.7 us -> 34.2 us  [local(): middle.append(lax.ppermute(ready, ('ctx', 'tp'), route(op)))]
    pallas_call x8 -> x6, Pallas kernels: 23.6 us -> 17.7 us  [place(): pl.pallas_call(functools.partial(place_kernel, features, tab.t, len(piece...]
    ppermute x4, starting transfers between devices: 16.3 us -> 12.4 us  [local(): middle.append(lax.ppermute(ready, ('ctx', 'tp'), route(op)))]
    ppermute x4, starting transfers between devices: 12.6 us -> 15 us  [local(): lax.ppermute(gated[2][op], ('ctx', 'tp'), route(op))]
    pallas_call x1 -> x2, Pallas kernels: 10.4 us -> 12.1 us  [the longest x1 8.35 us: prelude(): pl.pallas_call(functools.partial(prelude_kernel, tab, tile), in_specs=[sm...]
  transfers between devices with their start and end apart: 12 -> 12, of which waited for: 6 -> 5; matrix products, arithmetic and copies ran while one was open for 0% -> 0% of each run, Pallas kernels for 28% -> 27%
where the time goes in v5:
time: 231 us; the launch traced here: 229 us
  waiting for transfers between devices  104 us (45%)
  Pallas kernels  73 us (32%)
  starting transfers between devices  41 us (18%)
  blocking collectives  7.38 us (3%)
  local copies, waits for them, and re-layouts  2.91 us (1%)
    ppermute x4, waiting for transfers between devices, local(): lax.ppermute(gated[2][op], ('ctx', 'tp'), route(op))  68 us
    ppermute x4, waiting for transfers between devices, local(): middle.append(lax.ppermute(ready, ('ctx', 'tp'), route(op)))  34.2 us
    pallas_call x2, Pallas kernels, attend(): pl.pallas_call(functools.partial(attend_kernel, tab, lo, hp, count, last)...  29.5 us
    pallas_call x6, Pallas kernels, place(): pl.pallas_call(functools.partial(place_kernel, features, tab.t, len(piece...  17.7 us
    ppermute x4, starting transfers between devices, local(): lax.ppermute(gated[2][op], ('ctx', 'tp'), route(op))  15 us
    ppermute x4, starting transfers between devices, local(): middle.append(lax.ppermute(ready, ('ctx', 'tp'), route(op)))  12.4 us
    pallas_call x1, Pallas kernels, attend_own(): pl.pallas_call(functools.partial(own_kernel, lo, hp, count), grid_spec=pl...  9.44 us
    pallas_call x1, Pallas kernels, prelude(): pl.pallas_call(functools.partial(prelude_kernel, tab, tile), in_specs=[sm...  8.35 us
  transfers between devices with their start and end apart: 12, of which 5 were waited for; matrix products, arithmetic and copies ran while one was open for 0% of the time, Pallas kernels for 27%

profile of v5, /device:TPU:9, one launch (start us, length us, event | category | flops | bytes accessed | tf_op | source)
XLA Modules:
  0.0 228.9 jit_solution(16187664047950691553)
XLA Ops:
  1.3 8.4 %prelude.1 = (f32[48,2048]{1,0:T(8,128)S(1)}, f32[2048,128]{1,0:T(8,128)S(1)}, f32[8,2048]{1,0:T(8,128)S(1)}, f32[16,128]{1,0:T(8,128)S(1)}, s32[65]{0:T(128)S(1...) custom-call(s32[16]{0:T(128)S(1)} %copy-done.6, s32[32]{0:T(128)S(1)} %copy-done.7, ...), custom_call_target="tpu_custom_call" | custom-call | tf_op jit(solution)/shard_map/prelude/pallas_call | solution.py:176
  9.7 3.2 %collective-permute-start = (bf16[16,128,128]{2,1,0:T(8,128)(2,1)S(1)}, bf16[16,128,128]{2,1,0:T(8,128)(2,1)S(1)}, u32[]{:S(2)}, u32[]{:S(2)}) collective-permute-start(bf16[16,128,128]{2,1,0:T(8,128)(2,1)S(1)} %get-tuple-element.44), channel_id=1, source_target_pairs={{0,2},{2,4},{4,6},{1,3},{3,5},{5,7},{8,10},{10,12},{12,14},{9,11},... | collective-permute-start | bytes 1572872 | tf_op jit(solution)/shard_map/ppermute | solution.py:562
  13.2 9.4 %attend_own.1 = (f32[2048,512]{1,0:T(8,128)S(1)}, bf16[2048,512]{1,0:T(8,128)(2,1)S(1)}, f32[2048,512]{1,0:T(8,128)S(1)}) custom-call(s32[65]{0:T(128)S(1)} %get-tuple-element.39.refs_0_.table_ref, bf16[2048,2048]{1,0:T(8,128)(2,1)} %refs_1_.5, bf16[2048,2048]{1,0:T(8,128)(2,1)} %refs_2_.5, bf16[2048,2048]{1,0:T(8,128)(2,1)} %refs_3_.5, ...), custom_call_target="tpu_custom_call" | custom-call | flops 2147483648 | bytes 10485760 | tf_op jit(solution)/shard_map/attend_own/pallas_call | solution.py:251
  24.7 3.2 %collective-permute-start.2 = (bf16[4,128,128]{2,1,0:T(8,128)(2,1)S(1)}, bf16[4,128,128]{2,1,0:T(8,128)(2,1)S(1)}, u32[]{:S(2)}, u32[]{:S(2)}) collective-permute-start(bf16[4,128,128]{2,1,0:T(8,128)(2,1)S(1)} %add_convert_fusion.1), channel_id=1, source_target_pairs={{0,2},{2,4},{4,6},{1,3},{3,5},{5,7},{8,10},{10,12},{12,14},{9,11},... | collective-permute-start | bytes 393224 | tf_op jit(solution)/shard_map/ppermute | solution.py:568
  27.9 3.2 %collective-permute-start.1 = (bf16[12,128,128]{2,1,0:T(8,128)(2,1)S(1)}, bf16[12,128,128]{2,1,0:T(8,128)(2,1)S(1)}, u32[]{:S(2)}, u32[]{:S(2)}) collective-permute-start(bf16[12,128,128]{2,1,0:T(8,128)(2,1)S(1)} %add_convert_fusion), channel_id=1, source_target_pairs={{0,2},{2,4},{4,6},{1,3},{3,5},{5,7},{8,10},{10,12},{12,14},{9,11},... | collective-permute-start | bytes 1179656 | tf_op jit(solution)/shard_map/ppermute | solution.py:568
  31.1 4.3 %attend_entered.1 = (bf16[8,256,512]{2,1,0:T(8,128)(2,1)}, f32[8,1,256]{2,1,0:T(1,128)S(1)}) custom-call(s32[65]{0:T(128)S(1)} %get-tuple-element.39.refs_0_.table_ref, f32[2048,512]{1,0:T(8,128)S(1)} %get-tuple-element.50.own_ref, bf16[2048,512]{1,0:T(8,128)(2,1)S(1)} %get-tuple-element.51.query_ref, f32[2048,512]{1,0:T(8,128)S(1)} %get-tuple-element.52.factor_ref, ...), custom_call_target="tpu_custom_call" | custom-call | flops 512 | bytes 512 | tf_op jit(solution)/shard_map/attend_entered/pallas_call | solution.py:297
  36.1 4.0 %all-to-all-start = ((bf16[8,256,512]{2,1,0:T(8,128)(2,1)}), bf16[8,256,512]{2,1,0:T(8,128)(2,1)S(1)}, u32[]{:S(2)}, u32[]{:S(2)}) async-start(bf16[8,256,512]{2,1,0:T(8,128)(2,1)} %get-tuple-element.72), calls=%async_computation | async-start | bytes 4194304 | tf_op jit(solution)/shard_map/all_to_all | solution.py:577
  40.9 17.4 %attend.2 = (bf16[2,256,1024]{2,1,0:T(8,128)(2,1)}, bf16[2,256,1024]{2,1,0:T(8,128)(2,1)}, bf16[2,256,1024]{2,1,0:T(8,128)(2,1)}, bf16[2,256,1024]{2,1,0:T(8,128)(2,1)}, f32[8,1,256]{2,1,0:T(1,128)}) custom-call(s32[65]{0:T(128)} %copy-done.4, bf16[2048,2048]{1,0:T(8,128)(2,1)} %refs_1_.5, bf16[2048,2048]{1,0:T(8,128)(2,1)} %refs_2_.5, ...), custom_call_target="tpu_custom_call" | custom-call | flops 8589934592 | bytes 20971520 | tf_op jit(solution)/shard_map/attend/pallas_call | solution.py:367
  58.3 12.1 %attend.3 = (bf16[2,272,512]{2,1,0:T(8,128)(2,1)}, bf16[2,272,512]{2,1,0:T(8,128)(2,1)}, bf16[2,272,512]{2,1,0:T(8,128)(2,1)}, bf16[2,272,512]{2,1,0:T(8,128)(2,1)}) custom-call(s32[65]{0:T(128)} %copy-done.4, bf16[2048,2048]{1,0:T(8,128)(2,1)} %refs_1_.5, bf16[2048,2048]{1,0:T(8,128)(2,1)} %refs_2_.5, bf16[2048,2048]{1,0:T(8,128)(2,1)} %refs_3_.5, ...), custom_call_target="tpu_custom_call" | custom-call | flops 4294967296 | bytes 10485760 | tf_op jit(solution)/shard_map/attend/pallas_call | solution.py:367
  70.4 6.6 %collective-permute-start.3 = (bf16[2,272,512]{2,1,0:T(8,128)(2,1)}, bf16[2,272,512]{2,1,0:T(8,128)(2,1)S(1)}, u32[]{:S(2)}, u32[]{:S(2)}) collective-permute-start(bf16[2,272,512]{2,1,0:T(8,128)(2,1)} %get-tuple-element.57), channel_id=1, source_target_pairs={{0,4},{1,0},{2,6},{3,2},{4,1},{5,5},{6,3},{7,7},{8,12},{9,8},{10,1... | collective-permute-start | bytes 1671176 | tf_op jit(solution)/shard_map/ppermute | solution.py:579
  76.9 3.9 %collective-permute-start.4 = (bf16[2,272,512]{2,1,0:T(8,128)(2,1)}, bf16[2,272,512]{2,1,0:T(8,128)(2,1)}, u32[]{:S(2)}, u32[]{:S(2)}) collective-permute-start(bf16[2,272,512]{2,1,0:T(8,128)(2,1)} %get-tuple-element.60), channel_id=1, source_target_pairs={{0,0},{1,4},{2,2},{3,6},{4,5},{5,1},{6,7},{7,3},{8,8},{9,12},{10,1... | collective-permute-start | bytes 1671176 | tf_op jit(solution)/shard_map/ppermute | solution.py:579
  80.9 4.5 %collective-permute-start.6 = (bf16[2,272,512]{2,1,0:T(8,128)(2,1)}, bf16[2,272,512]{2,1,0:T(8,128)(2,1)}, u32[]{:S(2)}, u32[]{:S(2)}) collective-permute-start(bf16[2,272,512]{2,1,0:T(8,128)(2,1)} %get-tuple-element.66), channel_id=1, source_target_pairs={{0,2},{1,6},{2,4},{3,0},{4,7},{5,3},{6,1},{7,5},{8,10},{9,14},{10,... | collective-permute-start | bytes 1671176 | tf_op jit(solution)/shard_map/ppermute | solution.py:579
  85.4 5.4 %collective-permute-start.10 = (bf16[2,256,1024]{2,1,0:T(8,128)(2,1)}, bf16[2,256,1024]{2,1,0:T(8,128)(2,1)}, u32[]{:S(2)}, u32[]{:S(2)}) collective-permute-start(bf16[2,256,1024]{2,1,0:T(8,128)(2,1)} %get-tuple-element.71), channel_id=1, source_target_pairs={{0,0},{1,4},{2,2},{3,6},{4,5},{5,1},{6,7},{7,3},{8,8},{9,12},{10,1... | collective-permute-start | bytes 3145736 | tf_op jit(solution)/shard_map/ppermute | solution.py:585
  90.8 37.1 %collective-permute-done.4.refs_0_.refs_2_.refs_1_ = bf16[2,272,512]{2,1,0:T(8,128)(2,1)} collective-permute-done((bf16[2,272,512]{2,1,0:T(8,128)(2,1)}, bf16[2,272,512]{2,1,0:T(8,128)(2,1)}, u32[]{:S(2)}, u32[]{:S(2)}) %collective-permute-start.4) | collective-permute-done | bytes 557088 | tf_op jit(solution)/shard_map/ppermute | solution.py:579
  127.9 30.9 %collective-permute-done.5.refs_1_.refs_0_.refs_2_ = bf16[2,272,512]{2,1,0:T(8,128)(2,1)} collective-permute-done((bf16[2,272,512]{2,1,0:T(8,128)(2,1)}, bf16[2,272,512]{2,1,0:T(8,128)(2,1)}, u32[]{:S(2)}, u32[]{:S(2)}) %collective-permute-start.5) | collective-permute-done | bytes 557088 | tf_op jit(solution)/shard_map/ppermute | solution.py:579
  158.8 7.0 %collective-permute-start.7 = (bf16[2,256,1024]{2,1,0:T(8,128)(2,1)}, bf16[2,256,1024]{2,1,0:T(8,128)(2,1)}, u32[]{:S(2)}, u32[]{:S(2)}) collective-permute-start(bf16[2,256,1024]{2,1,0:T(8,128)(2,1)} %get-tuple-element.68), channel_id=1, source_target_pairs={{0,4},{1,0},{2,6},{3,2},{4,1},{5,5},{6,3},{7,7},{8,12},{9,8},{10,1... | collective-permute-start | bytes 3145736 | tf_op jit(solution)/shard_map/ppermute | solution.py:585
  165.9 7.4 %all_to_all.10.refs_3_ = bf16[8,256,512]{2,1,0:T(8,128)(2,1)} all-to-all(bf16[8,256,512]{2,1,0:T(8,128)(2,1)S(1)} %all-to-all-done), channel_id=1, replica_groups=mesh['dp'=4,'ctx'=4,'tp'=2] {'tp'}, dimensions={0} | all-to-all | bytes 4194304 | tf_op jit(solution)/shard_map/all_to_all | solution.py:578
  173.3 3.0 %place.6.refs_4_ = bf16[1024,4096]{1,0:T(8,128)(2,1)} custom-call(s32[65]{0:T(128)} %copy-done.4, bf16[2,272,512]{2,1,0:T(8,128)(2,1)} %collective-permute-done.4.refs_0_.refs_2_.refs_1_, bf16[2,272,512]{2,1,0:T(8,128)(2,1)} %copy-done.8, bf16[2,272,512]{2,1,0:T(8,128)(2,1)} %collective-permute-done.4.refs_0_.refs_2_.refs_1_, ...), custom_call_target="tpu_custom_call" | custom-call | flops 1024 | bytes 1024 | tf_op jit(solution)/shard_map/place/pallas_call | solution.py:440
  176.2 3.0 %place.7.refs_4_ = bf16[1024,4096]{1,0:T(8,128)(2,1)} custom-call(s32[65]{0:T(128)} %copy-done.4, bf16[2,272,512]{2,1,0:T(8,128)(2,1)} %collective-permute-done.6.refs_0_.refs_2_.refs_1_.refs_3_, bf16[2,272,512]{2,1,0:T(8,128)(2,1)} %collective-permute-done.5.refs_1_.refs_0_.refs_2_, ...), custom_call_target="tpu_custom_call", output_to_operand_aliasing={{}: (5, {})} | custom-call | flops 1024 | bytes 1024 | tf_op jit(solution)/shard_map/place/pallas_call | solution.py:440
  185.1 3.0 %place.10.refs_3_ = bf16[1024,4096]{1,0:T(8,128)(2,1)} custom-call(s32[65]{0:T(128)} %copy-done.4, bf16[2,272,512]{2,1,0:T(8,128)(2,1)} %collective-permute-done.4.refs_0_.refs_2_.refs_1_, bf16[2,272,512]{2,1,0:T(8,128)(2,1)} %copy-done.8, bf16[2,256,1024]{2,1,0:T(8,128)(2,1)} %collective-permute-done.10.refs_2_, ...), custom_call_target="tpu_custom_call", output_to_operand_aliasing={{}: (4, {})} | custom-call | flops 1024 | bytes 1024 | tf_op jit(solution)/shard_map/place/pallas_call | solution.py:440
  188.0 28.9 %collective-permute-done.9.refs_2_ = bf16[2,256,1024]{2,1,0:T(8,128)(2,1)} collective-permute-done((bf16[2,256,1024]{2,1,0:T(8,128)(2,1)}, bf16[2,256,1024]{2,1,0:T(8,128)(2,1)}, u32[]{:S(2)}, u32[]{:S(2)}) %collective-permute-start.9) | collective-permute-done | bytes 1048608 | tf_op jit(solution)/shard_map/ppermute | solution.py:585
  217.0 3.0 %place.11.refs_6_ = bf16[1024,4096]{1,0:T(8,128)(2,1)} custom-call(s32[65]{0:T(128)} %copy-done.4, bf16[2,272,512]{2,1,0:T(8,128)(2,1)} %collective-permute-done.6.refs_0_.refs_2_.refs_1_.refs_3_, bf16[2,272,512]{2,1,0:T(8,128)(2,1)} %collective-permute-done.5.refs_1_.refs_0_.refs_2_, ...), custom_call_target="tpu_custom_call", output_to_operand_aliasing={{}: (4, {})} | custom-call | flops 1024 | bytes 1024 | tf_op jit(solution)/shard_map/place/pallas_call | solution.py:440
  219.9 5.3 %collective-permute-done.8.refs_5_ = bf16[2,256,1024]{2,1,0:T(8,128)(2,1)} collective-permute-done((bf16[2,256,1024]{2,1,0:T(8,128)(2,1)}, bf16[2,256,1024]{2,1,0:T(8,128)(2,1)}, u32[]{:S(2)}, u32[]{:S(2)}) %collective-permute-start.8) | collective-permute-done | bytes 1048608 | tf_op jit(solution)/shard_map/ppermute | solution.py:585
  225.2 3.7 %place_last.1 = bf16[1024,4096]{1,0:T(8,128)(2,1)} custom-call(s32[65]{0:T(128)} %copy-done.4, bf16[2,272,512]{2,1,0:T(8,128)(2,1)} %copy-done.8, bf16[2,272,512]{2,1,0:T(8,128)(2,1)} %collective-permute-done.4.refs_0_.refs_2_.refs_1_, bf16[2,272,512]{2,1,0:T(8,128)(2,1)} %collective-permute-done.5.refs_1_.refs_0_.refs_2_, ...), custom_call_target="tpu_custom_call", output_to_operand_aliasing={{}: (7, {})} | custom-call | flops 256 | bytes 256 | tf_op jit(solution)/shard_map/place_last/pallas_call | solution.py:511
  (37 shorter events, 11.0 us)
Async XLA Ops:
  0.0 0.7 copy-start.6
  0.7 0.7 copy-start.7
  1.3 11.8 %copy-start.3 = (f32[4096]{0:T(1024)S(1)}, f32[4096]{0:T(1024)}, u32[]{:S(2)}) copy-start(f32[4096]{0:T(1024)} %param.13) | copy-start | bytes 49156
  9.7 12.9 %copy-start.1 = (f32[48,2048]{1,0:T(8,128)}, f32[48,2048]{1,0:T(8,128)S(1)}, u32[]{:S(2)}) copy-start(f32[48,2048]{1,0:T(8,128)S(1)} %get-tuple-element.40.refs_6_) | copy-start | bytes 1179652
  9.7 12.9 %copy-start.2 = (f32[8,2048]{1,0:T(8,128)}, f32[8,2048]{1,0:T(8,128)S(1)}, u32[]{:S(2)}) copy-start(f32[8,2048]{1,0:T(8,128)S(1)} %get-tuple-element.42.refs_8_) | copy-start | bytes 196612
  9.7 21.4 %copy-start = (f32[2048,128]{1,0:T(8,128)}, f32[2048,128]{1,0:T(8,128)S(1)}, u32[]{:S(2)}) copy-start(f32[2048,128]{1,0:T(8,128)S(1)} %get-tuple-element.41.refs_7_.cols_ref) | copy-start | bytes 3145732
  9.7 21.4 %copy-start.4 = (s32[65]{0:T(128)}, s32[65]{0:T(128)S(1)}, u32[]{:S(2)}) copy-start(s32[65]{0:T(128)S(1)} %get-tuple-element.39.refs_0_.table_ref) | copy-start | bytes 784
  9.7 14.7 %collective-permute-start = (bf16[16,128,128]{2,1,0:T(8,128)(2,1)S(1)}, bf16[16,128,128]{2,1,0:T(8,128)(2,1)S(1)}, u32[]{:S(2)}, u32[]{:S(2)}) collective-permute-start(bf16[16,128,128]{2,1,0:T(8,128)(2,1)S(1)} %get-tuple-element.44), channel_id=1, source_target_pairs={{0,2},{2,4},{4,6},{1,3},{3,5},{5,7},{8,10},{10,12},{12,14},{9,11},... | collective-permute-start | bytes 1572872 | tf_op jit(solution)/shard_map/ppermute | solution.py:562
  24.7 6.4 %collective-permute-start.2 = (bf16[4,128,128]{2,1,0:T(8,128)(2,1)S(1)}, bf16[4,128,128]{2,1,0:T(8,128)(2,1)S(1)}, u32[]{:S(2)}, u32[]{:S(2)}) collective-permute-start(bf16[4,128,128]{2,1,0:T(8,128)(2,1)S(1)} %add_convert_fusion.1), channel_id=1, source_target_pairs={{0,2},{2,4},{4,6},{1,3},{3,5},{5,7},{8,10},{10,12},{12,14},{9,11},... | collective-permute-start | bytes 393224 | tf_op jit(solution)/shard_map/ppermute | solution.py:568
  27.9 12.2 %collective-permute-start.1 = (bf16[12,128,128]{2,1,0:T(8,128)(2,1)S(1)}, bf16[12,128,128]{2,1,0:T(8,128)(2,1)S(1)}, u32[]{:S(2)}, u32[]{:S(2)}) collective-permute-start(bf16[12,128,128]{2,1,0:T(8,128)(2,1)S(1)} %add_convert_fusion), channel_id=1, source_target_pairs={{0,2},{2,4},{4,6},{1,3},{3,5},{5,7},{8,10},{10,12},{12,14},{9,11},... | collective-permute-start | bytes 1179656 | tf_op jit(solution)/shard_map/ppermute | solution.py:568
  35.5 0.6 copy-start.5
  36.1 129.8 %all-to-all-start = ((bf16[8,256,512]{2,1,0:T(8,128)(2,1)}), bf16[8,256,512]{2,1,0:T(8,128)(2,1)S(1)}, u32[]{:S(2)}, u32[]{:S(2)}) async-start(bf16[8,256,512]{2,1,0:T(8,128)(2,1)} %get-tuple-element.72), calls=%async_computation | async-start | bytes 4194304 | tf_op jit(solution)/shard_map/all_to_all | solution.py:577
  40.1 0.8 copy-start.9
  70.4 20.4 %collective-permute-start.3 = (bf16[2,272,512]{2,1,0:T(8,128)(2,1)}, bf16[2,272,512]{2,1,0:T(8,128)(2,1)S(1)}, u32[]{:S(2)}, u32[]{:S(2)}) collective-permute-start(bf16[2,272,512]{2,1,0:T(8,128)(2,1)} %get-tuple-element.57), channel_id=1, source_target_pairs={{0,4},{1,0},{2,6},{3,2},{4,1},{5,5},{6,3},{7,7},{8,12},{9,8},{10,1... | collective-permute-start | bytes 1671176 | tf_op jit(solution)/shard_map/ppermute | solution.py:579
  76.9 51.0 %collective-permute-start.4 = (bf16[2,272,512]{2,1,0:T(8,128)(2,1)}, bf16[2,272,512]{2,1,0:T(8,128)(2,1)}, u32[]{:S(2)}, u32[]{:S(2)}) collective-permute-start(bf16[2,272,512]{2,1,0:T(8,128)(2,1)} %get-tuple-element.60), channel_id=1, source_target_pairs={{0,0},{1,4},{2,2},{3,6},{4,5},{5,1},{6,7},{7,3},{8,8},{9,12},{10,1... | collective-permute-start | bytes 1671176 | tf_op jit(solution)/shard_map/ppermute | solution.py:579
  80.8 78.0 %collective-permute-start.5 = (bf16[2,272,512]{2,1,0:T(8,128)(2,1)}, bf16[2,272,512]{2,1,0:T(8,128)(2,1)}, u32[]{:S(2)}, u32[]{:S(2)}) collective-permute-start(bf16[2,272,512]{2,1,0:T(8,128)(2,1)} %get-tuple-element.63), channel_id=1, source_target_pairs={{0,6},{1,2},{2,0},{3,4},{4,3},{5,7},{6,5},{7,1},{8,14},{9,10},{10,... | collective-permute-start | bytes 1671176 | tf_op jit(solution)/shard_map/ppermute | solution.py:579
  80.9 77.9 %collective-permute-start.6 = (bf16[2,272,512]{2,1,0:T(8,128)(2,1)}, bf16[2,272,512]{2,1,0:T(8,128)(2,1)}, u32[]{:S(2)}, u32[]{:S(2)}) collective-permute-start(bf16[2,272,512]{2,1,0:T(8,128)(2,1)} %get-tuple-element.66), channel_id=1, source_target_pairs={{0,2},{1,6},{2,4},{3,0},{4,7},{5,3},{6,1},{7,5},{8,10},{9,14},{10,... | collective-permute-start | bytes 1671176 | tf_op jit(solution)/shard_map/ppermute | solution.py:579
  85.4 99.7 %collective-permute-start.10 = (bf16[2,256,1024]{2,1,0:T(8,128)(2,1)}, bf16[2,256,1024]{2,1,0:T(8,128)(2,1)}, u32[]{:S(2)}, u32[]{:S(2)}) collective-permute-start(bf16[2,256,1024]{2,1,0:T(8,128)(2,1)} %get-tuple-element.71), channel_id=1, source_target_pairs={{0,0},{1,4},{2,2},{3,6},{4,5},{5,1},{6,7},{7,3},{8,8},{9,12},{10,1... | collective-permute-start | bytes 3145736 | tf_op jit(solution)/shard_map/ppermute | solution.py:585
  90.8 82.5 %copy-start.8 = (bf16[2,272,512]{2,1,0:T(8,128)(2,1)}, bf16[2,272,512]{2,1,0:T(8,128)(2,1)S(1)}, u32[]{:S(2)}) copy-start(bf16[2,272,512]{2,1,0:T(8,128)(2,1)S(1)} %collective-permute-done.3.refs_1_.refs_0_.refs_2_) | copy-start | bytes 1671172
  158.8 58.1 %collective-permute-start.9 = (bf16[2,256,1024]{2,1,0:T(8,128)(2,1)}, bf16[2,256,1024]{2,1,0:T(8,128)(2,1)}, u32[]{:S(2)}, u32[]{:S(2)}) collective-permute-start(bf16[2,256,1024]{2,1,0:T(8,128)(2,1)} %get-tuple-element.70), channel_id=1, source_target_pairs={{0,2},{1,6},{2,4},{3,0},{4,7},{5,3},{6,1},{7,5},{8,10},{9,14},{10,... | collective-permute-start | bytes 3145736 | tf_op jit(solution)/shard_map/ppermute | solution.py:585
  158.8 61.1 %collective-permute-start.7 = (bf16[2,256,1024]{2,1,0:T(8,128)(2,1)}, bf16[2,256,1024]{2,1,0:T(8,128)(2,1)}, u32[]{:S(2)}, u32[]{:S(2)}) collective-permute-start(bf16[2,256,1024]{2,1,0:T(8,128)(2,1)} %get-tuple-element.68), channel_id=1, source_target_pairs={{0,4},{1,0},{2,6},{3,2},{4,1},{5,5},{6,3},{7,7},{8,12},{9,8},{10,1... | collective-permute-start | bytes 3145736 | tf_op jit(solution)/shard_map/ppermute | solution.py:585
  165.8 59.4 %collective-permute-start.8 = (bf16[2,256,1024]{2,1,0:T(8,128)(2,1)}, bf16[2,256,1024]{2,1,0:T(8,128)(2,1)}, u32[]{:S(2)}, u32[]{:S(2)}) collective-permute-start(bf16[2,256,1024]{2,1,0:T(8,128)(2,1)} %get-tuple-element.69), channel_id=1, source_target_pairs={{0,6},{1,2},{2,0},{3,4},{4,3},{5,7},{6,5},{7,1},{8,14},{9,10},{10,... | collective-permute-start | bytes 3145736 | tf_op jit(solution)/shard_map/ppermute | solution.py:585

commit v6 on v5

--- a/solution.py
+++ b/solution.py
@@ -190,7 +190,7 @@
         ],
         compiler_params=params(32 * 2**20),
         name="prelude",
-    )(doc_lengths, block_shard, in_hbm(decay), in_hbm(key), in_hbm(value))
+    )(*map(in_hbm, (doc_lengths, block_shard, decay, key, value)))
 
 
 def barred_pairs(hp, cols_ref, docs_ref):
@@ -318,8 +318,6 @@
     @pl.when(step == 0)
     def _():
         state[...] = state_ref[...].astype(F32)
-        if last:
-            gated[BLK:, :] = jnp.zeros((16, gated.shape[1]), BF16)
 
     barred = barred_pairs(hp, cols_ref, docs_ref)
     square = jnp.zeros((BLK, 128), F32)
@@ -339,7 +337,6 @@
             for line in range(lines):
                 piece = part[:, line * lanes : (line + 1) * lanes]
                 extra = jnp.where(row == term * lines + line, piece, extra)
-        gated[BLK:, :lanes] = extra.astype(BF16)
     else:
         refs[11 + ops][0] = total
     which = table_ref[tab.which + step]
@@ -347,7 +344,36 @@
 
         @pl.when(which == op)
         def _():
-            outs[op][0] = gated[...]
+            outs[op][...] = gated[...]
+            if last:
+                refs[11 + ops + op][...] = extra.astype(BF16)
+
+
+def stitch_kernel(count, *refs):
+    extras, outs, arrived = refs[:count], refs[2 * count : 3 * count], refs[-1]
+    copies = []
+    for k in range(count):
+        target = outs[k].at[pl.ds(outs[k].shape[0] - 16, 16)]
+        copies.append(pltpu.make_async_copy(extras[k], target, arrived.at[k]))
+        copies[-1].start()
+    for copy in copies:
+        copy.wait()
+
+
+def stitch(pieces, extras):
+    count = len(pieces)
+    hbm = pl.BlockSpec(memory_space=pl.ANY)
+    return pl.pallas_call(
+        functools.partial(stitch_kernel, count),
+        in_specs=[hbm] * (2 * count),
+        out_specs=[hbm] * count,
+        out_shape=[jax.ShapeDtypeStruct(piece.shape, BF16) for piece in pieces],
+        scratch_shapes=[pltpu.SemaphoreType.DMA((count,))],
+        input_output_aliases={count + k: k for k in range(count)},
+        compiler_params=params(63 * 2**20),
+        cost_estimate=pl.CostEstimate(flops=128, bytes_accessed=128, transcendentals=0),
+        name="stitch",
+    )(*extras, *pieces)
 
 
 def attend(tab, table, query, key, value, gate, gain, rows, cols, docs, entering, base, lo, count, squares, last):
@@ -357,13 +383,21 @@
     hp = rows.shape[0] // 3
     width = count * 128
     at = lo * 128 // width
-    height = BLK + 16 * last
+    lanes, _ = extra_rows(width)
     wide = pl.BlockSpec((BLK, width), lambda c, tbl: (c, at))
     square_spec = pl.BlockSpec((1, 1, BLK), lambda c, tbl: (tbl[tab.slot + c], 0, 0))
 
     def out_map(op, c, tbl):
-        return (tbl[tab.place + op * chunks + c], 0, 0)
-
+        return (tbl[tab.place + op * chunks + c], 0)
+
+    def extra_map(op, c, tbl):
+        return (0, tbl[tab.place + op * chunks + c])
+
+    if last:
+        square_specs = [pl.BlockSpec((16, lanes), functools.partial(extra_map, op)) for op in range(ops)]
+        square_shapes = [jax.ShapeDtypeStruct((16, width), BF16)] * ops
+    else:
+        square_specs, square_shapes = [square_spec], [jax.ShapeDtypeStruct((chunks, 1, BLK), F32)]
     out = pl.pallas_call(
         functools.partial(attend_kernel, tab, lo, hp, count, last),
         grid_spec=pltpu.PrefetchScalarGridSpec(
@@ -382,53 +416,61 @@
             ]
             + [square_spec],
             out_specs=[
-                pl.BlockSpec((1, height, width), functools.partial(out_map, op)) for op in range(ops)
+                pl.BlockSpec((BLK, width), functools.partial(out_map, op)) for op in range(ops)
             ]
-            + [square_spec] * (not last),
+            + square_specs,
             scratch_shapes=[
                 pltpu.VMEM((count, 128, 128), F32),
-                pltpu.VMEM((height, width), BF16),
+                pltpu.VMEM((BLK, width), BF16),
             ],
         ),
-        out_shape=[jax.ShapeDtypeStruct((chunks // ops, height, width), BF16)] * ops
-        + [jax.ShapeDtypeStruct((chunks, 1, BLK), F32)] * (not last),
+        out_shape=[jax.ShapeDtypeStruct((per * BLK + 16 * last, width), BF16)] * ops + square_shapes,
         compiler_params=params(),
         cost_estimate=pl.CostEstimate(flops=16 * tokens * width * BLK, bytes_accessed=10 * tokens * width, transcendentals=tokens * width),
         name="attend",
     )(table, query, key, value, gate, gain, rows, cols, docs, entering, squares)
-    return out[:ops], None if last else out[ops]
+    if last:
+        return stitch(out[:ops], out[ops:]), None
+    return out[:ops], out[ops]
+
+
+def row_scale(extras, features, lanes, lines):
+    square = []
+    for line in range(lines):
+        at = [term * lines + line for term in range(3)]
+        parts = [extra[row : row + 1, :] for extra in extras for row in at]
+        square.append(sum(part.astype(F32) for part in parts))
+    scale = [lax.rsqrt(row / features + norm_eps) for row in square]
+    return jnp.concatenate([jnp.broadcast_to(row, (128, lanes)).T for row in scale], axis=0)
 
 
 def place_kernel(features, t, count, lanes, lines, table_ref, *refs):
     out_ref = refs[-1]
-    square = []
-    for line in range(lines):
-        parts = [refs[k][0, term * lines + line : term * lines + line + 1, :] for k in range(t) for term in range(3)]
-        square.append(sum(part.astype(F32) for part in parts))
-    scale = [lax.rsqrt(row / features + norm_eps) for row in square]
-    scale = jnp.concatenate([jnp.broadcast_to(row, (128, lanes)).T for row in scale], axis=0)
+    scale = row_scale(refs[:t], features, lanes, lines)
     done = 0
     for piece_ref in refs[t : t + count]:
-        for c in range(piece_ref.shape[2] // 128):
-            piece = piece_ref[0, :BLK, c * 128 : (c + 1) * 128].astype(F32)
+        for c in range(piece_ref.shape[1] // 128):
+            piece = piece_ref[:, c * 128 : (c + 1) * 128].astype(F32)
             out_ref[:, done : done + 128] = (piece * scale).astype(BF16)
             done += 128
 
 
 def place(tab, table, op, lo, pieces, extras, out, shape, local_width, features):
+    rows = tab.per * BLK
+
     def piece_map(all_blocks, c, tbl):
         block = tbl[tab.side + op] * tab.stride * tab.per + tbl[tab.row + op] if all_blocks else 0
-        return (block + c, 0, 0)
-
-    lanes, lines = extra_rows(extras[0].shape[2])
-    unit = sum(piece.shape[2] for piece in pieces)
+        return (block + c, 0)
+
+    lanes, lines = extra_rows(extras[0].shape[1])
+    unit = sum(piece.shape[1] for piece in pieces)
 
     def out_map(c, tbl):
         return (tbl[tab.row + op] + c, tbl[tab.side + op] * (local_width // unit) + lo * 128 // unit)
 
-    in_specs = [pl.BlockSpec((1, 16, lanes), lambda c, tbl: (c, BLK // 16, 0))] * tab.t
+    in_specs = [pl.BlockSpec((16, lanes), lambda c, tbl: (rows // 16, c))] * tab.t
     in_specs += [
-        pl.BlockSpec((1, *piece.shape[1:]), functools.partial(piece_map, piece.shape[0] > tab.per))
+        pl.BlockSpec((BLK, piece.shape[1]), functools.partial(piece_map, piece.shape[0] == tab.chunks * BLK))
         for piece in pieces
     ]
     operands = [table, *extras, *pieces]
@@ -453,32 +495,22 @@
     )(*operands)
 
 
-def row_scale(extra_ref, features, t, lanes, lines):
-    square = []
-    for line in range(lines):
-        at = [term * lines + line for term in range(3)]
-        parts = [extra_ref[k, row : row + 1, :] for k in range(t) for row in at]
-        square.append(sum(part.astype(F32) for part in parts))
-    scale = [lax.rsqrt(row / features + norm_eps) for row in square]
-    return jnp.concatenate([jnp.broadcast_to(row, (128, lanes)).T for row in scale], axis=0)
-
-
 def place_last_kernel(tab, features, ops, lo, local_width, lanes, lines, table_ref, *refs):
     t, per, count = tab.t, tab.per, len(ops)
     extras, pieces = refs[: count * t], refs[count * t : count * (t + 1)]
     out_ref, extra, block, extra_in, block_in, block_out = refs[-6:]
-    unit = block.shape[2]
+    unit, rows = block.shape[2], per * BLK
     moves, fetched, stores = [], [], []
     for j in range(count):
         for c in range(per):
             for k in range(t):
-                source = extras[j * t + k].at[c, pl.ds(BLK, 16), pl.ds(0, lanes)]
+                source = extras[j * t + k].at[pl.ds(rows, 16), pl.ds(c * lanes, lanes)]
                 moves.append(pltpu.make_async_copy(source, extra.at[j * per + c, k], extra_in.at[j * per + c, k]))
                 moves[-1].start()
     for j in range(count):
         for c in range(per):
             b = j * per + c
-            fetched.append(pltpu.make_async_copy(pieces[j].at[c], block.at[b], block_in.at[b]))
+            fetched.append(pltpu.make_async_copy(pieces[j].at[pl.ds(c * BLK, BLK)], block.at[b], block_in.at[b]))
             fetched[-1].start()
     for j, op in enumerate(ops):
         row = table_ref[tab.row + op] * BLK
@@ -487,7 +519,7 @@
             b = j * per + c
             for k in range(t):
                 moves[b * t + k].wait()
-            scale = row_scale(extra.at[b], features, t, lanes, lines)
+            scale = row_scale([extra.at[b, k] for k in range(t)], features, lanes, lines)
             fetched[b].wait()
             for col in range(0, unit, 128):
                 cols = slice(col, col + 128)
@@ -504,7 +536,7 @@
 
 
 def place_last(tab, table, ops, lo, pieces, extras, out, local_width, features):
-    lanes, lines = extra_rows(extras[0].shape[2])
+    lanes, lines = extra_rows(extras[0].shape[1])
     blocks = len(ops) * tab.per
     hbm = pl.BlockSpec(memory_space=pl.ANY)
     operands = [table, *extras, *pieces, out]
@@ -515,7 +547,7 @@
         out_shape=jax.ShapeDtypeStruct(out.shape, BF16),
         scratch_shapes=[
             pltpu.VMEM((blocks, tab.t, 16, lanes), BF16),
-            pltpu.VMEM((blocks, BLK, pieces[0].shape[2]), BF16),
+            pltpu.VMEM((blocks, BLK, pieces[0].shape[1]), BF16),
             pltpu.SemaphoreType.DMA((blocks, tab.t)),
             pltpu.SemaphoreType.DMA((blocks,)),
             pltpu.SemaphoreType.DMA((blocks,)),
@@ -575,7 +607,7 @@
         )
         gated.append(outs)
     head = lax.all_to_all(ready, "ctx", split_axis=0, concat_axis=0, tiled=True)
-    head = lax.all_to_all(head, "tp", split_axis=0, concat_axis=0, tiled=True)
+    head = lax.all_to_all(head, "tp", split_axis=0, concat_axis=0, tiled=True).reshape(tokens, -1)
     tail = [lax.ppermute(gated[2][op], ("ctx", "tp"), route(op)) for op in range(n)]
     middle = []
     for op in range(n):

time: 231 us -> 229 us (level)
  starting transfers between devices: 41 us -> 34.7 us
  Pallas kernels: 73 us -> 76.2 us
    ppermute x4, starting transfers between devices: 15 us -> 11.4 us  [local(): lax.ppermute(gated[2][op], ('ctx', 'tp'), route(op))]
    ppermute x4, starting transfers between devices: 12.4 us -> 9.15 us  [local(): middle.append(lax.ppermute(ready, ('ctx', 'tp'), route(op)))]
    pallas_call x0 -> x1, Pallas kernels: none -> 3.12 us  [stitch(): pl.pallas_call(functools.partial(stitch_kernel, count), in_specs=[hbm] *...]
  transfers between devices with their start and end apart: 12 -> 12, of which waited for: 5 -> 6; matrix products, arithmetic and copies ran while one was open for 0% -> 0% of each run, Pallas kernels for 27% -> 28%
where the time goes in v6:
time: 229 us; the launch traced here: 227 us
  waiting for transfers between devices  104 us (45%)
  Pallas kernels  76.2 us (33%)
  starting transfers between devices  34.7 us (15%)
  blocking collectives  9.62 us (4%)
    ppermute x4, waiting for transfers between devices, local(): lax.ppermute(gated[2][op], ('ctx', 'tp'), route(op))  67.9 us
    ppermute x4, waiting for transfers between devices, local(): middle.append(lax.ppermute(ready, ('ctx', 'tp'), route(op)))  34.2 us
    pallas_call x2, Pallas kernels, attend(): pl.pallas_call(functools.partial(attend_kernel, tab, lo, hp, count, last)...  29.7 us
    pallas_call x6, Pallas kernels, place(): pl.pallas_call(functools.partial(place_kernel, features, tab.t, len(piece...  17.7 us
    ppermute x4, starting transfers between devices, local(): lax.ppermute(gated[2][op], ('ctx', 'tp'), route(op))  11.4 us
    all_to_all x1, blocking collectives, local(): lax.all_to_all(head, 'tp', split_axis=0, concat_axis=0, tiled=True)  9.62 us
    pallas_call x1, Pallas kernels, attend_own(): pl.pallas_call(functools.partial(own_kernel, lo, hp, count), grid_spec=pl...  9.44 us
    ppermute x4, starting transfers between devices, local(): middle.append(lax.ppermute(ready, ('ctx', 'tp'), route(op)))  9.15 us
  transfers between devices with their start and end apart: 12, of which 6 were waited for; matrix products, arithmetic and copies ran while one was open for 0% of the time, Pallas kernels for 28%

profile of v6, /device:TPU:9, one launch (start us, length us, event | category | flops | bytes accessed | tf_op | source)
XLA Modules:
  0.0 226.8 jit_solution(18139679672884930696)
XLA Ops:
  0.0 8.4 %prelude.1 = (f32[48,2048]{1,0:T(8,128)S(1)}, f32[2048,128]{1,0:T(8,128)S(1)}, f32[8,2048]{1,0:T(8,128)S(1)}, f32[16,128]{1,0:T(8,128)S(1)}, s32[65]{0:T(128)S(1...) custom-call(s32[16]{0:T(128)} %len_ref.1, s32[32]{0:T(128)} %shard_ref.1, f32[16,2048]{1,0:T(8,128)} %decay_ref.1, ...), custom_call_target="tpu_custom_call" | custom-call | tf_op jit(solution)/shard_map/prelude/pallas_call | solution.py:176
  8.4 3.2 %collective-permute-start = (bf16[16,128,128]{2,1,0:T(8,128)(2,1)S(1)}, bf16[16,128,128]{2,1,0:T(8,128)(2,1)S(1)}, u32[]{:S(2)}, u32[]{:S(2)}) collective-permute-start(bf16[16,128,128]{2,1,0:T(8,128)(2,1)S(1)} %get-tuple-element.52), channel_id=1, source_target_pairs={{0,2},{2,4},{4,6},{1,3},{3,5},{5,7},{8,10},{10,12},{12,14},{9,11},... | collective-permute-start | bytes 1572872 | tf_op jit(solution)/shard_map/ppermute | solution.py:594
  11.9 9.4 %attend_own.1 = (f32[2048,512]{1,0:T(8,128)S(1)}, bf16[2048,512]{1,0:T(8,128)(2,1)S(1)}, f32[2048,512]{1,0:T(8,128)S(1)}) custom-call(s32[65]{0:T(128)S(1)} %get-tuple-element.47.refs_0_.table_ref, bf16[2048,2048]{1,0:T(8,128)(2,1)} %refs_1_.5, bf16[2048,2048]{1,0:T(8,128)(2,1)} %refs_2_.5, bf16[2048,2048]{1,0:T(8,128)(2,1)} %refs_3_.5, ...), custom_call_target="tpu_custom_call" | custom-call | flops 2147483648 | bytes 10485760 | tf_op jit(solution)/shard_map/attend_own/pallas_call | solution.py:251
  23.4 3.2 %collective-permute-start.2 = (bf16[4,128,128]{2,1,0:T(8,128)(2,1)S(1)}, bf16[4,128,128]{2,1,0:T(8,128)(2,1)S(1)}, u32[]{:S(2)}, u32[]{:S(2)}) collective-permute-start(bf16[4,128,128]{2,1,0:T(8,128)(2,1)S(1)} %add_convert_fusion.1), channel_id=1, source_target_pairs={{0,2},{2,4},{4,6},{1,3},{3,5},{5,7},{8,10},{10,12},{12,14},{9,11},... | collective-permute-start | bytes 393224 | tf_op jit(solution)/shard_map/ppermute | solution.py:600
  26.6 3.2 %collective-permute-start.1 = (bf16[12,128,128]{2,1,0:T(8,128)(2,1)S(1)}, bf16[12,128,128]{2,1,0:T(8,128)(2,1)S(1)}, u32[]{:S(2)}, u32[]{:S(2)}) collective-permute-start(bf16[12,128,128]{2,1,0:T(8,128)(2,1)S(1)} %add_convert_fusion), channel_id=1, source_target_pairs={{0,2},{2,4},{4,6},{1,3},{3,5},{5,7},{8,10},{10,12},{12,14},{9,11},... | collective-permute-start | bytes 1179656 | tf_op jit(solution)/shard_map/ppermute | solution.py:600
  29.8 4.1 %attend_entered.1 = (bf16[8,256,512]{2,1,0:T(8,128)(2,1)}, f32[8,1,256]{2,1,0:T(1,128)S(1)}) custom-call(s32[65]{0:T(128)S(1)} %get-tuple-element.47.refs_0_.table_ref, f32[2048,512]{1,0:T(8,128)S(1)} %get-tuple-element.58.own_ref, bf16[2048,512]{1,0:T(8,128)(2,1)S(1)} %get-tuple-element.59.query_ref, f32[2048,512]{1,0:T(8,128)S(1)} %get-tuple-element.60.factor_ref, ...), custom_call_target="tpu_custom_call" | custom-call | flops 512 | bytes 512 | tf_op jit(solution)/shard_map/attend_entered/pallas_call | solution.py:297
  34.6 4.6 %all-to-all-start = ((bf16[8,256,512]{2,1,0:T(8,128)(2,1)}), bf16[8,256,512]{2,1,0:T(8,128)(2,1)}, u32[]{:S(2)}, u32[]{:S(2)}) async-start(bf16[8,256,512]{2,1,0:T(8,128)(2,1)} %get-tuple-element.88), calls=%async_computation | async-start | bytes 4194304 | tf_op jit(solution)/shard_map/all_to_all | solution.py:609
  40.0 17.5 %attend.2 = (bf16[512,1024]{1,0:T(8,128)(2,1)}, bf16[512,1024]{1,0:T(8,128)(2,1)}, bf16[512,1024]{1,0:T(8,128)(2,1)}, bf16[512,1024]{1,0:T(8,128)(2,1)}, f32[8,1,256]{2,1,0:T(1,128)}) custom-call(s32[65]{0:T(128)} %copy-done.4, bf16[2048,2048]{1,0:T(8,128)(2,1)} %refs_1_.5, bf16[2048,2048]{1,0:T(8,128)(2,1)} %refs_2_.5, bf16[2048,2048]{1,0:T(8,128)(2,1)} %refs_3_.5, ...), custom_call_target="tpu_custom_call" | custom-call | flops 8589934592 | bytes 20971520 | tf_op jit(solution)/shard_map/attend/pallas_call | solution.py:401
  57.5 12.2 %attend.3 = (bf16[528,512]{1,0:T(8,128)(2,1)}, bf16[528,512]{1,0:T(8,128)(2,1)}, bf16[528,512]{1,0:T(8,128)(2,1)}, bf16[528,512]{1,0:T(8,128)(2,1)}, bf16[16,512...) custom-call(s32[65]{0:T(128)} %copy-done.4, ...), custom_call_target="tpu_custom_call" | custom-call | flops 4294967296 | bytes 10485760 | tf_op jit(solution)/shard_map/attend/pallas_call | solution.py:401
  69.7 3.1 %stitch.1 = (bf16[528,512]{1,0:T(8,128)(2,1)}, bf16[528,512]{1,0:T(8,128)(2,1)}, bf16[528,512]{1,0:T(8,128)(2,1)}, bf16[528,512]{1,0:T(8,128)(2,1)}) custom-call(bf16[16,512]{1,0:T(8,128)(2,1)} %get-tuple-element.65.refs_0_, bf16[16,512]{1,0:T(8,128)(2,1)} %get-tuple-element.66.refs_1_, ...), custom_call_target="tpu_custom_call", output_to_operand_aliasing={{0}: (4, {}), {1}: (5, {}), {2}: (6, {}), {3}: (7, {})} | custom-call | flops 128 | bytes 128 | tf_op jit(solution)/shard_map/stitch/pallas_call | solution.py:366
  72.8 6.0 %collective-permute-start.3 = (bf16[528,512]{1,0:T(8,128)(2,1)}, bf16[528,512]{1,0:T(8,128)(2,1)S(1)}, u32[]{:S(2)}, u32[]{:S(2)}) collective-permute-start(bf16[528,512]{1,0:T(8,128)(2,1)} %get-tuple-element.73), channel_id=1, source_target_pairs={{0,4},{1,0},{2,6},{3,2},{4,1},{5,5},{6,3},{7,7},{8,12},{9,8},{10,1... | collective-permute-start | bytes 1622024 | tf_op jit(solution)/shard_map/ppermute | solution.py:611
  78.8 3.9 %collective-permute-start.4 = (bf16[528,512]{1,0:T(8,128)(2,1)}, bf16[528,512]{1,0:T(8,128)(2,1)S(1)}, u32[]{:S(2)}, u32[]{:S(2)}) collective-permute-start(bf16[528,512]{1,0:T(8,128)(2,1)} %get-tuple-element.76), channel_id=1, source_target_pairs={{0,0},{1,4},{2,2},{3,6},{4,5},{5,1},{6,7},{7,3},{8,8},{9,12},{10,1... | collective-permute-start | bytes 1622024 | tf_op jit(solution)/shard_map/ppermute | solution.py:611
  84.2 4.3 %collective-permute-start.10 = (bf16[512,1024]{1,0:T(8,128)(2,1)}, bf16[512,1024]{1,0:T(8,128)(2,1)}, u32[]{:S(2)}, u32[]{:S(2)}) collective-permute-start(bf16[512,1024]{1,0:T(8,128)(2,1)} %get-tuple-element.87), channel_id=1, source_target_pairs={{0,0},{1,4},{2,2},{3,6},{4,5},{5,1},{6,7},{7,3},{8,8},{9,12},{10,1... | collective-permute-start | bytes 3145736 | tf_op jit(solution)/shard_map/ppermute | solution.py:617
  88.5 3.4 %collective-permute-done.3.refs_1_.refs_0_.refs_2_ = bf16[528,512]{1,0:T(8,128)(2,1)S(1)} collective-permute-done((bf16[528,512]{1,0:T(8,128)(2,1)}, bf16[528,512]{1,0:T(8,128)(2,1)S(1)}, u32[]{:S(2)}, u32[]{:S(2)}) %collective-permute-start.3) | collective-permute-done | bytes 540704 | tf_op jit(solution)/shard_map/ppermute | solution.py:611
  91.8 23.5 %collective-permute-done.4.refs_0_.refs_2_.refs_1_ = bf16[528,512]{1,0:T(8,128)(2,1)S(1)} collective-permute-done((bf16[528,512]{1,0:T(8,128)(2,1)}, bf16[528,512]{1,0:T(8,128)(2,1)S(1)}, u32[]{:S(2)}, u32[]{:S(2)}) %collective-permute-start.4) | collective-permute-done | bytes 540704 | tf_op jit(solution)/shard_map/ppermute | solution.py:611
  115.4 41.0 %collective-permute-done.5.refs_1_.refs_0_.refs_2_ = bf16[528,512]{1,0:T(8,128)(2,1)S(1)} collective-permute-done((bf16[528,512]{1,0:T(8,128)(2,1)}, bf16[528,512]{1,0:T(8,128)(2,1)S(1)}, u32[]{:S(2)}, u32[]{:S(2)}) %collective-permute-start.5) | collective-permute-done | bytes 540704 | tf_op jit(solution)/shard_map/ppermute | solution.py:611
  156.7 4.6 %collective-permute-start.7 = (bf16[512,1024]{1,0:T(8,128)(2,1)}, bf16[512,1024]{1,0:T(8,128)(2,1)}, u32[]{:S(2)}, u32[]{:S(2)}) collective-permute-start(bf16[512,1024]{1,0:T(8,128)(2,1)} %get-tuple-element.84), channel_id=1, source_target_pairs={{0,4},{1,0},{2,6},{3,2},{4,1},{5,5},{6,3},{7,7},{8,12},{9,8},{10,1... | collective-permute-start | bytes 3145736 | tf_op jit(solution)/shard_map/ppermute | solution.py:617
  161.3 9.6 %all_to_all.10 = bf16[8,256,512]{2,1,0:T(8,128)(2,1)} all-to-all(bf16[8,256,512]{2,1,0:T(8,128)(2,1)} %all-to-all-done), channel_id=1, replica_groups=mesh['dp'=4,'ctx'=4,'tp'=2] {'tp'}, dimensions={0} | all-to-all | bytes 4194304 | tf_op jit(solution)/shard_map/all_to_all | solution.py:610
  173.9 2.9 %place.7.refs_4_ = bf16[1024,4096]{1,0:T(8,128)(2,1)} custom-call(s32[65]{0:T(128)} %copy-done.4, bf16[528,512]{1,0:T(8,128)(2,1)} %collective-permute-done.6.refs_0_.refs_2_.refs_1_.refs_3_, bf16[528,512]{1,0:T(8,128)(2,1)} %copy-done.6, bf16[528,512]{1,0:T(8,128)(2,1)} %collective-permute-done.6.refs_0_.refs_2_.refs_1_.refs_3_, ...), custom_call_target="tpu_custom_call", output_to_operand_aliasing={{}: (5, {})} | custom-call | flops 1024 | bytes 1024 | tf_op jit(solution)/shard_map/place/pallas_call | solution.py:482
  182.8 3.0 %place.10.refs_3_ = bf16[1024,4096]{1,0:T(8,128)(2,1)} custom-call(s32[65]{0:T(128)} %copy-done.4, bf16[528,512]{1,0:T(8,128)(2,1)} %copy-done.8, bf16[528,512]{1,0:T(8,128)(2,1)} %copy-done.7, bf16[512,1024]{1,0:T(8,128)(2,1)} %collective-permute-done.10.refs_2_, bf16[1024,4096]{1,0:T(8,128)(2,1)} %place.9.refs_3_), custom_call_target="tpu_custom_call", output_to_operand_aliasing={{}: (4, {})} | custom-call | flops 1024 | bytes 1024 | tf_op jit(solution)/shard_map/place/pallas_call | solution.py:482
  185.7 30.2 %collective-permute-done.9.refs_2_ = bf16[512,1024]{1,0:T(8,128)(2,1)} collective-permute-done((bf16[512,1024]{1,0:T(8,128)(2,1)}, bf16[512,1024]{1,0:T(8,128)(2,1)}, u32[]{:S(2)}, u32[]{:S(2)}) %collective-permute-start.9) | collective-permute-done | bytes 1048608 | tf_op jit(solution)/shard_map/ppermute | solution.py:617
  215.9 3.0 %place.11.refs_6_ = bf16[1024,4096]{1,0:T(8,128)(2,1)} custom-call(s32[65]{0:T(128)} %copy-done.4, bf16[528,512]{1,0:T(8,128)(2,1)} %collective-permute-done.6.refs_0_.refs_2_.refs_1_.refs_3_, bf16[528,512]{1,0:T(8,128)(2,1)} %copy-done.6, bf16[512,1024]{1,0:T(8,128)(2,1)} %collective-permute-done.9.refs_2_, ...), custom_call_target="tpu_custom_call", output_to_operand_aliasing={{}: (4, {})} | custom-call | flops 1024 | bytes 1024 | tf_op jit(solution)/shard_map/place/pallas_call | solution.py:482
  218.8 4.1 %collective-permute-done.8.refs_5_ = bf16[512,1024]{1,0:T(8,128)(2,1)} collective-permute-done((bf16[512,1024]{1,0:T(8,128)(2,1)}, bf16[512,1024]{1,0:T(8,128)(2,1)}, u32[]{:S(2)}, u32[]{:S(2)}) %collective-permute-start.8) | collective-permute-done | bytes 1048608 | tf_op jit(solution)/shard_map/ppermute | solution.py:617
  222.9 3.7 %place_last.1 = bf16[1024,4096]{1,0:T(8,128)(2,1)} custom-call(s32[65]{0:T(128)} %copy-done.4, bf16[528,512]{1,0:T(8,128)(2,1)} %copy-done.7, bf16[528,512]{1,0:T(8,128)(2,1)} %copy-done.8, bf16[528,512]{1,0:T(8,128)(2,1)} %copy-done.6, bf16[528,512]{1,0:T(8,128)(2,1)} %collective-permute-done.6.refs_0_.refs_2_.refs_1_.refs_3_, ...), custom_call_target="tpu_custom_call", output_to_operand_aliasing={{}: (7, {})} | custom-call | flops 256 | bytes 256 | tf_op jit(solution)/shard_map/place_last/pallas_call | solution.py:543
  (38 shorter events, 14.4 us)
Async XLA Ops:
  0.0 11.9 %copy-start.3 = (f32[4096]{0:T(1024)S(1)}, f32[4096]{0:T(1024)}, u32[]{:S(2)}) copy-start(f32[4096]{0:T(1024)} %param.13) | copy-start | bytes 49156
  8.4 12.9 %copy-start.1 = (f32[48,2048]{1,0:T(8,128)}, f32[48,2048]{1,0:T(8,128)S(1)}, u32[]{:S(2)}) copy-start(f32[48,2048]{1,0:T(8,128)S(1)} %get-tuple-element.48.refs_6_) | copy-start | bytes 1179652
  8.4 12.9 %copy-start.2 = (f32[8,2048]{1,0:T(8,128)}, f32[8,2048]{1,0:T(8,128)S(1)}, u32[]{:S(2)}) copy-start(f32[8,2048]{1,0:T(8,128)S(1)} %get-tuple-element.50.refs_8_) | copy-start | bytes 196612
  8.4 21.4 %copy-start = (f32[2048,128]{1,0:T(8,128)}, f32[2048,128]{1,0:T(8,128)S(1)}, u32[]{:S(2)}) copy-start(f32[2048,128]{1,0:T(8,128)S(1)} %get-tuple-element.49.refs_7_.cols_ref) | copy-start | bytes 3145732
  8.4 21.4 %copy-start.4 = (s32[65]{0:T(128)}, s32[65]{0:T(128)S(1)}, u32[]{:S(2)}) copy-start(s32[65]{0:T(128)S(1)} %get-tuple-element.47.refs_0_.table_ref) | copy-start | bytes 784
  8.4 14.7 %collective-permute-start = (bf16[16,128,128]{2,1,0:T(8,128)(2,1)S(1)}, bf16[16,128,128]{2,1,0:T(8,128)(2,1)S(1)}, u32[]{:S(2)}, u32[]{:S(2)}) collective-permute-start(bf16[16,128,128]{2,1,0:T(8,128)(2,1)S(1)} %get-tuple-element.52), channel_id=1, source_target_pairs={{0,2},{2,4},{4,6},{1,3},{3,5},{5,7},{8,10},{10,12},{12,14},{9,11},... | collective-permute-start | bytes 1572872 | tf_op jit(solution)/shard_map/ppermute | solution.py:594
  23.4 6.4 %collective-permute-start.2 = (bf16[4,128,128]{2,1,0:T(8,128)(2,1)S(1)}, bf16[4,128,128]{2,1,0:T(8,128)(2,1)S(1)}, u32[]{:S(2)}, u32[]{:S(2)}) collective-permute-start(bf16[4,128,128]{2,1,0:T(8,128)(2,1)S(1)} %add_convert_fusion.1), channel_id=1, source_target_pairs={{0,2},{2,4},{4,6},{1,3},{3,5},{5,7},{8,10},{10,12},{12,14},{9,11},... | collective-permute-start | bytes 393224 | tf_op jit(solution)/shard_map/ppermute | solution.py:600
  26.6 12.6 %collective-permute-start.1 = (bf16[12,128,128]{2,1,0:T(8,128)(2,1)S(1)}, bf16[12,128,128]{2,1,0:T(8,128)(2,1)S(1)}, u32[]{:S(2)}, u32[]{:S(2)}) collective-permute-start(bf16[12,128,128]{2,1,0:T(8,128)(2,1)S(1)} %add_convert_fusion), channel_id=1, source_target_pairs={{0,2},{2,4},{4,6},{1,3},{3,5},{5,7},{8,10},{10,12},{12,14},{9,11},... | collective-permute-start | bytes 1179656 | tf_op jit(solution)/shard_map/ppermute | solution.py:600
  34.0 0.6 copy-start.5
  34.6 126.8 %all-to-all-start = ((bf16[8,256,512]{2,1,0:T(8,128)(2,1)}), bf16[8,256,512]{2,1,0:T(8,128)(2,1)}, u32[]{:S(2)}, u32[]{:S(2)}) async-start(bf16[8,256,512]{2,1,0:T(8,128)(2,1)} %get-tuple-element.88), calls=%async_computation | async-start | bytes 4194304 | tf_op jit(solution)/shard_map/all_to_all | solution.py:609
  39.2 0.8 copy-start.9
  72.8 19.0 %collective-permute-start.3 = (bf16[528,512]{1,0:T(8,128)(2,1)}, bf16[528,512]{1,0:T(8,128)(2,1)S(1)}, u32[]{:S(2)}, u32[]{:S(2)}) collective-permute-start(bf16[528,512]{1,0:T(8,128)(2,1)} %get-tuple-element.73), channel_id=1, source_target_pairs={{0,4},{1,0},{2,6},{3,2},{4,1},{5,5},{6,3},{7,7},{8,12},{9,8},{10,1... | collective-permute-start | bytes 1622024 | tf_op jit(solution)/shard_map/ppermute | solution.py:611
  78.8 36.6 %collective-permute-start.4 = (bf16[528,512]{1,0:T(8,128)(2,1)}, bf16[528,512]{1,0:T(8,128)(2,1)S(1)}, u32[]{:S(2)}, u32[]{:S(2)}) collective-permute-start(bf16[528,512]{1,0:T(8,128)(2,1)} %get-tuple-element.76), channel_id=1, source_target_pairs={{0,0},{1,4},{2,2},{3,6},{4,5},{5,1},{6,7},{7,3},{8,8},{9,12},{10,1... | collective-permute-start | bytes 1622024 | tf_op jit(solution)/shard_map/ppermute | solution.py:611
  82.7 73.7 %collective-permute-start.5 = (bf16[528,512]{1,0:T(8,128)(2,1)}, bf16[528,512]{1,0:T(8,128)(2,1)S(1)}, u32[]{:S(2)}, u32[]{:S(2)}) collective-permute-start(bf16[528,512]{1,0:T(8,128)(2,1)} %get-tuple-element.79), channel_id=1, source_target_pairs={{0,6},{1,2},{2,0},{3,4},{4,3},{5,7},{6,5},{7,1},{8,14},{9,10},{10,... | collective-permute-start | bytes 1622024 | tf_op jit(solution)/shard_map/ppermute | solution.py:611
  82.7 73.7 %collective-permute-start.6 = (bf16[528,512]{1,0:T(8,128)(2,1)}, bf16[528,512]{1,0:T(8,128)(2,1)}, u32[]{:S(2)}, u32[]{:S(2)}) collective-permute-start(bf16[528,512]{1,0:T(8,128)(2,1)} %get-tuple-element.82), channel_id=1, source_target_pairs={{0,2},{1,6},{2,4},{3,0},{4,7},{5,3},{6,1},{7,5},{8,10},{9,14},{10,... | collective-permute-start | bytes 1622024 | tf_op jit(solution)/shard_map/ppermute | solution.py:611
  84.2 98.6 %collective-permute-start.10 = (bf16[512,1024]{1,0:T(8,128)(2,1)}, bf16[512,1024]{1,0:T(8,128)(2,1)}, u32[]{:S(2)}, u32[]{:S(2)}) collective-permute-start(bf16[512,1024]{1,0:T(8,128)(2,1)} %get-tuple-element.87), channel_id=1, source_target_pairs={{0,0},{1,4},{2,2},{3,6},{4,5},{5,1},{6,7},{7,3},{8,8},{9,12},{10,1... | collective-permute-start | bytes 3145736 | tf_op jit(solution)/shard_map/ppermute | solution.py:617
  91.8 64.6 %copy-start.7 = (bf16[528,512]{1,0:T(8,128)(2,1)}, bf16[528,512]{1,0:T(8,128)(2,1)S(1)}, u32[]{:S(2)}) copy-start(bf16[528,512]{1,0:T(8,128)(2,1)S(1)} %collective-permute-done.3.refs_1_.refs_0_.refs_2_) | copy-start | bytes 1622020
  115.4 41.0 %copy-start.8 = (bf16[528,512]{1,0:T(8,128)(2,1)}, bf16[528,512]{1,0:T(8,128)(2,1)S(1)}, u32[]{:S(2)}) copy-start(bf16[528,512]{1,0:T(8,128)(2,1)S(1)} %collective-permute-done.4.refs_0_.refs_2_.refs_1_) | copy-start | bytes 1622020
  156.4 17.5 %copy-start.6 = (bf16[528,512]{1,0:T(8,128)(2,1)}, bf16[528,512]{1,0:T(8,128)(2,1)S(1)}, u32[]{:S(2)}) copy-start(bf16[528,512]{1,0:T(8,128)(2,1)S(1)} %collective-permute-done.5.refs_1_.refs_0_.refs_2_) | copy-start | bytes 1622020
  156.4 59.5 %collective-permute-start.9 = (bf16[512,1024]{1,0:T(8,128)(2,1)}, bf16[512,1024]{1,0:T(8,128)(2,1)}, u32[]{:S(2)}, u32[]{:S(2)}) collective-permute-start(bf16[512,1024]{1,0:T(8,128)(2,1)} %get-tuple-element.86), channel_id=1, source_target_pairs={{0,2},{1,6},{2,4},{3,0},{4,7},{5,3},{6,1},{7,5},{8,10},{9,14},{10,... | collective-permute-start | bytes 3145736 | tf_op jit(solution)/shard_map/ppermute | solution.py:617
  156.7 62.2 %collective-permute-start.7 = (bf16[512,1024]{1,0:T(8,128)(2,1)}, bf16[512,1024]{1,0:T(8,128)(2,1)}, u32[]{:S(2)}, u32[]{:S(2)}) collective-permute-start(bf16[512,1024]{1,0:T(8,128)(2,1)} %get-tuple-element.84), channel_id=1, source_target_pairs={{0,4},{1,0},{2,6},{3,2},{4,1},{5,5},{6,3},{7,7},{8,12},{9,8},{10,1... | collective-permute-start | bytes 3145736 | tf_op jit(solution)/shard_map/ppermute | solution.py:617
  161.3 61.6 %collective-permute-start.8 = (bf16[512,1024]{1,0:T(8,128)(2,1)}, bf16[512,1024]{1,0:T(8,128)(2,1)}, u32[]{:S(2)}, u32[]{:S(2)}) collective-permute-start(bf16[512,1024]{1,0:T(8,128)(2,1)} %get-tuple-element.85), channel_id=1, source_target_pairs={{0,6},{1,2},{2,0},{3,4},{4,3},{5,7},{6,5},{7,1},{8,14},{9,10},{10,... | collective-permute-start | bytes 3145736 | tf_op jit(solution)/shard_map/ppermute | solution.py:617

commit v7 on v6

--- a/solution.py
+++ b/solution.py
@@ -168,7 +168,7 @@
 def prelude(tab, doc_lengths, block_shard, decay, key, value):
     heads, tokens = decay.shape
     hp = pad8(heads)
-    tile = 2 * BLK
+    tile = BLK
     smem = pl.BlockSpec(memory_space=pltpu.SMEM)
     vmem = pl.BlockSpec(memory_space=pltpu.VMEM)
     hbm = pl.BlockSpec(memory_space=pl.ANY)
@@ -500,18 +500,20 @@
     extras, pieces = refs[: count * t], refs[count * t : count * (t + 1)]
     out_ref, extra, block, extra_in, block_in, block_out = refs[-6:]
     unit, rows = block.shape[2], per * BLK
+    part = BLK // 2
     moves, fetched, stores = [], [], []
     for j in range(count):
         for c in range(per):
+            b = j * per + c
             for k in range(t):
                 source = extras[j * t + k].at[pl.ds(rows, 16), pl.ds(c * lanes, lanes)]
-                moves.append(pltpu.make_async_copy(source, extra.at[j * per + c, k], extra_in.at[j * per + c, k]))
+                moves.append(pltpu.make_async_copy(source, extra.at[b, k], extra_in.at[b, k]))
                 moves[-1].start()
-    for j in range(count):
-        for c in range(per):
-            b = j * per + c
-            fetched.append(pltpu.make_async_copy(pieces[j].at[pl.ds(c * BLK, BLK)], block.at[b], block_in.at[b]))
-            fetched[-1].start()
+            for half in range(2):
+                source = pieces[j].at[pl.ds(c * BLK + half * part, part)]
+                target = block.at[b, pl.ds(half * part, part)]
+                fetched.append(pltpu.make_async_copy(source, target, block_in.at[b, half]))
+                fetched[-1].start()
     for j, op in enumerate(ops):
         row = table_ref[tab.row + op] * BLK
         left = pl.multiple_of(table_ref[tab.side + op] * local_width + lo * 128, 128)
@@ -520,17 +522,17 @@
             for k in range(t):
                 moves[b * t + k].wait()
             scale = row_scale([extra.at[b, k] for k in range(t)], features, lanes, lines)
-            fetched[b].wait()
-            for col in range(0, unit, 128):
-                cols = slice(col, col + 128)
-                block[b, :, cols] = (block[b, :, cols].astype(F32) * scale).astype(BF16)
-            top = pl.multiple_of(row + c * BLK, BLK)
-            stores.append(
-                pltpu.make_async_copy(
-                    block.at[b], out_ref.at[pl.ds(top, BLK), pl.ds(left, unit)], block_out.at[b]
-                )
-            )
-            stores[-1].start()
+            for half in range(2):
+                fetched[2 * b + half].wait()
+                span = slice(half * part, (half + 1) * part)
+                for col in range(0, unit, 128):
+                    cols = slice(col, col + 128)
+                    block[b, span, cols] = (block[b, span, cols].astype(F32) * scale[span]).astype(BF16)
+                top = pl.multiple_of(row + c * BLK + half * part, part)
+                target = out_ref.at[pl.ds(top, part), pl.ds(left, unit)]
+                source = block.at[b, pl.ds(half * part, part)]
+                stores.append(pltpu.make_async_copy(source, target, block_out.at[b, half]))
+                stores[-1].start()
     for store in stores:
         store.wait()
 
@@ -549,8 +551,8 @@
             pltpu.VMEM((blocks, tab.t, 16, lanes), BF16),
             pltpu.VMEM((blocks, BLK, pieces[0].shape[1]), BF16),
             pltpu.SemaphoreType.DMA((blocks, tab.t)),
-            pltpu.SemaphoreType.DMA((blocks,)),
-            pltpu.SemaphoreType.DMA((blocks,)),
+            pltpu.SemaphoreType.DMA((blocks, 2)),
+            pltpu.SemaphoreType.DMA((blocks, 2)),
         ],
         input_output_aliases={len(operands) - 1: 0},
         compiler_params=params(63 * 2**20),

time: 229 us -> 228 us (level)
  no operation moved by 1% of the time
where the time goes in v7:
time: 228 us; the launch traced here: 226 us
  waiting for transfers between devices  104 us (46%)
  Pallas kernels  75.5 us (33%)
  starting transfers between devices  34.7 us (15%)
  blocking collectives  9.62 us (4%)
    ppermute x4, waiting for transfers between devices, local(): lax.ppermute(gated[2][op], ('ctx', 'tp'), route(op))  67.9 us
    ppermute x4, waiting for transfers between devices, local(): middle.append(lax.ppermute(ready, ('ctx', 'tp'), route(op)))  34.2 us
    pallas_call x2, Pallas kernels, attend(): pl.pallas_call(functools.partial(attend_kernel, tab, lo, hp, count, last)...  29.7 us
    pallas_call x6, Pallas kernels, place(): pl.pallas_call(functools.partial(place_kernel, features, tab.t, len(piece...  17.7 us
    ppermute x4, starting transfers between devices, local(): lax.ppermute(gated[2][op], ('ctx', 'tp'), route(op))  11.6 us
    all_to_all x1, blocking collectives, local(): lax.all_to_all(head, 'tp', split_axis=0, concat_axis=0, tiled=True)  9.62 us
    pallas_call x1, Pallas kernels, attend_own(): pl.pallas_call(functools.partial(own_kernel, lo, hp, count), grid_spec=pl...  9.44 us
    ppermute x4, starting transfers between devices, local(): middle.append(lax.ppermute(ready, ('ctx', 'tp'), route(op)))  8.96 us
  transfers between devices with their start and end apart: 12, of which 6 were waited for; matrix products, arithmetic and copies ran while one was open for 0% of the time, Pallas kernels for 28%

profile of v7, /device:TPU:9, one launch (start us, length us, event | category | flops | bytes accessed | tf_op | source)
XLA Modules:
  0.0 226.1 jit_solution(14553616994935002426)
XLA Ops:
  0.0 8.0 %prelude.1 = (f32[48,2048]{1,0:T(8,128)S(1)}, f32[2048,128]{1,0:T(8,128)S(1)}, f32[8,2048]{1,0:T(8,128)S(1)}, f32[16,128]{1,0:T(8,128)S(1)}, s32[65]{0:T(128)S(1...) custom-call(s32[16]{0:T(128)} %len_ref.1, s32[32]{0:T(128)} %shard_ref.1, f32[16,2048]{1,0:T(8,128)} %decay_ref.1, ...), custom_call_target="tpu_custom_call" | custom-call | tf_op jit(solution)/shard_map/prelude/pallas_call | solution.py:176
  8.0 3.2 %collective-permute-start = (bf16[16,128,128]{2,1,0:T(8,128)(2,1)S(1)}, bf16[16,128,128]{2,1,0:T(8,128)(2,1)S(1)}, u32[]{:S(2)}, u32[]{:S(2)}) collective-permute-start(bf16[16,128,128]{2,1,0:T(8,128)(2,1)S(1)} %get-tuple-element.52), channel_id=1, source_target_pairs={{0,2},{2,4},{4,6},{1,3},{3,5},{5,7},{8,10},{10,12},{12,14},{9,11},... | collective-permute-start | bytes 1572872 | tf_op jit(solution)/shard_map/ppermute | solution.py:596
  11.4 9.4 %attend_own.1 = (f32[2048,512]{1,0:T(8,128)S(1)}, bf16[2048,512]{1,0:T(8,128)(2,1)S(1)}, f32[2048,512]{1,0:T(8,128)S(1)}) custom-call(s32[65]{0:T(128)S(1)} %get-tuple-element.47.refs_0_.table_ref, bf16[2048,2048]{1,0:T(8,128)(2,1)} %refs_1_.5, bf16[2048,2048]{1,0:T(8,128)(2,1)} %refs_2_.5, bf16[2048,2048]{1,0:T(8,128)(2,1)} %refs_3_.5, ...), custom_call_target="tpu_custom_call" | custom-call | flops 2147483648 | bytes 10485760 | tf_op jit(solution)/shard_map/attend_own/pallas_call | solution.py:251
  23.0 3.2 %collective-permute-start.2 = (bf16[4,128,128]{2,1,0:T(8,128)(2,1)S(1)}, bf16[4,128,128]{2,1,0:T(8,128)(2,1)S(1)}, u32[]{:S(2)}, u32[]{:S(2)}) collective-permute-start(bf16[4,128,128]{2,1,0:T(8,128)(2,1)S(1)} %add_convert_fusion.1), channel_id=1, source_target_pairs={{0,2},{2,4},{4,6},{1,3},{3,5},{5,7},{8,10},{10,12},{12,14},{9,11},... | collective-permute-start | bytes 393224 | tf_op jit(solution)/shard_map/ppermute | solution.py:602
  26.2 3.2 %collective-permute-start.1 = (bf16[12,128,128]{2,1,0:T(8,128)(2,1)S(1)}, bf16[12,128,128]{2,1,0:T(8,128)(2,1)S(1)}, u32[]{:S(2)}, u32[]{:S(2)}) collective-permute-start(bf16[12,128,128]{2,1,0:T(8,128)(2,1)S(1)} %add_convert_fusion), channel_id=1, source_target_pairs={{0,2},{2,4},{4,6},{1,3},{3,5},{5,7},{8,10},{10,12},{12,14},{9,11},... | collective-permute-start | bytes 1179656 | tf_op jit(solution)/shard_map/ppermute | solution.py:602
  29.4 4.1 %attend_entered.1 = (bf16[8,256,512]{2,1,0:T(8,128)(2,1)}, f32[8,1,256]{2,1,0:T(1,128)S(1)}) custom-call(s32[65]{0:T(128)S(1)} %get-tuple-element.47.refs_0_.table_ref, f32[2048,512]{1,0:T(8,128)S(1)} %get-tuple-element.58.own_ref, bf16[2048,512]{1,0:T(8,128)(2,1)S(1)} %get-tuple-element.59.query_ref, f32[2048,512]{1,0:T(8,128)S(1)} %get-tuple-element.60.factor_ref, ...), custom_call_target="tpu_custom_call" | custom-call | flops 512 | bytes 512 | tf_op jit(solution)/shard_map/attend_entered/pallas_call | solution.py:297
  34.2 4.6 %all-to-all-start = ((bf16[8,256,512]{2,1,0:T(8,128)(2,1)}), bf16[8,256,512]{2,1,0:T(8,128)(2,1)}, u32[]{:S(2)}, u32[]{:S(2)}) async-start(bf16[8,256,512]{2,1,0:T(8,128)(2,1)} %get-tuple-element.88), calls=%async_computation | async-start | bytes 4194304 | tf_op jit(solution)/shard_map/all_to_all | solution.py:611
  39.5 17.5 %attend.2 = (bf16[512,1024]{1,0:T(8,128)(2,1)}, bf16[512,1024]{1,0:T(8,128)(2,1)}, bf16[512,1024]{1,0:T(8,128)(2,1)}, bf16[512,1024]{1,0:T(8,128)(2,1)}, f32[8,1,256]{2,1,0:T(1,128)}) custom-call(s32[65]{0:T(128)} %copy-done.4, bf16[2048,2048]{1,0:T(8,128)(2,1)} %refs_1_.5, bf16[2048,2048]{1,0:T(8,128)(2,1)} %refs_2_.5, bf16[2048,2048]{1,0:T(8,128)(2,1)} %refs_3_.5, ...), custom_call_target="tpu_custom_call" | custom-call | flops 8589934592 | bytes 20971520 | tf_op jit(solution)/shard_map/attend/pallas_call | solution.py:401
  57.0 12.2 %attend.3 = (bf16[528,512]{1,0:T(8,128)(2,1)}, bf16[528,512]{1,0:T(8,128)(2,1)}, bf16[528,512]{1,0:T(8,128)(2,1)}, bf16[528,512]{1,0:T(8,128)(2,1)}, bf16[16,512...) custom-call(s32[65]{0:T(128)} %copy-done.4, ...), custom_call_target="tpu_custom_call" | custom-call | flops 4294967296 | bytes 10485760 | tf_op jit(solution)/shard_map/attend/pallas_call | solution.py:401
  69.2 3.1 %stitch.1 = (bf16[528,512]{1,0:T(8,128)(2,1)}, bf16[528,512]{1,0:T(8,128)(2,1)}, bf16[528,512]{1,0:T(8,128)(2,1)}, bf16[528,512]{1,0:T(8,128)(2,1)}) custom-call(bf16[16,512]{1,0:T(8,128)(2,1)} %get-tuple-element.65.refs_0_, bf16[16,512]{1,0:T(8,128)(2,1)} %get-tuple-element.66.refs_1_, ...), custom_call_target="tpu_custom_call", output_to_operand_aliasing={{0}: (4, {}), {1}: (5, {}), {2}: (6, {}), {3}: (7, {})} | custom-call | flops 128 | bytes 128 | tf_op jit(solution)/shard_map/stitch/pallas_call | solution.py:366
  72.4 6.0 %collective-permute-start.3 = (bf16[528,512]{1,0:T(8,128)(2,1)}, bf16[528,512]{1,0:T(8,128)(2,1)S(1)}, u32[]{:S(2)}, u32[]{:S(2)}) collective-permute-start(bf16[528,512]{1,0:T(8,128)(2,1)} %get-tuple-element.73), channel_id=1, source_target_pairs={{0,4},{1,0},{2,6},{3,2},{4,1},{5,5},{6,3},{7,7},{8,12},{9,8},{10,1... | collective-permute-start | bytes 1622024 | tf_op jit(solution)/shard_map/ppermute | solution.py:613
  78.4 4.1 %collective-permute-start.4 = (bf16[528,512]{1,0:T(8,128)(2,1)}, bf16[528,512]{1,0:T(8,128)(2,1)S(1)}, u32[]{:S(2)}, u32[]{:S(2)}) collective-permute-start(bf16[528,512]{1,0:T(8,128)(2,1)} %get-tuple-element.76), channel_id=1, source_target_pairs={{0,0},{1,4},{2,2},{3,6},{4,5},{5,1},{6,7},{7,3},{8,8},{9,12},{10,1... | collective-permute-start | bytes 1622024 | tf_op jit(solution)/shard_map/ppermute | solution.py:613
  84.0 4.1 %collective-permute-start.10 = (bf16[512,1024]{1,0:T(8,128)(2,1)}, bf16[512,1024]{1,0:T(8,128)(2,1)}, u32[]{:S(2)}, u32[]{:S(2)}) collective-permute-start(bf16[512,1024]{1,0:T(8,128)(2,1)} %get-tuple-element.87), channel_id=1, source_target_pairs={{0,0},{1,4},{2,2},{3,6},{4,5},{5,1},{6,7},{7,3},{8,8},{9,12},{10,1... | collective-permute-start | bytes 3145736 | tf_op jit(solution)/shard_map/ppermute | solution.py:619
  88.0 3.4 %collective-permute-done.3.refs_1_.refs_0_.refs_2_ = bf16[528,512]{1,0:T(8,128)(2,1)S(1)} collective-permute-done((bf16[528,512]{1,0:T(8,128)(2,1)}, bf16[528,512]{1,0:T(8,128)(2,1)S(1)}, u32[]{:S(2)}, u32[]{:S(2)}) %collective-permute-start.3) | collective-permute-done | bytes 540704 | tf_op jit(solution)/shard_map/ppermute | solution.py:613
  91.4 23.6 %collective-permute-done.4.refs_0_.refs_2_.refs_1_ = bf16[528,512]{1,0:T(8,128)(2,1)S(1)} collective-permute-done((bf16[528,512]{1,0:T(8,128)(2,1)}, bf16[528,512]{1,0:T(8,128)(2,1)S(1)}, u32[]{:S(2)}, u32[]{:S(2)}) %collective-permute-start.4) | collective-permute-done | bytes 540704 | tf_op jit(solution)/shard_map/ppermute | solution.py:613
  115.0 41.0 %collective-permute-done.5.refs_1_.refs_0_.refs_2_ = bf16[528,512]{1,0:T(8,128)(2,1)S(1)} collective-permute-done((bf16[528,512]{1,0:T(8,128)(2,1)}, bf16[528,512]{1,0:T(8,128)(2,1)S(1)}, u32[]{:S(2)}, u32[]{:S(2)}) %collective-permute-start.5) | collective-permute-done | bytes 540704 | tf_op jit(solution)/shard_map/ppermute | solution.py:613
  156.1 4.8 %collective-permute-start.7 = (bf16[512,1024]{1,0:T(8,128)(2,1)}, bf16[512,1024]{1,0:T(8,128)(2,1)}, u32[]{:S(2)}, u32[]{:S(2)}) collective-permute-start(bf16[512,1024]{1,0:T(8,128)(2,1)} %get-tuple-element.84), channel_id=1, source_target_pairs={{0,4},{1,0},{2,6},{3,2},{4,1},{5,5},{6,3},{7,7},{8,12},{9,8},{10,1... | collective-permute-start | bytes 3145736 | tf_op jit(solution)/shard_map/ppermute | solution.py:619
  160.9 9.6 %all_to_all.10 = bf16[8,256,512]{2,1,0:T(8,128)(2,1)} all-to-all(bf16[8,256,512]{2,1,0:T(8,128)(2,1)} %all-to-all-done), channel_id=1, replica_groups=mesh['dp'=4,'ctx'=4,'tp'=2] {'tp'}, dimensions={0} | all-to-all | bytes 4194304 | tf_op jit(solution)/shard_map/all_to_all | solution.py:612
  173.5 2.9 %place.7.refs_4_ = bf16[1024,4096]{1,0:T(8,128)(2,1)} custom-call(s32[65]{0:T(128)} %copy-done.4, bf16[528,512]{1,0:T(8,128)(2,1)} %collective-permute-done.6.refs_0_.refs_2_.refs_1_.refs_3_, bf16[528,512]{1,0:T(8,128)(2,1)} %copy-done.6, bf16[528,512]{1,0:T(8,128)(2,1)} %collective-permute-done.6.refs_0_.refs_2_.refs_1_.refs_3_, ...), custom_call_target="tpu_custom_call", output_to_operand_aliasing={{}: (5, {})} | custom-call | flops 1024 | bytes 1024 | tf_op jit(solution)/shard_map/place/pallas_call | solution.py:482
  182.3 3.0 %place.10.refs_3_ = bf16[1024,4096]{1,0:T(8,128)(2,1)} custom-call(s32[65]{0:T(128)} %copy-done.4, bf16[528,512]{1,0:T(8,128)(2,1)} %copy-done.8, bf16[528,512]{1,0:T(8,128)(2,1)} %copy-done.7, bf16[512,1024]{1,0:T(8,128)(2,1)} %collective-permute-done.10.refs_2_, bf16[1024,4096]{1,0:T(8,128)(2,1)} %place.9.refs_3_), custom_call_target="tpu_custom_call", output_to_operand_aliasing={{}: (4, {})} | custom-call | flops 1024 | bytes 1024 | tf_op jit(solution)/shard_map/place/pallas_call | solution.py:482
  185.3 30.2 %collective-permute-done.9.refs_2_ = bf16[512,1024]{1,0:T(8,128)(2,1)} collective-permute-done((bf16[512,1024]{1,0:T(8,128)(2,1)}, bf16[512,1024]{1,0:T(8,128)(2,1)}, u32[]{:S(2)}, u32[]{:S(2)}) %collective-permute-start.9) | collective-permute-done | bytes 1048608 | tf_op jit(solution)/shard_map/ppermute | solution.py:619
  215.5 3.0 %place.11.refs_6_ = bf16[1024,4096]{1,0:T(8,128)(2,1)} custom-call(s32[65]{0:T(128)} %copy-done.4, bf16[528,512]{1,0:T(8,128)(2,1)} %collective-permute-done.6.refs_0_.refs_2_.refs_1_.refs_3_, bf16[528,512]{1,0:T(8,128)(2,1)} %copy-done.6, bf16[512,1024]{1,0:T(8,128)(2,1)} %collective-permute-done.9.refs_2_, ...), custom_call_target="tpu_custom_call", output_to_operand_aliasing={{}: (4, {})} | custom-call | flops 1024 | bytes 1024 | tf_op jit(solution)/shard_map/place/pallas_call | solution.py:482
  218.4 4.0 %collective-permute-done.8.refs_5_ = bf16[512,1024]{1,0:T(8,128)(2,1)} collective-permute-done((bf16[512,1024]{1,0:T(8,128)(2,1)}, bf16[512,1024]{1,0:T(8,128)(2,1)}, u32[]{:S(2)}, u32[]{:S(2)}) %collective-permute-start.8) | collective-permute-done | bytes 1048608 | tf_op jit(solution)/shard_map/ppermute | solution.py:619
  222.5 3.5 %place_last.1 = bf16[1024,4096]{1,0:T(8,128)(2,1)} custom-call(s32[65]{0:T(128)} %copy-done.4, bf16[528,512]{1,0:T(8,128)(2,1)} %copy-done.7, bf16[528,512]{1,0:T(8,128)(2,1)} %copy-done.8, bf16[528,512]{1,0:T(8,128)(2,1)} %copy-done.6, bf16[528,512]{1,0:T(8,128)(2,1)} %collective-permute-done.6.refs_0_.refs_2_.refs_1_.refs_3_, ...), custom_call_target="tpu_custom_call", output_to_operand_aliasing={{}: (7, {})} | custom-call | flops 256 | bytes 256 | tf_op jit(solution)/shard_map/place_last/pallas_call | solution.py:545
  (38 shorter events, 14.2 us)
Async XLA Ops:
  0.0 11.4 %copy-start.3 = (f32[4096]{0:T(1024)S(1)}, f32[4096]{0:T(1024)}, u32[]{:S(2)}) copy-start(f32[4096]{0:T(1024)} %param.13) | copy-start | bytes 49156
  8.0 12.9 %copy-start.1 = (f32[48,2048]{1,0:T(8,128)}, f32[48,2048]{1,0:T(8,128)S(1)}, u32[]{:S(2)}) copy-start(f32[48,2048]{1,0:T(8,128)S(1)} %get-tuple-element.48.refs_6_) | copy-start | bytes 1179652
  8.0 12.9 %copy-start.2 = (f32[8,2048]{1,0:T(8,128)}, f32[8,2048]{1,0:T(8,128)S(1)}, u32[]{:S(2)}) copy-start(f32[8,2048]{1,0:T(8,128)S(1)} %get-tuple-element.50.refs_8_) | copy-start | bytes 196612
  8.0 21.4 %copy-start = (f32[2048,128]{1,0:T(8,128)}, f32[2048,128]{1,0:T(8,128)S(1)}, u32[]{:S(2)}) copy-start(f32[2048,128]{1,0:T(8,128)S(1)} %get-tuple-element.49.refs_7_.cols_ref) | copy-start | bytes 3145732
  8.0 21.4 %copy-start.4 = (s32[65]{0:T(128)}, s32[65]{0:T(128)S(1)}, u32[]{:S(2)}) copy-start(s32[65]{0:T(128)S(1)} %get-tuple-element.47.refs_0_.table_ref) | copy-start | bytes 784
  8.0 14.7 %collective-permute-start = (bf16[16,128,128]{2,1,0:T(8,128)(2,1)S(1)}, bf16[16,128,128]{2,1,0:T(8,128)(2,1)S(1)}, u32[]{:S(2)}, u32[]{:S(2)}) collective-permute-start(bf16[16,128,128]{2,1,0:T(8,128)(2,1)S(1)} %get-tuple-element.52), channel_id=1, source_target_pairs={{0,2},{2,4},{4,6},{1,3},{3,5},{5,7},{8,10},{10,12},{12,14},{9,11},... | collective-permute-start | bytes 1572872 | tf_op jit(solution)/shard_map/ppermute | solution.py:596
  23.0 6.4 %collective-permute-start.2 = (bf16[4,128,128]{2,1,0:T(8,128)(2,1)S(1)}, bf16[4,128,128]{2,1,0:T(8,128)(2,1)S(1)}, u32[]{:S(2)}, u32[]{:S(2)}) collective-permute-start(bf16[4,128,128]{2,1,0:T(8,128)(2,1)S(1)} %add_convert_fusion.1), channel_id=1, source_target_pairs={{0,2},{2,4},{4,6},{1,3},{3,5},{5,7},{8,10},{10,12},{12,14},{9,11},... | collective-permute-start | bytes 393224 | tf_op jit(solution)/shard_map/ppermute | solution.py:602
  26.2 12.6 %collective-permute-start.1 = (bf16[12,128,128]{2,1,0:T(8,128)(2,1)S(1)}, bf16[12,128,128]{2,1,0:T(8,128)(2,1)S(1)}, u32[]{:S(2)}, u32[]{:S(2)}) collective-permute-start(bf16[12,128,128]{2,1,0:T(8,128)(2,1)S(1)} %add_convert_fusion), channel_id=1, source_target_pairs={{0,2},{2,4},{4,6},{1,3},{3,5},{5,7},{8,10},{10,12},{12,14},{9,11},... | collective-permute-start | bytes 1179656 | tf_op jit(solution)/shard_map/ppermute | solution.py:602
  33.6 0.6 copy-start.5
  34.2 126.8 %all-to-all-start = ((bf16[8,256,512]{2,1,0:T(8,128)(2,1)}), bf16[8,256,512]{2,1,0:T(8,128)(2,1)}, u32[]{:S(2)}, u32[]{:S(2)}) async-start(bf16[8,256,512]{2,1,0:T(8,128)(2,1)} %get-tuple-element.88), calls=%async_computation | async-start | bytes 4194304 | tf_op jit(solution)/shard_map/all_to_all | solution.py:611
  38.8 0.8 copy-start.9
  72.4 19.0 %collective-permute-start.3 = (bf16[528,512]{1,0:T(8,128)(2,1)}, bf16[528,512]{1,0:T(8,128)(2,1)S(1)}, u32[]{:S(2)}, u32[]{:S(2)}) collective-permute-start(bf16[528,512]{1,0:T(8,128)(2,1)} %get-tuple-element.73), channel_id=1, source_target_pairs={{0,4},{1,0},{2,6},{3,2},{4,1},{5,5},{6,3},{7,7},{8,12},{9,8},{10,1... | collective-permute-start | bytes 1622024 | tf_op jit(solution)/shard_map/ppermute | solution.py:613
  78.4 36.6 %collective-permute-start.4 = (bf16[528,512]{1,0:T(8,128)(2,1)}, bf16[528,512]{1,0:T(8,128)(2,1)S(1)}, u32[]{:S(2)}, u32[]{:S(2)}) collective-permute-start(bf16[528,512]{1,0:T(8,128)(2,1)} %get-tuple-element.76), channel_id=1, source_target_pairs={{0,0},{1,4},{2,2},{3,6},{4,5},{5,1},{6,7},{7,3},{8,8},{9,12},{10,1... | collective-permute-start | bytes 1622024 | tf_op jit(solution)/shard_map/ppermute | solution.py:613
  82.4 73.5 %collective-permute-start.5 = (bf16[528,512]{1,0:T(8,128)(2,1)}, bf16[528,512]{1,0:T(8,128)(2,1)S(1)}, u32[]{:S(2)}, u32[]{:S(2)}) collective-permute-start(bf16[528,512]{1,0:T(8,128)(2,1)} %get-tuple-element.79), channel_id=1, source_target_pairs={{0,6},{1,2},{2,0},{3,4},{4,3},{5,7},{6,5},{7,1},{8,14},{9,10},{10,... | collective-permute-start | bytes 1622024 | tf_op jit(solution)/shard_map/ppermute | solution.py:613
  82.5 73.5 %collective-permute-start.6 = (bf16[528,512]{1,0:T(8,128)(2,1)}, bf16[528,512]{1,0:T(8,128)(2,1)}, u32[]{:S(2)}, u32[]{:S(2)}) collective-permute-start(bf16[528,512]{1,0:T(8,128)(2,1)} %get-tuple-element.82), channel_id=1, source_target_pairs={{0,2},{1,6},{2,4},{3,0},{4,7},{5,3},{6,1},{7,5},{8,10},{9,14},{10,... | collective-permute-start | bytes 1622024 | tf_op jit(solution)/shard_map/ppermute | solution.py:613
  84.0 98.4 %collective-permute-start.10 = (bf16[512,1024]{1,0:T(8,128)(2,1)}, bf16[512,1024]{1,0:T(8,128)(2,1)}, u32[]{:S(2)}, u32[]{:S(2)}) collective-permute-start(bf16[512,1024]{1,0:T(8,128)(2,1)} %get-tuple-element.87), channel_id=1, source_target_pairs={{0,0},{1,4},{2,2},{3,6},{4,5},{5,1},{6,7},{7,3},{8,8},{9,12},{10,1... | collective-permute-start | bytes 3145736 | tf_op jit(solution)/shard_map/ppermute | solution.py:619
  91.4 64.6 %copy-start.7 = (bf16[528,512]{1,0:T(8,128)(2,1)}, bf16[528,512]{1,0:T(8,128)(2,1)S(1)}, u32[]{:S(2)}) copy-start(bf16[528,512]{1,0:T(8,128)(2,1)S(1)} %collective-permute-done.3.refs_1_.refs_0_.refs_2_) | copy-start | bytes 1622020
  115.0 41.0 %copy-start.8 = (bf16[528,512]{1,0:T(8,128)(2,1)}, bf16[528,512]{1,0:T(8,128)(2,1)S(1)}, u32[]{:S(2)}) copy-start(bf16[528,512]{1,0:T(8,128)(2,1)S(1)} %collective-permute-done.4.refs_0_.refs_2_.refs_1_) | copy-start | bytes 1622020
  156.0 17.5 %copy-start.6 = (bf16[528,512]{1,0:T(8,128)(2,1)}, bf16[528,512]{1,0:T(8,128)(2,1)S(1)}, u32[]{:S(2)}) copy-start(bf16[528,512]{1,0:T(8,128)(2,1)S(1)} %collective-permute-done.5.refs_1_.refs_0_.refs_2_) | copy-start | bytes 1622020
  156.0 59.5 %collective-permute-start.9 = (bf16[512,1024]{1,0:T(8,128)(2,1)}, bf16[512,1024]{1,0:T(8,128)(2,1)}, u32[]{:S(2)}, u32[]{:S(2)}) collective-permute-start(bf16[512,1024]{1,0:T(8,128)(2,1)} %get-tuple-element.86), channel_id=1, source_target_pairs={{0,2},{1,6},{2,4},{3,0},{4,7},{5,3},{6,1},{7,5},{8,10},{9,14},{10,... | collective-permute-start | bytes 3145736 | tf_op jit(solution)/shard_map/ppermute | solution.py:619
  156.1 62.4 %collective-permute-start.7 = (bf16[512,1024]{1,0:T(8,128)(2,1)}, bf16[512,1024]{1,0:T(8,128)(2,1)}, u32[]{:S(2)}, u32[]{:S(2)}) collective-permute-start(bf16[512,1024]{1,0:T(8,128)(2,1)} %get-tuple-element.84), channel_id=1, source_target_pairs={{0,4},{1,0},{2,6},{3,2},{4,1},{5,5},{6,3},{7,7},{8,12},{9,8},{10,1... | collective-permute-start | bytes 3145736 | tf_op jit(solution)/shard_map/ppermute | solution.py:619
  160.8 61.6 %collective-permute-start.8 = (bf16[512,1024]{1,0:T(8,128)(2,1)}, bf16[512,1024]{1,0:T(8,128)(2,1)}, u32[]{:S(2)}, u32[]{:S(2)}) collective-permute-start(bf16[512,1024]{1,0:T(8,128)(2,1)} %get-tuple-element.85), channel_id=1, source_target_pairs={{0,6},{1,2},{2,0},{3,4},{4,3},{5,7},{6,5},{7,1},{8,14},{9,10},{10,... | collective-permute-start | bytes 3145736 | tf_op jit(solution)/shard_map/ppermute | solution.py:619

commit v8 on v7

--- a/solution.py
+++ b/solution.py
@@ -275,7 +275,8 @@
     )(table, *map(in_hbm, (query, key, value, gate)), gain, rows, cols, docs)
 
 
-def enter_kernel(tab, lo, hp, count, table_ref, own_ref, query_ref, factor_ref, cols_ref, state_ref, out_ref, square_ref):
+def enter_kernel(tab, lo, hp, count, table_ref, own_ref, query_ref, factor_ref, cols_ref, state_ref, out_ref, square_ref, gated, stored):
+    stores = []
     for c in range(tab.chunks):
         span = slice(c * BLK, (c + 1) * BLK)
         place, slot = table_ref[tab.shard + c], table_ref[tab.slot + c]
@@ -286,9 +287,13 @@
             column = 2 * hp + 8 + lo + h
             attended = own_ref[span, cols] + cols_ref[span, column : column + 1] * reached
             attended = attended.astype(BF16).astype(F32)
-            out_ref[place, :, cols] = (attended * factor_ref[span, cols]).astype(BF16)
+            gated[span, cols] = (attended * factor_ref[span, cols]).astype(BF16)
             square = square + attended * attended
         square_ref[slot] = jnp.sum(square.T, axis=0, keepdims=True)
+        stores.append(pltpu.make_async_copy(gated.at[pl.ds(c * BLK, BLK)], out_ref.at[place], stored.at[c]))
+        stores[-1].start()
+    for store in stores:
+        store.wait()
 
 
 def attend_entered(tab, table, own, cols, entering, lo, count, hp):
@@ -297,10 +302,14 @@
     return pl.pallas_call(
         functools.partial(enter_kernel, tab, lo, hp, count),
         in_specs=[pl.BlockSpec(memory_space=pltpu.SMEM)] + [vmem] * 5,
-        out_specs=[vmem] * 2,
+        out_specs=[pl.BlockSpec(memory_space=pl.ANY), vmem],
         out_shape=[
             jax.ShapeDtypeStruct((tab.chunks, BLK, width), BF16),
             jax.ShapeDtypeStruct((tab.chunks, 1, BLK), F32),
+        ],
+        scratch_shapes=[
+            pltpu.VMEM((tab.chunks * BLK, width), BF16),
+            pltpu.SemaphoreType.DMA((tab.chunks,)),
         ],
         compiler_params=params(24 * 2**20),
         cost_estimate=pl.CostEstimate(flops=width, bytes_accessed=width, transcendentals=0),

time: 228 us -> 227 us (level)
  no operation moved by 1% of the time
where the time goes in v8:
time: 227 us; the launch traced here: 225 us
  waiting for transfers between devices  104 us (46%)
  Pallas kernels  74.8 us (33%)
  starting transfers between devices  34.8 us (15%)
  blocking collectives  9.62 us (4%)
    ppermute x4, waiting for transfers between devices, local(): lax.ppermute(gated[2][op], ('ctx', 'tp'), route(op))  67.9 us
    ppermute x4, waiting for transfers between devices, local(): middle.append(lax.ppermute(ready, ('ctx', 'tp'), route(op)))  34.2 us
    pallas_call x2, Pallas kernels, attend(): pl.pallas_call(functools.partial(attend_kernel, tab, lo, hp, count, last)...  29.7 us
    pallas_call x6, Pallas kernels, place(): pl.pallas_call(functools.partial(place_kernel, features, tab.t, len(piece...  17.7 us
    ppermute x4, starting transfers between devices, local(): lax.ppermute(gated[2][op], ('ctx', 'tp'), route(op))  11.6 us
    all_to_all x1, blocking collectives, local(): lax.all_to_all(head, 'tp', split_axis=0, concat_axis=0, tiled=True)  9.62 us
    pallas_call x1, Pallas kernels, attend_own(): pl.pallas_call(functools.partial(own_kernel, lo, hp, count), grid_spec=pl...  9.44 us
    ppermute x4, starting transfers between devices, local(): middle.append(lax.ppermute(ready, ('ctx', 'tp'), route(op)))  8.97 us
  transfers between devices with their start and end apart: 12, of which 6 were waited for; matrix products, arithmetic and copies ran while one was open for 0% of the time, Pallas kernels for 28%

profile of v8, /device:TPU:9, one launch (start us, length us, event | category | flops | bytes accessed | tf_op | source)
XLA Modules:
  0.0 225.4 jit_solution(5211148473072560093)
XLA Ops:
  0.0 8.0 %prelude.1 = (f32[48,2048]{1,0:T(8,128)S(1)}, f32[2048,128]{1,0:T(8,128)S(1)}, f32[8,2048]{1,0:T(8,128)S(1)}, f32[16,128]{1,0:T(8,128)S(1)}, s32[65]{0:T(128)S(1...) custom-call(s32[16]{0:T(128)} %len_ref.1, s32[32]{0:T(128)} %shard_ref.1, f32[16,2048]{1,0:T(8,128)} %decay_ref.1, ...), custom_call_target="tpu_custom_call" | custom-call | tf_op jit(solution)/shard_map/prelude/pallas_call | solution.py:176
  8.0 3.2 %collective-permute-start = (bf16[16,128,128]{2,1,0:T(8,128)(2,1)S(1)}, bf16[16,128,128]{2,1,0:T(8,128)(2,1)S(1)}, u32[]{:S(2)}, u32[]{:S(2)}) collective-permute-start(bf16[16,128,128]{2,1,0:T(8,128)(2,1)S(1)} %get-tuple-element.52), channel_id=1, source_target_pairs={{0,2},{2,4},{4,6},{1,3},{3,5},{5,7},{8,10},{10,12},{12,14},{9,11},... | collective-permute-start | bytes 1572872 | tf_op jit(solution)/shard_map/ppermute | solution.py:605
  11.4 9.4 %attend_own.1 = (f32[2048,512]{1,0:T(8,128)S(1)}, bf16[2048,512]{1,0:T(8,128)(2,1)S(1)}, f32[2048,512]{1,0:T(8,128)S(1)}) custom-call(s32[65]{0:T(128)S(1)} %get-tuple-element.47.refs_0_.table_ref, bf16[2048,2048]{1,0:T(8,128)(2,1)} %refs_1_.5, bf16[2048,2048]{1,0:T(8,128)(2,1)} %refs_2_.5, bf16[2048,2048]{1,0:T(8,128)(2,1)} %refs_3_.5, ...), custom_call_target="tpu_custom_call" | custom-call | flops 2147483648 | bytes 10485760 | tf_op jit(solution)/shard_map/attend_own/pallas_call | solution.py:251
  23.0 3.2 %collective-permute-start.2 = (bf16[4,128,128]{2,1,0:T(8,128)(2,1)S(1)}, bf16[4,128,128]{2,1,0:T(8,128)(2,1)S(1)}, u32[]{:S(2)}, u32[]{:S(2)}) collective-permute-start(bf16[4,128,128]{2,1,0:T(8,128)(2,1)S(1)} %add_convert_fusion.1), channel_id=1, source_target_pairs={{0,2},{2,4},{4,6},{1,3},{3,5},{5,7},{8,10},{10,12},{12,14},{9,11},... | collective-permute-start | bytes 393224 | tf_op jit(solution)/shard_map/ppermute | solution.py:611
  26.2 3.2 %collective-permute-start.1 = (bf16[12,128,128]{2,1,0:T(8,128)(2,1)S(1)}, bf16[12,128,128]{2,1,0:T(8,128)(2,1)S(1)}, u32[]{:S(2)}, u32[]{:S(2)}) collective-permute-start(bf16[12,128,128]{2,1,0:T(8,128)(2,1)S(1)} %add_convert_fusion), channel_id=1, source_target_pairs={{0,2},{2,4},{4,6},{1,3},{3,5},{5,7},{8,10},{10,12},{12,14},{9,11},... | collective-permute-start | bytes 1179656 | tf_op jit(solution)/shard_map/ppermute | solution.py:611
  29.4 3.4 %attend_entered.1 = (bf16[8,256,512]{2,1,0:T(8,128)(2,1)}, f32[8,1,256]{2,1,0:T(1,128)S(1)}) custom-call(s32[65]{0:T(128)S(1)} %get-tuple-element.47.refs_0_.table_ref, f32[2048,512]{1,0:T(8,128)S(1)} %get-tuple-element.58.own_ref, bf16[2048,512]{1,0:T(8,128)(2,1)S(1)} %get-tuple-element.59.query_ref, f32[2048,512]{1,0:T(8,128)S(1)} %get-tuple-element.60.factor_ref, ...), custom_call_target="tpu_custom_call" | custom-call | flops 512 | bytes 512 | tf_op jit(solution)/shard_map/attend_entered/pallas_call | solution.py:302
  33.4 4.6 %all-to-all-start = ((bf16[8,256,512]{2,1,0:T(8,128)(2,1)}), bf16[8,256,512]{2,1,0:T(8,128)(2,1)}, u32[]{:S(2)}, u32[]{:S(2)}) async-start(bf16[8,256,512]{2,1,0:T(8,128)(2,1)} %get-tuple-element.88), calls=%async_computation | async-start | bytes 4194304 | tf_op jit(solution)/shard_map/all_to_all | solution.py:620
  38.8 17.5 %attend.2 = (bf16[512,1024]{1,0:T(8,128)(2,1)}, bf16[512,1024]{1,0:T(8,128)(2,1)}, bf16[512,1024]{1,0:T(8,128)(2,1)}, bf16[512,1024]{1,0:T(8,128)(2,1)}, f32[8,1,256]{2,1,0:T(1,128)}) custom-call(s32[65]{0:T(128)} %copy-done.4, bf16[2048,2048]{1,0:T(8,128)(2,1)} %refs_1_.5, bf16[2048,2048]{1,0:T(8,128)(2,1)} %refs_2_.5, bf16[2048,2048]{1,0:T(8,128)(2,1)} %refs_3_.5, ...), custom_call_target="tpu_custom_call" | custom-call | flops 8589934592 | bytes 20971520 | tf_op jit(solution)/shard_map/attend/pallas_call | solution.py:410
  56.3 12.2 %attend.3 = (bf16[528,512]{1,0:T(8,128)(2,1)}, bf16[528,512]{1,0:T(8,128)(2,1)}, bf16[528,512]{1,0:T(8,128)(2,1)}, bf16[528,512]{1,0:T(8,128)(2,1)}, bf16[16,512...) custom-call(s32[65]{0:T(128)} %copy-done.4, ...), custom_call_target="tpu_custom_call" | custom-call | flops 4294967296 | bytes 10485760 | tf_op jit(solution)/shard_map/attend/pallas_call | solution.py:410
  68.5 3.1 %stitch.1 = (bf16[528,512]{1,0:T(8,128)(2,1)}, bf16[528,512]{1,0:T(8,128)(2,1)}, bf16[528,512]{1,0:T(8,128)(2,1)}, bf16[528,512]{1,0:T(8,128)(2,1)}) custom-call(bf16[16,512]{1,0:T(8,128)(2,1)} %get-tuple-element.65.refs_0_, bf16[16,512]{1,0:T(8,128)(2,1)} %get-tuple-element.66.refs_1_, ...), custom_call_target="tpu_custom_call", output_to_operand_aliasing={{0}: (4, {}), {1}: (5, {}), {2}: (6, {}), {3}: (7, {})} | custom-call | flops 128 | bytes 128 | tf_op jit(solution)/shard_map/stitch/pallas_call | solution.py:375
  71.6 6.0 %collective-permute-start.3 = (bf16[528,512]{1,0:T(8,128)(2,1)}, bf16[528,512]{1,0:T(8,128)(2,1)S(1)}, u32[]{:S(2)}, u32[]{:S(2)}) collective-permute-start(bf16[528,512]{1,0:T(8,128)(2,1)} %get-tuple-element.73), channel_id=1, source_target_pairs={{0,4},{1,0},{2,6},{3,2},{4,1},{5,5},{6,3},{7,7},{8,12},{9,8},{10,1... | collective-permute-start | bytes 1622024 | tf_op jit(solution)/shard_map/ppermute | solution.py:622
  77.6 4.1 %collective-permute-start.4 = (bf16[528,512]{1,0:T(8,128)(2,1)}, bf16[528,512]{1,0:T(8,128)(2,1)S(1)}, u32[]{:S(2)}, u32[]{:S(2)}) collective-permute-start(bf16[528,512]{1,0:T(8,128)(2,1)} %get-tuple-element.76), channel_id=1, source_target_pairs={{0,0},{1,4},{2,2},{3,6},{4,5},{5,1},{6,7},{7,3},{8,8},{9,12},{10,1... | collective-permute-start | bytes 1622024 | tf_op jit(solution)/shard_map/ppermute | solution.py:622
  83.2 4.1 %collective-permute-start.10 = (bf16[512,1024]{1,0:T(8,128)(2,1)}, bf16[512,1024]{1,0:T(8,128)(2,1)}, u32[]{:S(2)}, u32[]{:S(2)}) collective-permute-start(bf16[512,1024]{1,0:T(8,128)(2,1)} %get-tuple-element.87), channel_id=1, source_target_pairs={{0,0},{1,4},{2,2},{3,6},{4,5},{5,1},{6,7},{7,3},{8,8},{9,12},{10,1... | collective-permute-start | bytes 3145736 | tf_op jit(solution)/shard_map/ppermute | solution.py:628
  87.3 3.4 %collective-permute-done.3.refs_1_.refs_0_.refs_2_ = bf16[528,512]{1,0:T(8,128)(2,1)S(1)} collective-permute-done((bf16[528,512]{1,0:T(8,128)(2,1)}, bf16[528,512]{1,0:T(8,128)(2,1)S(1)}, u32[]{:S(2)}, u32[]{:S(2)}) %collective-permute-start.3) | collective-permute-done | bytes 540704 | tf_op jit(solution)/shard_map/ppermute | solution.py:622
  90.7 23.5 %collective-permute-done.4.refs_0_.refs_2_.refs_1_ = bf16[528,512]{1,0:T(8,128)(2,1)S(1)} collective-permute-done((bf16[528,512]{1,0:T(8,128)(2,1)}, bf16[528,512]{1,0:T(8,128)(2,1)S(1)}, u32[]{:S(2)}, u32[]{:S(2)}) %collective-permute-start.4) | collective-permute-done | bytes 540704 | tf_op jit(solution)/shard_map/ppermute | solution.py:622
  114.2 41.0 %collective-permute-done.5.refs_1_.refs_0_.refs_2_ = bf16[528,512]{1,0:T(8,128)(2,1)S(1)} collective-permute-done((bf16[528,512]{1,0:T(8,128)(2,1)}, bf16[528,512]{1,0:T(8,128)(2,1)S(1)}, u32[]{:S(2)}, u32[]{:S(2)}) %collective-permute-start.5) | collective-permute-done | bytes 540704 | tf_op jit(solution)/shard_map/ppermute | solution.py:622
  155.3 4.8 %collective-permute-start.7 = (bf16[512,1024]{1,0:T(8,128)(2,1)}, bf16[512,1024]{1,0:T(8,128)(2,1)}, u32[]{:S(2)}, u32[]{:S(2)}) collective-permute-start(bf16[512,1024]{1,0:T(8,128)(2,1)} %get-tuple-element.84), channel_id=1, source_target_pairs={{0,4},{1,0},{2,6},{3,2},{4,1},{5,5},{6,3},{7,7},{8,12},{9,8},{10,1... | collective-permute-start | bytes 3145736 | tf_op jit(solution)/shard_map/ppermute | solution.py:628
  160.2 9.6 %all_to_all.10 = bf16[8,256,512]{2,1,0:T(8,128)(2,1)} all-to-all(bf16[8,256,512]{2,1,0:T(8,128)(2,1)} %all-to-all-done), channel_id=1, replica_groups=mesh['dp'=4,'ctx'=4,'tp'=2] {'tp'}, dimensions={0} | all-to-all | bytes 4194304 | tf_op jit(solution)/shard_map/all_to_all | solution.py:621
  172.8 2.9 %place.7.refs_4_ = bf16[1024,4096]{1,0:T(8,128)(2,1)} custom-call(s32[65]{0:T(128)} %copy-done.4, bf16[528,512]{1,0:T(8,128)(2,1)} %collective-permute-done.6.refs_0_.refs_2_.refs_1_.refs_3_, bf16[528,512]{1,0:T(8,128)(2,1)} %copy-done.6, bf16[528,512]{1,0:T(8,128)(2,1)} %collective-permute-done.6.refs_0_.refs_2_.refs_1_.refs_3_, ...), custom_call_target="tpu_custom_call", output_to_operand_aliasing={{}: (5, {})} | custom-call | flops 1024 | bytes 1024 | tf_op jit(solution)/shard_map/place/pallas_call | solution.py:491
  181.6 3.0 %place.10.refs_3_ = bf16[1024,4096]{1,0:T(8,128)(2,1)} custom-call(s32[65]{0:T(128)} %copy-done.4, bf16[528,512]{1,0:T(8,128)(2,1)} %copy-done.8, bf16[528,512]{1,0:T(8,128)(2,1)} %copy-done.7, bf16[512,1024]{1,0:T(8,128)(2,1)} %collective-permute-done.10.refs_2_, bf16[1024,4096]{1,0:T(8,128)(2,1)} %place.9.refs_3_), custom_call_target="tpu_custom_call", output_to_operand_aliasing={{}: (4, {})} | custom-call | flops 1024 | bytes 1024 | tf_op jit(solution)/shard_map/place/pallas_call | solution.py:491
  184.6 30.2 %collective-permute-done.9.refs_2_ = bf16[512,1024]{1,0:T(8,128)(2,1)} collective-permute-done((bf16[512,1024]{1,0:T(8,128)(2,1)}, bf16[512,1024]{1,0:T(8,128)(2,1)}, u32[]{:S(2)}, u32[]{:S(2)}) %collective-permute-start.9) | collective-permute-done | bytes 1048608 | tf_op jit(solution)/shard_map/ppermute | solution.py:628
  214.7 3.0 %place.11.refs_6_ = bf16[1024,4096]{1,0:T(8,128)(2,1)} custom-call(s32[65]{0:T(128)} %copy-done.4, bf16[528,512]{1,0:T(8,128)(2,1)} %collective-permute-done.6.refs_0_.refs_2_.refs_1_.refs_3_, bf16[528,512]{1,0:T(8,128)(2,1)} %copy-done.6, bf16[512,1024]{1,0:T(8,128)(2,1)} %collective-permute-done.9.refs_2_, ...), custom_call_target="tpu_custom_call", output_to_operand_aliasing={{}: (4, {})} | custom-call | flops 1024 | bytes 1024 | tf_op jit(solution)/shard_map/place/pallas_call | solution.py:491
  217.7 4.1 %collective-permute-done.8.refs_5_ = bf16[512,1024]{1,0:T(8,128)(2,1)} collective-permute-done((bf16[512,1024]{1,0:T(8,128)(2,1)}, bf16[512,1024]{1,0:T(8,128)(2,1)}, u32[]{:S(2)}, u32[]{:S(2)}) %collective-permute-start.8) | collective-permute-done | bytes 1048608 | tf_op jit(solution)/shard_map/ppermute | solution.py:628
  221.7 3.5 %place_last.1 = bf16[1024,4096]{1,0:T(8,128)(2,1)} custom-call(s32[65]{0:T(128)} %copy-done.4, bf16[528,512]{1,0:T(8,128)(2,1)} %copy-done.7, bf16[528,512]{1,0:T(8,128)(2,1)} %copy-done.8, bf16[528,512]{1,0:T(8,128)(2,1)} %copy-done.6, bf16[528,512]{1,0:T(8,128)(2,1)} %collective-permute-done.6.refs_0_.refs_2_.refs_1_.refs_3_, ...), custom_call_target="tpu_custom_call", output_to_operand_aliasing={{}: (7, {})} | custom-call | flops 256 | bytes 256 | tf_op jit(solution)/shard_map/place_last/pallas_call | solution.py:554
  (38 shorter events, 14.2 us)
Async XLA Ops:
  0.0 11.4 %copy-start.3 = (f32[4096]{0:T(1024)S(1)}, f32[4096]{0:T(1024)}, u32[]{:S(2)}) copy-start(f32[4096]{0:T(1024)} %param.13) | copy-start | bytes 49156
  8.0 12.9 %copy-start.1 = (f32[48,2048]{1,0:T(8,128)}, f32[48,2048]{1,0:T(8,128)S(1)}, u32[]{:S(2)}) copy-start(f32[48,2048]{1,0:T(8,128)S(1)} %get-tuple-element.48.refs_6_) | copy-start | bytes 1179652
  8.0 12.9 %copy-start.2 = (f32[8,2048]{1,0:T(8,128)}, f32[8,2048]{1,0:T(8,128)S(1)}, u32[]{:S(2)}) copy-start(f32[8,2048]{1,0:T(8,128)S(1)} %get-tuple-element.50.refs_8_) | copy-start | bytes 196612
  8.0 21.4 %copy-start = (f32[2048,128]{1,0:T(8,128)}, f32[2048,128]{1,0:T(8,128)S(1)}, u32[]{:S(2)}) copy-start(f32[2048,128]{1,0:T(8,128)S(1)} %get-tuple-element.49.refs_7_.cols_ref) | copy-start | bytes 3145732
  8.0 21.4 %copy-start.4 = (s32[65]{0:T(128)}, s32[65]{0:T(128)S(1)}, u32[]{:S(2)}) copy-start(s32[65]{0:T(128)S(1)} %get-tuple-element.47.refs_0_.table_ref) | copy-start | bytes 784
  8.0 14.7 %collective-permute-start = (bf16[16,128,128]{2,1,0:T(8,128)(2,1)S(1)}, bf16[16,128,128]{2,1,0:T(8,128)(2,1)S(1)}, u32[]{:S(2)}, u32[]{:S(2)}) collective-permute-start(bf16[16,128,128]{2,1,0:T(8,128)(2,1)S(1)} %get-tuple-element.52), channel_id=1, source_target_pairs={{0,2},{2,4},{4,6},{1,3},{3,5},{5,7},{8,10},{10,12},{12,14},{9,11},... | collective-permute-start | bytes 1572872 | tf_op jit(solution)/shard_map/ppermute | solution.py:605
  23.0 6.4 %collective-permute-start.2 = (bf16[4,128,128]{2,1,0:T(8,128)(2,1)S(1)}, bf16[4,128,128]{2,1,0:T(8,128)(2,1)S(1)}, u32[]{:S(2)}, u32[]{:S(2)}) collective-permute-start(bf16[4,128,128]{2,1,0:T(8,128)(2,1)S(1)} %add_convert_fusion.1), channel_id=1, source_target_pairs={{0,2},{2,4},{4,6},{1,3},{3,5},{5,7},{8,10},{10,12},{12,14},{9,11},... | collective-permute-start | bytes 393224 | tf_op jit(solution)/shard_map/ppermute | solution.py:611
  26.2 11.8 %collective-permute-start.1 = (bf16[12,128,128]{2,1,0:T(8,128)(2,1)S(1)}, bf16[12,128,128]{2,1,0:T(8,128)(2,1)S(1)}, u32[]{:S(2)}, u32[]{:S(2)}) collective-permute-start(bf16[12,128,128]{2,1,0:T(8,128)(2,1)S(1)} %add_convert_fusion), channel_id=1, source_target_pairs={{0,2},{2,4},{4,6},{1,3},{3,5},{5,7},{8,10},{10,12},{12,14},{9,11},... | collective-permute-start | bytes 1179656 | tf_op jit(solution)/shard_map/ppermute | solution.py:611
  32.8 0.6 copy-start.5
  33.4 126.8 %all-to-all-start = ((bf16[8,256,512]{2,1,0:T(8,128)(2,1)}), bf16[8,256,512]{2,1,0:T(8,128)(2,1)}, u32[]{:S(2)}, u32[]{:S(2)}) async-start(bf16[8,256,512]{2,1,0:T(8,128)(2,1)} %get-tuple-element.88), calls=%async_computation | async-start | bytes 4194304 | tf_op jit(solution)/shard_map/all_to_all | solution.py:620
  38.0 0.8 copy-start.9
  71.6 19.1 %collective-permute-start.3 = (bf16[528,512]{1,0:T(8,128)(2,1)}, bf16[528,512]{1,0:T(8,128)(2,1)S(1)}, u32[]{:S(2)}, u32[]{:S(2)}) collective-permute-start(bf16[528,512]{1,0:T(8,128)(2,1)} %get-tuple-element.73), channel_id=1, source_target_pairs={{0,4},{1,0},{2,6},{3,2},{4,1},{5,5},{6,3},{7,7},{8,12},{9,8},{10,1... | collective-permute-start | bytes 1622024 | tf_op jit(solution)/shard_map/ppermute | solution.py:622
  77.6 36.6 %collective-permute-start.4 = (bf16[528,512]{1,0:T(8,128)(2,1)}, bf16[528,512]{1,0:T(8,128)(2,1)S(1)}, u32[]{:S(2)}, u32[]{:S(2)}) collective-permute-start(bf16[528,512]{1,0:T(8,128)(2,1)} %get-tuple-element.76), channel_id=1, source_target_pairs={{0,0},{1,4},{2,2},{3,6},{4,5},{5,1},{6,7},{7,3},{8,8},{9,12},{10,1... | collective-permute-start | bytes 1622024 | tf_op jit(solution)/shard_map/ppermute | solution.py:622
  81.7 73.5 %collective-permute-start.5 = (bf16[528,512]{1,0:T(8,128)(2,1)}, bf16[528,512]{1,0:T(8,128)(2,1)S(1)}, u32[]{:S(2)}, u32[]{:S(2)}) collective-permute-start(bf16[528,512]{1,0:T(8,128)(2,1)} %get-tuple-element.79), channel_id=1, source_target_pairs={{0,6},{1,2},{2,0},{3,4},{4,3},{5,7},{6,5},{7,1},{8,14},{9,10},{10,... | collective-permute-start | bytes 1622024 | tf_op jit(solution)/shard_map/ppermute | solution.py:622
  81.8 73.5 %collective-permute-start.6 = (bf16[528,512]{1,0:T(8,128)(2,1)}, bf16[528,512]{1,0:T(8,128)(2,1)}, u32[]{:S(2)}, u32[]{:S(2)}) collective-permute-start(bf16[528,512]{1,0:T(8,128)(2,1)} %get-tuple-element.82), channel_id=1, source_target_pairs={{0,2},{1,6},{2,4},{3,0},{4,7},{5,3},{6,1},{7,5},{8,10},{9,14},{10,... | collective-permute-start | bytes 1622024 | tf_op jit(solution)/shard_map/ppermute | solution.py:622
  83.2 98.4 %collective-permute-start.10 = (bf16[512,1024]{1,0:T(8,128)(2,1)}, bf16[512,1024]{1,0:T(8,128)(2,1)}, u32[]{:S(2)}, u32[]{:S(2)}) collective-permute-start(bf16[512,1024]{1,0:T(8,128)(2,1)} %get-tuple-element.87), channel_id=1, source_target_pairs={{0,0},{1,4},{2,2},{3,6},{4,5},{5,1},{6,7},{7,3},{8,8},{9,12},{10,1... | collective-permute-start | bytes 3145736 | tf_op jit(solution)/shard_map/ppermute | solution.py:628
  90.7 64.6 %copy-start.7 = (bf16[528,512]{1,0:T(8,128)(2,1)}, bf16[528,512]{1,0:T(8,128)(2,1)S(1)}, u32[]{:S(2)}) copy-start(bf16[528,512]{1,0:T(8,128)(2,1)S(1)} %collective-permute-done.3.refs_1_.refs_0_.refs_2_) | copy-start | bytes 1622020
  114.2 41.0 %copy-start.8 = (bf16[528,512]{1,0:T(8,128)(2,1)}, bf16[528,512]{1,0:T(8,128)(2,1)S(1)}, u32[]{:S(2)}) copy-start(bf16[528,512]{1,0:T(8,128)(2,1)S(1)} %collective-permute-done.4.refs_0_.refs_2_.refs_1_) | copy-start | bytes 1622020
  155.2 17.5 %copy-start.6 = (bf16[528,512]{1,0:T(8,128)(2,1)}, bf16[528,512]{1,0:T(8,128)(2,1)S(1)}, u32[]{:S(2)}) copy-start(bf16[528,512]{1,0:T(8,128)(2,1)S(1)} %collective-permute-done.5.refs_1_.refs_0_.refs_2_) | copy-start | bytes 1622020
  155.3 59.5 %collective-permute-start.9 = (bf16[512,1024]{1,0:T(8,128)(2,1)}, bf16[512,1024]{1,0:T(8,128)(2,1)}, u32[]{:S(2)}, u32[]{:S(2)}) collective-permute-start(bf16[512,1024]{1,0:T(8,128)(2,1)} %get-tuple-element.86), channel_id=1, source_target_pairs={{0,2},{1,6},{2,4},{3,0},{4,7},{5,3},{6,1},{7,5},{8,10},{9,14},{10,... | collective-permute-start | bytes 3145736 | tf_op jit(solution)/shard_map/ppermute | solution.py:628
  155.3 62.3 %collective-permute-start.7 = (bf16[512,1024]{1,0:T(8,128)(2,1)}, bf16[512,1024]{1,0:T(8,128)(2,1)}, u32[]{:S(2)}, u32[]{:S(2)}) collective-permute-start(bf16[512,1024]{1,0:T(8,128)(2,1)} %get-tuple-element.84), channel_id=1, source_target_pairs={{0,4},{1,0},{2,6},{3,2},{4,1},{5,5},{6,3},{7,7},{8,12},{9,8},{10,1... | collective-permute-start | bytes 3145736 | tf_op jit(solution)/shard_map/ppermute | solution.py:628
  160.1 61.6 %collective-permute-start.8 = (bf16[512,1024]{1,0:T(8,128)(2,1)}, bf16[512,1024]{1,0:T(8,128)(2,1)}, u32[]{:S(2)}, u32[]{:S(2)}) collective-permute-start(bf16[512,1024]{1,0:T(8,128)(2,1)} %get-tuple-element.85), channel_id=1, source_target_pairs={{0,6},{1,2},{2,0},{3,4},{4,3},{5,7},{6,5},{7,1},{8,14},{9,10},{10,... | collective-permute-start | bytes 3145736 | tf_op jit(solution)/shard_map/ppermute | solution.py:628
